TPU v7x, 32 devices: a whole 2x2x4 slice. The times are simulated.
32 devices in a mesh: pair: 4 (over y, x), feat: 8 (over z, core).
Axes of the slice: x: 2, y: 2, z: 4, core: 2. Of those that a mesh axis runs over, the one named last changes fastest.
Arguments:
- decoder: float32 [8, 16384, 2048], P('pair', 'feat'), may hold values from -0.3125 to 0.3125
- pair_map: int32 [8, 2], P('pair'), may hold values from 0 to 3, as said below
- indices: int32 [3, 256, 128], replicated, may hold values from 0 to 16383, as said below
- values: float32 [3, 256, 128], replicated, may hold values from 0.2 to 3
- target: float32 [3, 256, 2048], P(None, ('pair', 'feat')), may hold values from -6 to 6
Outputs:
- recon: bfloat16 [3, 256, 2048], P(None, ('pair', 'feat'))
- dec_grad: float32 [8, 16384, 2048], P('pair', 'feat')
- feat_grad: float32 [3, 256, 128], P(None, ('pair', 'feat'))
Inputs may be any that keep to these rules, and one draw needn't show every extreme that they name: `pair_map`: each pair (s, t) of layers with s <= t < 3 stands in exactly one row as (s, t); every other row is (3, 3), an empty slot. For each layer and token the 128 indices are distinct.
All inputs are finite; a program needn't handle non-finite values.
Results may differ from a plain program's by a relative error of at most 0.0027.
Values may be sent and summed in bfloat16 or wider, within the bound.
No kernel may reach another device: no remote copies, remote signals or barrier semaphores. Data moves between devices by JAX's collectives and lax.ppermute only.
A program may use at most 192 MiB of HBM per device.

v0:
```python
import jax
import jax.numpy as jnp
from jax import lax
from jax.sharding import PartitionSpec as P


def pick_layer(stack, chosen_layer):
    layer_ids = jnp.arange(stack.shape[0], dtype=jnp.int32)[:, None, None]
    return jnp.sum(jnp.where(layer_ids == chosen_layer, stack, jnp.zeros_like(stack)), axis=0)


def body(decoder, pair_map, indices, values, target):
    slot_count, block_width, model_width = decoder.shape
    layers = indices.shape[0]
    tokens = indices.shape[1]
    first_feature = lax.axis_index("feat") * block_width
    columns = jnp.arange(block_width, dtype=jnp.int32)
    sources = pair_map[:, 0]
    goals = pair_map[:, 1]
    local_list = []
    active_list = []
    product_list = []
    for slot_index in range(slot_count):
        picked = jnp.minimum(sources[slot_index], layers - 1)
        local_ids = pick_layer(indices, picked) - first_feature
        weights = pick_layer(values, picked)
        matches = (local_ids[:, :, None] == columns).astype(jnp.float32)
        active = jnp.einsum(
            "tk,tkf->tf",
            weights,
            matches,
            precision=lax.Precision.HIGHEST,
            preferred_element_type=jnp.float32,
        )
        product = jnp.dot(
            active,
            decoder[slot_index],
            precision=lax.Precision.HIGHEST,
            preferred_element_type=jnp.float32,
        )
        local_list.append(local_ids)
        active_list.append(active)
        product_list.append(product)
    stacked = jnp.stack(product_list)
    choose_goal = jax.nn.one_hot(goals, layers, dtype=jnp.float32)
    choose_narrow = choose_goal.astype(jnp.bfloat16)
    pair_count = lax.axis_size("pair")
    feat_count = lax.axis_size("feat")
    share_rows = tokens // (pair_count * feat_count)
    reordered = stacked.reshape(slot_count, pair_count, feat_count, share_rows, model_width)
    reordered = reordered.transpose(0, 2, 1, 3, 4).reshape(slot_count, tokens, model_width)
    slot_block = lax.psum_scatter(reordered, "feat", scatter_dimension=1, tiled=True)
    layer_term = jnp.einsum(
        "jl,jtd->ltd",
        choose_goal,
        slot_block,
        precision=lax.Precision.HIGHEST,
        preferred_element_type=jnp.float32,
    )
    shares = lax.psum_scatter(layer_term, "pair", scatter_dimension=1, tiled=True)
    error_share = (shares - target).astype(jnp.bfloat16)
    layer_block = lax.all_gather(error_share, "pair", axis=1, tiled=True)
    chosen = jnp.einsum(
        "jl,ltd->jtd", choose_narrow, layer_block, preferred_element_type=jnp.float32
    ).astype(jnp.bfloat16)
    gathered = lax.all_gather(chosen, "feat", axis=1, tiled=True)
    gathered = gathered.reshape(slot_count, feat_count, pair_count, share_rows, model_width)
    slot_errors = gathered.transpose(0, 2, 1, 3, 4).reshape(slot_count, tokens, model_width)
    recon = shares.astype(jnp.bfloat16)
    grad_list = []
    feature_term = jnp.zeros((layers, tokens, indices.shape[2]), jnp.float32)
    for slot_index in range(slot_count):
        slot_error = slot_errors[slot_index].astype(jnp.float32)
        tile_grad = jnp.dot(
            active_list[slot_index].T,
            slot_error,
            precision=lax.Precision.HIGHEST,
            preferred_element_type=jnp.float32,
        )
        grad_list.append(tile_grad)
        back = jnp.dot(
            slot_error,
            decoder[slot_index].T,
            precision=lax.Precision.HIGHEST,
            preferred_element_type=jnp.float32,
        )
        matches = (local_list[slot_index][:, :, None] == columns).astype(jnp.float32)
        picked_grad = jnp.einsum(
            "tkf,tf->tk",
            matches,
            back,
            precision=lax.Precision.HIGHEST,
            preferred_element_type=jnp.float32,
        )
        choose_source = jax.nn.one_hot(sources[slot_index], layers, dtype=jnp.float32)
        feature_term = feature_term + choose_source[:, None, None] * picked_grad[None]
    dec_grad = jnp.stack(grad_list)
    feat_grad = lax.psum_scatter(feature_term, ("pair", "feat"), scatter_dimension=1, tiled=True)
    return (recon, dec_grad, feat_grad)


def solution(mesh):
    in_specs = (P("pair", "feat", None), P("pair", None), P(), P(), P(None, ("pair", "feat"), None))
    out_specs = (
        P(None, ("pair", "feat"), None),
        P("pair", "feat", None),
        P(None, ("pair", "feat"), None),
    )
    return jax.shard_map(body, mesh=mesh, in_specs=in_specs, out_specs=out_specs, check_vma=False)
```

profile of v0, /device:TPU:0, one launch (start us, length us, event | category | flops | bytes accessed | tf_op | source)
XLA Modules:
  0.0 806.0 jit_solution(72291712159844005)
XLA Ops:
  7.2 1.3 fusion.49
  12.1 84.0 %fusion.3 = f32[256,1,2048]{2,1,0:T(1,128)S(1)} fusion(f32[256,128,1]{1,2,0:T(1,128)S(1)} %bitcast.97, s32[256,128]{1,0:T(8,128)S(1)} %broadcast_subtract_fusion.1), kind=kOutput, calls=%fused_computation.5 | convolution fusion | flops 872415232 | bytes 2359296 | tf_op jit(solution)/shard_map/tk,tkf->tf/dot_general | solution.py:28
  96.2 2.2 copy.39
  98.4 84.9 %fusion.1 = f32[256,1,2048]{2,1,0:T(1,128)} fusion(f32[256,128,1]{1,2,0:T(1,128)S(1)} %bitcast.95, s32[256,128]{1,0:T(8,128)S(1)} %broadcast_subtract_fusion), kind=kOutput, calls=%fused_computation.2 | convolution fusion | flops 872415232 | bytes 2359296 | tf_op jit(solution)/shard_map/tk,tkf->tf/dot_general | solution.py:28
  183.3 2.6 copy.42
  186.0 18.2 %fusion.26 = f32[1,4,8,8,2048]{4,3,2,1,0:T(8,128)} fusion(f32[4,8,8,2048]{3,2,1,0:T(8,128)S(1)} %bitcast.87, f32[2,2048,2048]{2,1,0:T(8,128)} %param.5), kind=kOutput, calls=%fused_computation.28 | convolution fusion | flops 12884901888 | bytes 20971520 | tf_op jit(solution)/shard_map/dot_general | solution.py:35
  204.2 15.6 %fusion.29 = f32[1,4,8,8,2048]{4,3,2,1,0:T(8,128)} fusion(f32[4,8,8,2048]{3,2,1,0:T(8,128)S(1)} %bitcast.88, f32[2,2048,2048]{2,1,0:T(8,128)S(1)} %bitcast.85), kind=kOutput, calls=%fused_computation.29 | convolution fusion | flops 12884901888 | bytes 20971520 | tf_op jit(solution)/shard_map/dot_general | solution.py:35
  219.8 2.5 maximum_bitcast_fusion
  222.3 2.3 copy.30
  225.4 52.0 %reduce-scatter.3.cloned.1.call-done = f32[2,32,2048]{2,1,0:T(8,128)} async-done(((f32[2,256,2048]{2,1,0:T(8,128)}), f32[2,32,2048]{2,1,0:T(8,128)}) %reduce-scatter.3.cloned.1.call-update) | async-done | bytes 524304 | tf_op jit(solution)/shard_map/reduce_scatter | solution.py:52
  277.4 3.5 fusion.36
  282.4 49.5 %all-reduce.3.cloned.1.call-done = f32[3,32,2048]{2,0,1:T(4,128)} async-done(((f32[3,32,2048]{2,0,1:T(4,128)}), f32[3,32,2048]{2,0,1:T(4,128)}) %all-reduce.3.cloned.1.call-update) | async-done | bytes 786448
  333.0 9.5 %all_gather.6 = bf16[3,32,2048]{2,1,0:T(8,128)(2,1)S(1)} all-gather(bf16[3,8,2048]{2,1,0:T(8,128)(2,1)S(1)} %fusion.39), channel_id=1, replica_groups=mesh['pair'=4,'feat'=8] {'pair'}, dimensions={1}, use_global_device_ids=true | all-gather | bytes 491520 | tf_op jit(solution)/shard_map/all_gather | solution.py:62
  343.8 1.3 compare_convert_fusion
  345.8 27.2 %all-gather.2.cloned.1.call-done = bf16[2,256,2048]{2,0,1:T(2,128)(2,1)} async-done(((bf16[2,32,2048]{2,0,1:T(2,128)(2,1)}), bf16[2,256,2048]{2,0,1:T(2,128)(2,1)}) %all-gather.2.cloned.1.call-update) | async-done | bytes 2097168 | tf_op jit(solution)/shard_map/all_gather | solution.py:66
  373.0 2.5 copy.34
  375.7 12.3 %fusion.20 = f32[256,2048,1]{1,0,2:T(8,128)S(1)} fusion(bf16[256,2048]{1,0:T(8,128)(2,1)S(1)} %bitcast.89, f32[2,2048,2048]{2,1,0:T(8,128)} %param.5), kind=kOutput, calls=%fused_computation.26 | convolution fusion | flops 12884901888 | bytes 19922944 | tf_op jit(solution)/shard_map/dot_general | solution.py:81
  388.0 10.7 %convolution_bitcast_fusion.1 = f32[1,2048,2048]{2,1,0:T(8,128)} fusion(bf16[256,2048]{1,0:T(8,128)(2,1)S(1)} %bitcast.90, f32[256,1,2048]{2,1,0:T(1,128)S(1)} %copy-done.3), kind=kOutput, calls=%fused_computation.24 | convolution fusion | flops 12884901888 | bytes 19922944 | tf_op jit(solution)/shard_map/dot_general | solution.py:74
  398.9 12.0 %fusion.23 = f32[256,2048,1]{1,0,2:T(8,128)S(1)} fusion(bf16[256,2048]{1,0:T(8,128)(2,1)S(1)} %bitcast.91, f32[2,2048,2048]{2,1,0:T(8,128)} %param.5), kind=kOutput, calls=%fused_computation.27 | convolution fusion | flops 12884901888 | bytes 19922944 | tf_op jit(solution)/shard_map/dot_general | solution.py:81
  410.9 10.7 %convolution_bitcast_fusion = f32[1,2048,2048]{2,1,0:T(8,128)} fusion(bf16[256,2048]{1,0:T(8,128)(2,1)S(1)} %bitcast.92, f32[256,1,2048]{2,1,0:T(1,128)S(1)} %copy-done.1), kind=kOutput, calls=%fused_computation.23 | convolution fusion | flops 12884901888 | bytes 19922944 | tf_op jit(solution)/shard_map/dot_general | solution.py:74
  421.7 121.5 %fusion = f32[256,1,128]{2,1,0:T(1,128)S(1)} fusion(s32[256,128]{1,0:T(8,128)S(1)} %broadcast_subtract_fusion, f32[256,2048,1]{1,0,2:T(8,128)S(1)} %fusion.23), kind=kOutput, calls=%fused_computation.1 | convolution fusion | flops 872415232 | bytes 2359296 | tf_op jit(solution)/shard_map/tkf,tf->tk/dot_general | solution.py:88
  543.2 121.6 %fusion.2 = f32[256,1,128]{2,1,0:T(1,128)S(1)} fusion(s32[256,128]{1,0:T(8,128)S(1)} %broadcast_subtract_fusion.1, f32[256,2048,1]{1,0,2:T(8,128)S(1)} %fusion.20), kind=kOutput, calls=%fused_computation.4 | convolution fusion | flops 872415232 | bytes 2359296 | tf_op jit(solution)/shard_map/tkf,tf->tk/dot_general | solution.py:88
  665.7 23.3 %pad_maximum_fusion = f32[2,2048,2048]{2,1,0:T(8,128)} fusion(f32[1,2048,2048]{2,1,0:T(8,128)} %convolution_bitcast_fusion, f32[1,2048,2048]{2,1,0:T(8,128)} %convolution_bitcast_fusion.1), kind=kLoop, calls=%fused_computation.10 | loop fusion | flops 8388608 | bytes 67108864 | tf_op jit(solution)/shard_map/stack | solution.py:97
  689.0 110.0 %reduce-scatter.5.cloned.1.call-done = f32[3,8,128]{2,1,0:T(8,128)} async-done(((f32[3,256,128]{2,1,0:T(8,128)}), f32[3,8,128]{2,1,0:T(8,128)}) %reduce-scatter.5.cloned.1.call-update) | async-done | bytes 12304 | tf_op jit(solution)/shard_map/reduce_scatter | solution.py:98
  (54 shorter events, 8.3 us)
Async XLA Ops:
  7.2 270.3 %reduce-scatter.3.cloned.1.call-start = ((), (), s32[]{:S(2)}) async-start(), calls=%async_computation.2 | async-start | bytes 4718592 | tf_op jit(solution)/shard_map/reduce_scatter | solution.py:52
  96.1 2.2 copy-start.2
  98.4 105.8 %slice-start = ((s8[33554432]{0:T(1024)(128)(4,1)}), s8[4194304]{0:T(1024)(128)(4,1)S(1)}, s32[]{:S(2)}) async-start(s8[33554432]{0:T(1024)(128)(4,1)} %bitcast.84), calls=%async_computation.6 | async-start | bytes 8388608
  98.4 105.8 %slice-start.1 = ((s8[33554432]{0:T(1024)(128)(4,1)}), s8[4194304]{0:T(1024)(128)(4,1)S(1)}, s32[]{:S(2)}) async-start(s8[33554432]{0:T(1024)(128)(4,1)} %bitcast.84), calls=%async_computation.7 | async-start | bytes 8388608
  98.4 105.8 %slice-start.2 = ((s8[33554432]{0:T(1024)(128)(4,1)}), s8[4194304]{0:T(1024)(128)(4,1)S(1)}, s32[]{:S(2)}) async-start(s8[33554432]{0:T(1024)(128)(4,1)} %bitcast.84), calls=%async_computation.8 | async-start | bytes 8388608
  98.4 105.8 %slice-start.3 = ((s8[33554432]{0:T(1024)(128)(4,1)}), s8[4194304]{0:T(1024)(128)(4,1)S(1)}, s32[]{:S(2)}) async-start(s8[33554432]{0:T(1024)(128)(4,1)} %bitcast.84), calls=%async_computation.9 | async-start | bytes 8388608
  98.4 105.8 %slice-start.4 = ((s8[33554432]{0:T(1024)(128)(4,1)}), s8[4194304]{0:T(1024)(128)(4,1)S(1)}, s32[]{:S(2)}) async-start(s8[33554432]{0:T(1024)(128)(4,1)} %bitcast.84), calls=%async_computation.10 | async-start | bytes 8388608
  98.4 105.8 %slice-start.5 = ((s8[33554432]{0:T(1024)(128)(4,1)}), s8[4194304]{0:T(1024)(128)(4,1)S(1)}, s32[]{:S(2)}) async-start(s8[33554432]{0:T(1024)(128)(4,1)} %bitcast.84), calls=%async_computation.11 | async-start | bytes 8388608
  183.3 2.6 copy-start
  185.9 18.2 %slice-start.6 = ((s8[33554432]{0:T(1024)(128)(4,1)}), s8[4194304]{0:T(1024)(128)(4,1)S(1)}, s32[]{:S(2)}) async-start(s8[33554432]{0:T(1024)(128)(4,1)} %bitcast.84), calls=%async_computation.12 | async-start | bytes 8388608
  186.0 18.2 %slice-start.7 = ((s8[33554432]{0:T(1024)(128)(4,1)}), s8[4194304]{0:T(1024)(128)(4,1)S(1)}, s32[]{:S(2)}) async-start(s8[33554432]{0:T(1024)(128)(4,1)} %bitcast.84), calls=%async_computation.13 | async-start | bytes 8388608
  224.5 0.7 copy-start.5
  224.6 56.5 %copy-start.6 = (u32[32]{0:T(128)S(1)}, u32[32]{0:T(128)}, u32[]{:S(2)}) copy-start(u32[32]{0:T(128)} %constant.19) | copy-start | bytes 388
  224.6 108.3 %copy-start.4 = (f32[3,8,2048]{2,1,0:T(8,128)S(1)}, f32[3,8,2048]{2,1,0:T(8,128)}, u32[]{:S(2)}) copy-start(f32[3,8,2048]{2,1,0:T(8,128)} %param.9) | copy-start | bytes 589828
  224.6 107.3 %all-reduce.3.cloned.1.call-start = ((), (), s32[]{:S(2)}) async-start(), calls=%async_computation.5 | async-start | bytes 2097152
  281.0 92.0 %all-gather.2.cloned.1.call-start = ((), (), s32[]{:S(2)}) async-start(), calls=%async_computation.3 | async-start | bytes 2359296 | tf_op jit(solution)/shard_map/all_gather | solution.py:66
  343.7 455.3 %reduce-scatter.5.cloned.1.call-start = ((), (), s32[]{:S(2)}) async-start(), calls=%async_computation.4 | async-start | bytes 405504 | tf_op jit(solution)/shard_map/reduce_scatter | solution.py:98
  375.7 12.4 %copy-start.3 = (f32[256,1,2048]{2,1,0:T(1,128)S(1)}, f32[256,1,2048]{2,1,0:T(1,128)}, u32[]{:S(2)}) copy-start(f32[256,1,2048]{2,1,0:T(1,128)} %copy-done.2) | copy-start | bytes 6291460
  398.9 12.0 %copy-start.1 = (f32[256,1,2048]{2,1,0:T(1,128)S(1)}, f32[256,1,2048]{2,1,0:T(1,128)}, u32[]{:S(2)}) copy-start(f32[256,1,2048]{2,1,0:T(1,128)} %fusion.1) | copy-start | bytes 6291460
Sparse Core Ops, SparseCore 0:
  224.7 52.6 reduce-scatter.2
  281.1 50.6 all-reduce.2
  343.9 29.0 all-gather.1
  665.8 133.1 reduce-scatter.4
where the time goes:
time: 815 us; the launch traced here: 806 us
  matrix products  496 us (61%)
  waiting for transfers between devices  239 us (29%)
  other arithmetic  31.5 us (4%)
  between operations  16.4 us (2%)
  local copies, waits for them, and re-layouts  13.4 us (2%)
  blocking collectives  9.47 us (1%)
    dot_general x2, matrix products, body(): jnp.einsum('tkf,tf->tk', matches, back, precision=lax.Precision.HIGHEST,...  243 us
    dot_general x2, matrix products, body(): jnp.einsum('tk,tkf->tf', weights, matches, precision=lax.Precision.HIGHES...  169 us
    reduce_scatter x1, waiting for transfers between devices, body(): lax.psum_scatter(feature_term, ('pair', 'feat'), scatter_dimension=1, til...  110 us
    reduce_scatter x1, waiting for transfers between devices, body(): lax.psum_scatter(reordered, 'feat', scatter_dimension=1, tiled=True)  52 us
    unnamed x5, waiting for transfers between devices  49.6 us
    dot_general x2, matrix products, body(): jnp.dot(active, decoder[slot_index], precision=lax.Precision.HIGHEST, pre...  33.7 us
    all_gather x1, waiting for transfers between devices, body(): gathered = lax.all_gather(chosen, 'feat', axis=1, tiled=True)  27.2 us
    dot_general x2, matrix products, body(): jnp.dot(slot_error, decoder[slot_index].T, precision=lax.Precision.HIGHES...  24.3 us
  transfers between devices with their start and end apart: 4, of which 4 were waited for; matrix products, arithmetic and copies ran while one was open for 3% of the time, Pallas kernels for 0%

commit v1 on v0

v1 whole, which is shorter than its diff:
```python
import jax
import jax.numpy as jnp
from jax import lax
from jax.experimental import pallas as pl
from jax.experimental.pallas import tpu as pltpu
from jax.sharding import PartitionSpec as P

f32=jnp.float32
bf16=jnp.bfloat16
WIRE_SCALE=128.0
LANES=128
NT=(((1,),(1,)),((),()))
TN=(((0,),(0,)),((),()))

def split(x):
    hi=x.astype(bf16)
    return hi,(x-hi.astype(f32)).astype(bf16)

def build_acts(first, idx_ref, val_ref, hi_out, lo_out, rows_scr, code_scr):
    T=idx_ref.shape[1]; K=idx_ref.shape[2]; W=hi_out.shape[-1]; H=W//LANES
    TB=rows_scr.shape[0]//(2*H)
    iota_h=lax.broadcasted_iota(jnp.int32,(H,K),0)
    iota_l=lax.broadcasted_iota(jnp.int32,(LANES,K),0)
    def block(b,_):
        base=pl.multiple_of(b*TB,TB)
        def eight(g,_):
            r0=pl.multiple_of(base+g*8,8)
            for i in range(8):
                ids=idx_ref[0,pl.ds(r0+i,1),:]-first
                v=val_ref[0,pl.ds(r0+i,1),:]
                vh,vl=split(v)
                hi=ids>>7
                lo=ids&127
                hit=hi==iota_h
                a=jnp.concatenate([jnp.where(hit,vh.astype(f32),0.0),jnp.where(hit,vl.astype(f32),0.0)],axis=0).astype(bf16)
                oh=jnp.where(lo==iota_l,1.0,0.0).astype(bf16)
                r=lax.dot_general(a,oh,NT,preferred_element_type=f32)
                rows_scr[pl.ds(pl.multiple_of((g*8+i)*2*H,2*H),2*H),:]=r
            return 0
        lax.fori_loop(0,TB//8,eight,0)
        for h in range(H):
            hi_out[pl.ds(base,TB),h*LANES:(h+1)*LANES]=rows_scr[pl.ds(h,TB,stride=2*H),:].astype(bf16)
            lo_out[pl.ds(base,TB),h*LANES:(h+1)*LANES]=rows_scr[pl.ds(H+h,TB,stride=2*H),:].astype(bf16)
        return 0
    lax.fori_loop(0,T//TB,block,0)

def build_kernel(src_ref, first_ref, idx_ref, val_ref, hi_ref, lo_ref, rows_scr):
    build_acts(first_ref[0], idx_ref, val_ref, hi_ref.at[0], lo_ref.at[0], rows_scr, None)

def build_call(src, first, indices, values, W, TB=64):
    S=src.shape[0]; L,T,K=indices.shape; H=W//LANES
    return pl.pallas_call(build_kernel,
        out_shape=(jax.ShapeDtypeStruct((S,T,W),bf16),)*2,
        grid_spec=pltpu.PrefetchScalarGridSpec(num_scalar_prefetch=2, grid=(S,),
            in_specs=[pl.BlockSpec((1,T,K),lambda j,s,f:(s[j],0,0))]*2,
            out_specs=[pl.BlockSpec((1,T,W),lambda j,s,f:(j,0,0))]*2,
            scratch_shapes=[pltpu.VMEM((TB*2*H,LANES),f32)]),
        compiler_params=pltpu.CompilerParams(vmem_limit_bytes=40<<20),
        name="build")(src,first,indices,values)

def recon_kernel(src_ref, first_ref, idx_ref, val_ref, dec_ref, prod_ref, hi_ref, lo_ref, rows_scr):
    @pl.when(pl.program_id(1)==0)
    def _(): build_acts(first_ref[0], idx_ref, val_ref, hi_ref.at[0], lo_ref.at[0], rows_scr, None)
    dh,dl=split(dec_ref[0])
    ah=hi_ref[0]
    p=jnp.dot(ah,dh,preferred_element_type=f32)
    p+=jnp.dot(lo_ref[0],dh,preferred_element_type=f32)
    p+=jnp.dot(ah,dl,preferred_element_type=f32)
    prod_ref[0]=p

def recon_call(src, first, indices, values, dec, TB=64, DT=512, nbuf=3):
    S,W,D=dec.shape; L,T,K=indices.shape; H=W//LANES
    return pl.pallas_call(recon_kernel,
        out_shape=(jax.ShapeDtypeStruct((S,T,D),f32),jax.ShapeDtypeStruct((S,T,W),bf16),jax.ShapeDtypeStruct((S,T,W),bf16)),
        grid_spec=pltpu.PrefetchScalarGridSpec(num_scalar_prefetch=2, grid=(S,D//DT),
            in_specs=[pl.BlockSpec((1,T,K),lambda j,n,s,f:(s[j],0,0))]*2+[pl.BlockSpec((1,W,DT),lambda j,n,s,f:(j,0,n))],
            out_specs=[pl.BlockSpec((1,T,DT),lambda j,n,s,f:(j,0,n))]+[pl.BlockSpec((1,T,W),lambda j,n,s,f:(j,0,0))]*2,
            scratch_shapes=[pltpu.VMEM((TB*2*H,LANES),f32)]),
        compiler_params=pltpu.CompilerParams(vmem_limit_bytes=56<<20),
        name="recon")(src,first,indices,values,dec)

def back_kernel(src_ref, first_ref, idx_ref, err_ref, dec_ref, out_ref):
    n=pl.program_id(1)
    FT=dec_ref.shape[1]
    @pl.when(n==0)
    def _(): out_ref[...]=jnp.zeros_like(out_ref)
    dh,dl=split(dec_ref[0])
    e=err_ref[0]
    g=lax.dot_general(e,dh,NT,preferred_element_type=f32)
    g+=lax.dot_general(e,dl,NT,preferred_element_type=f32)
    ids=idx_ref[0]-(first_ref[0]+n*FT)
    hi=ids>>7
    lo=ids&127
    acc=out_ref[0]
    for c in range(FT//LANES):
        acc=jnp.where(hi==c,jnp.take_along_axis(g[:,c*LANES:(c+1)*LANES],lo,axis=1),acc)
    out_ref[0]=acc

def back_call(src, first, indices, err, dec, FT=512, nbuf=2):
    S,W,D=dec.shape; L,T,K=indices.shape
    FT=min(FT,W)
    return pl.pallas_call(back_kernel,
        out_shape=jax.ShapeDtypeStruct((S,T,K),f32),
        grid_spec=pltpu.PrefetchScalarGridSpec(num_scalar_prefetch=2, grid=(S,W//FT),
            in_specs=[pl.BlockSpec((1,T,K),lambda j,n,s,f:(s[j],0,0)),pl.BlockSpec((1,T,D),lambda j,n,s,f:(j,0,0)),
                      pl.BlockSpec((1,FT,D),lambda j,n,s,f:(j,n,0))],
            out_specs=pl.BlockSpec((1,T,K),lambda j,n,s,f:(j,0,0))),
        compiler_params=pltpu.CompilerParams(vmem_limit_bytes=56<<20),
        name="back")(src,first,indices,err,dec)

def grad_kernel(hi_ref, lo_ref, err_ref, out_ref):
    e=err_ref[0]
    p=lax.dot_general(hi_ref[0],e,TN,preferred_element_type=f32)
    out_ref[0]=p+lax.dot_general(lo_ref[0],e,TN,preferred_element_type=f32)

def grad_call(hi, lo, err, FT=512):
    S,T,W=hi.shape; D=err.shape[2]
    FT=min(FT,W)
    return pl.pallas_call(grad_kernel,
        out_shape=jax.ShapeDtypeStruct((S,W,D),f32),
        grid=(S,W//FT),
        in_specs=[pl.BlockSpec((1,T,FT),lambda j,n:(j,0,n))]*2+[pl.BlockSpec((1,T,D),lambda j,n:(j,0,0))],
        out_specs=pl.BlockSpec((1,FT,D),lambda j,n:(j,n,0)),
        compiler_params=pltpu.CompilerParams(vmem_limit_bytes=56<<20),
        name="grad")(hi,lo,err)


def parts_of(feat_count):
    return feat_count // 2


def swap_cores(x):
    count = lax.axis_size("feat")
    return lax.ppermute(x, "feat", [(i, i ^ 1) for i in range(count)])


def shift_z(x, step):
    count = lax.axis_size("feat")
    return lax.ppermute(x, "feat", [(i, (i + 2 * step) % count) for i in range(count)])


def shift_pair(x, step):
    count = lax.axis_size("pair")
    return lax.ppermute(x, "pair", [(i, (i + step) % count) for i in range(count)])


def take(x, at, axis):
    return lax.dynamic_index_in_dim(x, at, axis, keepdims=False)


def pack(x):
    return (x * WIRE_SCALE).astype(jnp.float16)


def unpack(x):
    return x.astype(f32) * (1.0 / WIRE_SCALE)


def sum_full(prod, goals_all, layers):
    pairs, zs = lax.axis_size("pair"), lax.axis_size("feat") // 2
    p, feat = lax.axis_index("pair"), lax.axis_index("feat")
    z, core = feat // 2, feat % 2
    slots, tokens, width = prod.shape
    rows = tokens // (pairs * zs * 2)
    cut = prod.reshape(slots, pairs, zs, 2, rows, width)
    got = swap_cores(pack(take(cut, 1 - core, 3)))
    half = take(cut, core, 3) + unpack(got)
    arrived = [(p, take(half, p, 1))]
    for step in range(1, pairs):
        sent = pack(take(half, (p + step) % pairs, 1))
        arrived.append(((p - step) % pairs, unpack(shift_pair(sent, step))))
    layer_list = []
    for layer in range(layers):
        total = jnp.zeros(half.shape[2:], f32)
        for owner, block in arrived:
            goals = take(goals_all, owner, 0)
            for j in range(slots):
                total = total + jnp.where(goals[j] == layer, block[j], 0.0)
        layer_list.append(total)
    summed = jnp.stack(layer_list)
    full = take(summed, z, 1)
    for step in range(1, zs):
        full = full + unpack(shift_z(pack(take(summed, (z + step) % zs, 1)), step))
    return full


def spread_errors(error, goals_all):
    pairs, zs = lax.axis_size("pair"), lax.axis_size("feat") // 2
    p, feat = lax.axis_index("pair"), lax.axis_index("feat")
    z, core = feat // 2, feat % 2
    layers, rows, width = error.shape
    slots = goals_all.shape[1]
    column = jnp.zeros((layers, zs, rows, width), bf16)
    column = lax.dynamic_update_index_in_dim(column, error, z, 1)
    for step in range(1, zs):
        column = lax.dynamic_update_index_in_dim(column, shift_z(error, step), (z - step) % zs, 1)

    def choose(owner):
        goals = take(goals_all, owner, 0)
        return jnp.stack([
            jnp.where(goals[j] < layers, take(column, jnp.minimum(goals[j], layers - 1), 0), jnp.zeros((), bf16))
            for j in range(slots)
        ])

    plane = jnp.zeros((slots, pairs, zs, rows, width), bf16)
    plane = lax.dynamic_update_index_in_dim(plane, choose(p), p, 1)
    for step in range(1, pairs):
        got = shift_pair(choose((p + step) % pairs), step)
        plane = lax.dynamic_update_index_in_dim(plane, got, (p - step) % pairs, 1)
    other = swap_cores(plane)
    both = jnp.stack([jnp.where(core == 0, plane, other), jnp.where(core == 0, other, plane)], axis=3)
    return both.reshape(slots, pairs * zs * 2 * rows, width)


def sum_picks(picks, sources_all, layers):
    pairs, zs = lax.axis_size("pair"), lax.axis_size("feat") // 2
    p, feat = lax.axis_index("pair"), lax.axis_index("feat")
    z, core = feat // 2, feat % 2
    slots, tokens, width = picks.shape
    rows = tokens // (pairs * zs * 2)
    cut = picks.reshape(slots, pairs, zs, 2, rows, width)
    half = take(cut, core, 3) + swap_cores(take(cut, 1 - core, 3))
    column = take(half, z, 2)
    for step in range(1, zs):
        column = column + shift_z(take(half, (z + step) % zs, 2), step)
    arrived = [(p, take(column, p, 1))]
    for step in range(1, pairs):
        sent = take(column, (p + step) % pairs, 1)
        arrived.append(((p - step) % pairs, shift_pair(sent, step)))
    layer_list = []
    for layer in range(layers):
        total = jnp.zeros((rows, width), f32)
        for owner, block in arrived:
            sources = take(sources_all, owner, 0)
            for j in range(slots):
                total = total + jnp.where(sources[j] == layer, block[j], 0.0)
        layer_list.append(total)
    return jnp.stack(layer_list)


def body(decoder, pair_map, indices, values, target):
    slots, block_width, width = decoder.shape
    layers, tokens, active = indices.shape
    pairs = lax.axis_size("pair")
    first = (lax.axis_index("feat") * block_width).reshape(1).astype(jnp.int32)
    source = jnp.minimum(pair_map[:, 0], layers - 1)
    pair_all = lax.all_gather(pair_map, "pair", axis=0)
    sources_all, goals_all = pair_all[:, :, 0], pair_all[:, :, 1]
    prod, hi, lo = recon_call(source, first, indices, values, decoder)
    full = sum_full(prod, goals_all, layers)
    recon = full.astype(bf16)
    error = (full - target).astype(bf16)
    slot_error = spread_errors(error, goals_all)
    picks = back_call(source, first, indices, slot_error, decoder)
    feat_grad = sum_picks(picks, sources_all, layers)
    dec_grad = grad_call(hi, lo, slot_error)
    return recon, dec_grad, feat_grad


def solution(mesh):
    in_specs = (P("pair", "feat", None), P("pair", None), P(), P(), P(None, ("pair", "feat"), None))
    out_specs = (
        P(None, ("pair", "feat"), None),
        P("pair", "feat", None),
        P(None, ("pair", "feat"), None),
    )
    return jax.shard_map(body, mesh=mesh, in_specs=in_specs, out_specs=out_specs, check_vma=False)
```

time: 815 us -> 207 us (0.25)
  matrix products: 496 us -> 0 us
  waiting for transfers between devices: 239 us -> 27.2 us
  Pallas kernels: 0 us -> 78.6 us
  starting transfers between devices: 0.16 us -> 33.6 us
  between operations: 16.4 us -> 42.4 us
  other arithmetic: 31.5 us -> 10.2 us
  local copies, waits for them, and re-layouts: 13.4 us -> 4.84 us
    dot_general x12 -> x0, matrix products: 496 us -> none  [the longest x2 243 us: body(): jnp.einsum('tkf,tf->tk', matches, back, precision=lax.Precision.HIGHEST,...]
    reduce_scatter x2 -> x0, waiting for transfers between devices: 162 us -> none  [the longest x1 110 us: body(): lax.psum_scatter(feature_term, ('pair', 'feat'), scatter_dimension=1, til...]
    pallas_call x0 -> x3, Pallas kernels: none -> 78.6 us  [the longest x1 43.2 us: recon_call(): pl.pallas_call(recon_kernel, out_shape=(jax.ShapeDtypeStruct((S, T, D), f...]
    unnamed x5 -> x0, waiting for transfers between devices: 49.6 us -> none
    ppermute x0 -> x21, starting transfers between devices: none -> 33.6 us  [the longest x9 17.8 us: shift_pair(): lax.ppermute(x, 'pair', [(i, (i + step) % count) for i in range(count)])]
    all_gather x1 -> x0, waiting for transfers between devices: 27.2 us -> none  [body(): gathered = lax.all_gather(chosen, 'feat', axis=1, tiled=True)]
    ppermute x0 -> x21, waiting for transfers between devices: none -> 27.2 us  [the longest x9 13.7 us: shift_pair(): lax.ppermute(x, 'pair', [(i, (i + step) % count) for i in range(count)])]
    another operation x1 -> x7, other arithmetic: 23.3 us -> 2.44 us  [the longest x2 1.71 us: spread_errors(): jnp.stack([jnp.where(core == 0, plane, other), jnp.where(core == 0, other...]
  transfers between devices with their start and end apart: 4 -> 21, of which waited for: 4 -> 11; matrix products, arithmetic and copies ran while one was open for 3% -> 2% of each run, Pallas kernels for 0% -> 8%
where the time goes in v1:
time: 207 us; the launch traced here: 206 us
  Pallas kernels  78.6 us (38%)
  between operations  42.4 us (20%)
  starting transfers between devices  33.6 us (16%)
  waiting for transfers between devices  27.2 us (13%)
  other arithmetic  10.2 us (5%)
  blocking collectives  9.17 us (4%)
  local copies, waits for them, and re-layouts  4.84 us (2%)
    pallas_call x1, Pallas kernels, recon_call(): pl.pallas_call(recon_kernel, out_shape=(jax.ShapeDtypeStruct((S, T, D), f...  43.2 us
    pallas_call x1, Pallas kernels, back_call(): pl.pallas_call(back_kernel, out_shape=jax.ShapeDtypeStruct((S, T, K), f32...  18.8 us
    ppermute x9, starting transfers between devices, shift_pair(): lax.ppermute(x, 'pair', [(i, (i + step) % count) for i in range(count)])  17.8 us
    pallas_call x1, Pallas kernels, grad_call(): pl.pallas_call(grad_kernel, out_shape=jax.ShapeDtypeStruct((S, W, D), f32...  16.6 us
    ppermute x9, starting transfers between devices, shift_z(): lax.ppermute(x, 'feat', [(i, (i + 2 * step) % count) for i in range(count)])  15 us
    ppermute x9, waiting for transfers between devices, shift_pair(): lax.ppermute(x, 'pair', [(i, (i + step) % count) for i in range(count)])  13.7 us
    ppermute x9, waiting for transfers between devices, shift_z(): lax.ppermute(x, 'feat', [(i, (i + 2 * step) % count) for i in range(count)])  10.2 us
    all_gather x1, blocking collectives, body(): pair_all = lax.all_gather(pair_map, 'pair', axis=0)  9.17 us
  transfers between devices with their start and end apart: 21, of which 11 were waited for; matrix products, arithmetic and copies ran while one was open for 2% of the time, Pallas kernels for 8%

profile of v1, /device:TPU:0, one launch (start us, length us, event | category | flops | bytes accessed | tf_op | source)
XLA Modules:
  0.0 205.9 jit_solution(3274187635974831102)
XLA Ops:
  2.0 43.2 %recon.1 = (f32[2,256,2048]{2,1,0:T(8,128)}, bf16[2,256,2048]{2,1,0:T(8,128)(2,1)}, bf16[2,256,2048]{2,1,0:T(8,128)(2,1)}) custom-call(s32[2]{0:T(128)} %minimum_reduce_fusion.src_ref, s32[1]{0:T(128)} %bitcast.2.first_ref, s32[3,256,128]{2,1,0:T(8,128)} %idx_ref.3, f32[3,256,128]{2,1,0:T(8,128)} %val_ref.1, f32[2,2048,2048]{2,1,0:T(8,128)} %dec_ref.3), custom_call_target="tpu_custom_call" | custom-call | tf_op jit(solution)/shard_map/recon/pallas_call | solution.py:73
  45.1 1.8 fusion.1
  47.5 9.2 %all-gather.1 = s32[4,2,2]{2,1,0:T(2,128)S(1)} all-gather(s32[1,2,2]{2,1,0:T(2,128)S(1)} %bitcast.289), channel_id=2, replica_groups=mesh['pair'=4,'feat'=8] {'pair'}, dimensions={0}, use_global_device_ids=true | all-gather | bytes 80 | tf_op jit(solution)/shard_map/all_gather | solution.py:247
  56.7 1.9 bitcast_add_fusion
  58.8 1.5 collective-permute-start.1
  77.9 1.6 collective-permute-start.3
  80.9 3.4 %collective-permute-done.3 = f16[2,4,8,2048]{3,2,1,0:T(8,128)(2,1)S(1)} collective-permute-done((f16[2,4,8,2048]{3,2,1,0:T(8,128)(2,1)S(1)}, f16[2,4,8,2048]{3,2,1,0:T(8,128)(2,1)S(1)}, u32[]{:S(2)}, u32[]{:S(2)}) %collective-permute-start.3) | collective-permute-done | bytes 262176 | tf_op jit(solution)/shard_map/ppermute | solution.py:144
  86.5 1.6 collective-permute-start.4
  88.1 2.2 %collective-permute-start.6 = (f16[3,8,2048]{2,1,0:T(8,128)(2,1)S(1)}, f16[3,8,2048]{2,1,0:T(8,128)(2,1)S(1)}, u32[]{:S(2)}, u32[]{:S(2)}) collective-permute-start(f16[3,8,2048]{2,1,0:T(8,128)(2,1)S(1)} %get-tuple-element.17), channel_id=1, source_target_pairs={{0,6},{1,7},{2,0},{3,1},{4,2},{5,3},{6,4},{7,5},{8,14},{9,15},{10,... | collective-permute-start | bytes 294920 | tf_op jit(solution)/shard_map/ppermute | solution.py:139
  91.1 1.9 collective-permute-done.4
  93.0 1.6 collective-permute-done.6
  94.6 2.2 %collective-permute-done.5 = f16[3,8,2048]{2,1,0:T(8,128)(2,1)S(1)} collective-permute-done((f16[3,8,2048]{2,1,0:T(8,128)(2,1)S(1)}, f16[3,8,2048]{2,1,0:T(8,128)(2,1)S(1)}, u32[]{:S(2)}, u32[]{:S(2)}) %collective-permute-start.5) | collective-permute-done | bytes 98336 | tf_op jit(solution)/shard_map/ppermute | solution.py:139
  108.4 3.4 %collective-permute-start.8 = (bf16[3,8,2048]{2,1,0:T(8,128)(2,1)S(1)}, bf16[3,8,2048]{2,1,0:T(8,128)(2,1)S(1)}, u32[]{:S(2)}, u32[]{:S(2)}) collective-permute-start(bf16[3,8,2048]{2,1,0:T(8,128)(2,1)S(1)} %get-tuple-element.10), channel_id=1, source_target_pairs={{0,4},{1,5},{2,6},{3,7},{4,0},{5,1},{6,2},{7,3},{8,12},{9,13},{10,... | collective-permute-start | bytes 294920 | tf_op jit(solution)/shard_map/ppermute | solution.py:139
  112.1 3.5 %collective-permute-done.8 = bf16[3,8,2048]{2,1,0:T(8,128)(2,1)S(1)} collective-permute-done((bf16[3,8,2048]{2,1,0:T(8,128)(2,1)S(1)}, bf16[3,8,2048]{2,1,0:T(8,128)(2,1)S(1)}, u32[]{:S(2)}, u32[]{:S(2)}) %collective-permute-start.8) | collective-permute-done | bytes 98336 | tf_op jit(solution)/shard_map/ppermute | solution.py:139
  116.7 7.3 %collective-permute-start.10 = (bf16[2,4,8,2048]{3,2,1,0:T(8,128)(2,1)S(1)}, bf16[2,4,8,2048]{3,2,1,0:T(8,128)(2,1)S(1)}, u32[]{:S(2)}, u32[]{:S(2)}) collective-permute-start(bf16[2,4,8,2048]{3,2,1,0:T(8,128)(2,1)S(1)} %pad_maximum_fusion.2), channel_id=1, source_target_pairs={{0,8},{8,16},{16,24},{24,0},{1,9},{9,17},{17,25},{25,1},{2,10},{10... | collective-permute-start | bytes 786440 | tf_op jit(solution)/shard_map/ppermute | solution.py:144
  125.9 5.5 %collective-permute-done.10 = bf16[2,4,8,2048]{3,2,1,0:T(8,128)(2,1)S(1)} collective-permute-done((bf16[2,4,8,2048]{3,2,1,0:T(8,128)(2,1)S(1)}, bf16[2,4,8,2048]{3,2,1,0:T(8,128)(2,1)S(1)}, u32[]{:S(2)}, u32[]{:S(2)}) %collective-permute-start.10) | collective-permute-done | bytes 262176 | tf_op jit(solution)/shard_map/ppermute | solution.py:144
  131.4 3.3 %collective-permute-done.11 = bf16[2,4,8,2048]{3,2,1,0:T(8,128)(2,1)S(1)} collective-permute-done((bf16[2,4,8,2048]{3,2,1,0:T(8,128)(2,1)S(1)}, bf16[2,4,8,2048]{3,2,1,0:T(8,128)(2,1)S(1)}, u32[]{:S(2)}, u32[]{:S(2)}) %collective-permute-start.11) | collective-permute-done | bytes 262176 | tf_op jit(solution)/shard_map/ppermute | solution.py:144
  134.8 2.6 %collective-permute-done.13 = bf16[2,4,4,8,2048]{4,3,2,1,0:T(8,128)(2,1)S(1)} collective-permute-done((bf16[2,4,4,8,2048]{4,3,2,1,0:T(8,128)(2,1)S(1)}, bf16[2,4,4,8,2048]{4,3,2,1,0:T(8,128)(2,1)S(1)}, u32[]{:S(2)}, u32[]{:S(2)}) %collective-permute-start.13) | collective-permute-done | bytes 1048608 | tf_op jit(solution)/shard_map/ppermute | solution.py:134
  137.6 1.6 pad_maximum_fusion
  139.2 18.8 %back.1 = f32[2,256,128]{2,1,0:T(8,128)} custom-call(s32[2]{0:T(128)} %minimum_reduce_fusion.src_ref, s32[1]{0:T(128)} %bitcast.2.first_ref, s32[3,256,128]{2,1,0:T(8,128)} %idx_ref.3, bf16[2,256,2048]{2,1,0:T(8,128)(2,1)} %bitcast.283, f32[2,2048,2048]{2,1,0:T(8,128)} %dec_ref.3), custom_call_target="tpu_custom_call" | custom-call | tf_op jit(solution)/shard_map/back/pallas_call | solution.py:102
  161.3 2.9 %collective-permute-start.15 = (f32[2,4,8,128]{3,2,1,0:T(8,128)S(1)}, f32[2,4,8,128]{3,2,1,0:T(8,128)S(1)}, u32[]{:S(2)}, u32[]{:S(2)}) collective-permute-start(f32[2,4,8,128]{3,2,1,0:T(8,128)S(1)} %get-tuple-element.27), channel_id=1, source_target_pairs={{0,2},{1,3},{2,4},{3,5},{4,6},{5,7},{6,0},{7,1},{8,10},{9,11},{10,... | collective-permute-start | bytes 98312 | tf_op jit(solution)/shard_map/ppermute | solution.py:139
  164.2 2.9 %collective-permute-start.17 = (f32[2,4,8,128]{3,2,1,0:T(8,128)S(1)}, f32[2,4,8,128]{3,2,1,0:T(8,128)S(1)}, u32[]{:S(2)}, u32[]{:S(2)}) collective-permute-start(f32[2,4,8,128]{3,2,1,0:T(8,128)S(1)} %get-tuple-element.28), channel_id=1, source_target_pairs={{0,6},{1,7},{2,0},{3,1},{4,2},{5,3},{6,4},{7,5},{8,14},{9,15},{10,... | collective-permute-start | bytes 98312 | tf_op jit(solution)/shard_map/ppermute | solution.py:139
  183.5 1.8 collective-permute-start.18
  188.6 16.6 %grad.1 = f32[2,2048,2048]{2,1,0:T(8,128)} custom-call(bf16[2,256,2048]{2,1,0:T(8,128)(2,1)} %get-tuple-element.7.hi_ref, bf16[2,256,2048]{2,1,0:T(8,128)(2,1)} %get-tuple-element.8.lo_ref, bf16[2,256,2048]{2,1,0:T(8,128)(2,1)} %bitcast.284), custom_call_target="tpu_custom_call" | custom-call | tf_op jit(solution)/shard_map/grad/pallas_call | solution.py:119
  (73 shorter events, 21.1 us)
Async XLA Ops:
  45.1 2.3 %copy-start.1 = (s32[2,2]{1,0:T(2,128)S(1)}, s32[2,2]{1,0:T(2,128)}, u32[]{:S(2)}) copy-start(s32[2,2]{1,0:T(2,128)} %param.6) | copy-start | bytes 52
  47.0 9.8 %collective-permute-start = (f16[2,4,4,8,2048]{4,3,2,1,0:T(8,128)(2,1)S(1)}, f16[2,4,4,8,2048]{4,3,2,1,0:T(8,128)(2,1)S(1)}, u32[]{:S(2)}, u32[]{:S(2)}) collective-permute-start(f16[2,4,4,8,2048]{4,3,2,1,0:T(8,128)(2,1)S(1)} %fusion.1), channel_id=1, source_target_pairs={{0,1},{1,0},{2,3},{3,2},{4,5},{5,4},{6,7},{7,6},{8,9},{9,8},{10,11... | collective-permute-start | bytes 3145736 | tf_op jit(solution)/shard_map/ppermute | solution.py:134
  58.8 22.0 %collective-permute-start.1 = (f16[2,4,8,2048]{3,2,1,0:T(8,128)(2,1)S(1)}, f16[2,4,8,2048]{3,2,1,0:T(8,128)(2,1)S(1)}, u32[]{:S(2)}, u32[]{:S(2)}) collective-permute-start(f16[2,4,8,2048]{3,2,1,0:T(8,128)(2,1)S(1)} %get-tuple-element.13), channel_id=1, source_target_pairs={{0,8},{8,16},{16,24},{24,0},{1,9},{9,17},{17,25},{25,1},{2,10},{10... | collective-permute-start | bytes 786440 | tf_op jit(solution)/shard_map/ppermute | solution.py:144
  77.9 6.4 %collective-permute-start.3 = (f16[2,4,8,2048]{3,2,1,0:T(8,128)(2,1)S(1)}, f16[2,4,8,2048]{3,2,1,0:T(8,128)(2,1)S(1)}, u32[]{:S(2)}, u32[]{:S(2)}) collective-permute-start(f16[2,4,8,2048]{3,2,1,0:T(8,128)(2,1)S(1)} %get-tuple-element.14), channel_id=1, source_target_pairs={{0,24},{8,0},{16,8},{24,16},{1,25},{9,1},{17,9},{25,17},{2,26},{10... | collective-permute-start | bytes 786440 | tf_op jit(solution)/shard_map/ppermute | solution.py:144
  79.4 6.4 %collective-permute-start.2 = (f16[2,4,8,2048]{3,2,1,0:T(8,128)(2,1)S(1)}, f16[2,4,8,2048]{3,2,1,0:T(8,128)(2,1)S(1)}, u32[]{:S(2)}, u32[]{:S(2)}) collective-permute-start(f16[2,4,8,2048]{3,2,1,0:T(8,128)(2,1)S(1)} %get-tuple-element.15), channel_id=1, source_target_pairs={{0,16},{8,24},{16,0},{24,8},{1,17},{9,25},{17,1},{25,9},{2,18},{10... | collective-permute-start | bytes 786440 | tf_op jit(solution)/shard_map/ppermute | solution.py:144
  86.2 10.7 %copy-start = (f32[3,8,2048]{2,1,0:T(8,128)S(1)}, f32[3,8,2048]{2,1,0:T(8,128)}, u32[]{:S(2)}) copy-start(f32[3,8,2048]{2,1,0:T(8,128)} %param.9) | copy-start | bytes 589828
  86.5 6.6 %collective-permute-start.4 = (f16[3,8,2048]{2,1,0:T(8,128)(2,1)S(1)}, f16[3,8,2048]{2,1,0:T(8,128)(2,1)S(1)}, u32[]{:S(2)}, u32[]{:S(2)}) collective-permute-start(f16[3,8,2048]{2,1,0:T(8,128)(2,1)S(1)} %get-tuple-element.16), channel_id=1, source_target_pairs={{0,2},{1,3},{2,4},{3,5},{4,6},{5,7},{6,0},{7,1},{8,10},{9,11},{10,... | collective-permute-start | bytes 294920 | tf_op jit(solution)/shard_map/ppermute | solution.py:139
  88.1 6.5 %collective-permute-start.6 = (f16[3,8,2048]{2,1,0:T(8,128)(2,1)S(1)}, f16[3,8,2048]{2,1,0:T(8,128)(2,1)S(1)}, u32[]{:S(2)}, u32[]{:S(2)}) collective-permute-start(f16[3,8,2048]{2,1,0:T(8,128)(2,1)S(1)} %get-tuple-element.17), channel_id=1, source_target_pairs={{0,6},{1,7},{2,0},{3,1},{4,2},{5,3},{6,4},{7,5},{8,14},{9,15},{10,... | collective-permute-start | bytes 294920 | tf_op jit(solution)/shard_map/ppermute | solution.py:139
  90.4 6.5 %collective-permute-start.5 = (f16[3,8,2048]{2,1,0:T(8,128)(2,1)S(1)}, f16[3,8,2048]{2,1,0:T(8,128)(2,1)S(1)}, u32[]{:S(2)}, u32[]{:S(2)}) collective-permute-start(f16[3,8,2048]{2,1,0:T(8,128)(2,1)S(1)} %get-tuple-element.18), channel_id=1, source_target_pairs={{0,4},{1,5},{2,6},{3,7},{4,0},{5,1},{6,2},{7,3},{8,12},{9,13},{10,... | collective-permute-start | bytes 294920 | tf_op jit(solution)/shard_map/ppermute | solution.py:139
  97.0 15.1 %collective-permute-start.7 = (bf16[3,8,2048]{2,1,0:T(8,128)(2,1)S(1)}, bf16[3,8,2048]{2,1,0:T(8,128)(2,1)S(1)}, u32[]{:S(2)}, u32[]{:S(2)}) collective-permute-start(bf16[3,8,2048]{2,1,0:T(8,128)(2,1)S(1)} %get-tuple-element.10), channel_id=1, source_target_pairs={{0,2},{1,3},{2,4},{3,5},{4,6},{5,7},{6,0},{7,1},{8,10},{9,11},{10,... | collective-permute-start | bytes 294920 | tf_op jit(solution)/shard_map/ppermute | solution.py:139
  108.4 7.1 %collective-permute-start.8 = (bf16[3,8,2048]{2,1,0:T(8,128)(2,1)S(1)}, bf16[3,8,2048]{2,1,0:T(8,128)(2,1)S(1)}, u32[]{:S(2)}, u32[]{:S(2)}) collective-permute-start(bf16[3,8,2048]{2,1,0:T(8,128)(2,1)S(1)} %get-tuple-element.10), channel_id=1, source_target_pairs={{0,4},{1,5},{2,6},{3,7},{4,0},{5,1},{6,2},{7,3},{8,12},{9,13},{10,... | collective-permute-start | bytes 294920 | tf_op jit(solution)/shard_map/ppermute | solution.py:139
  111.9 4.7 %collective-permute-start.9 = (bf16[3,8,2048]{2,1,0:T(8,128)(2,1)S(1)}, bf16[3,8,2048]{2,1,0:T(8,128)(2,1)S(1)}, u32[]{:S(2)}, u32[]{:S(2)}) collective-permute-start(bf16[3,8,2048]{2,1,0:T(8,128)(2,1)S(1)} %get-tuple-element.10), channel_id=1, source_target_pairs={{0,6},{1,7},{2,0},{3,1},{4,2},{5,3},{6,4},{7,5},{8,14},{9,15},{10,... | collective-permute-start | bytes 294920 | tf_op jit(solution)/shard_map/ppermute | solution.py:139
  116.7 14.6 %collective-permute-start.10 = (bf16[2,4,8,2048]{3,2,1,0:T(8,128)(2,1)S(1)}, bf16[2,4,8,2048]{3,2,1,0:T(8,128)(2,1)S(1)}, u32[]{:S(2)}, u32[]{:S(2)}) collective-permute-start(bf16[2,4,8,2048]{3,2,1,0:T(8,128)(2,1)S(1)} %pad_maximum_fusion.2), channel_id=1, source_target_pairs={{0,8},{8,16},{16,24},{24,0},{1,9},{9,17},{17,25},{25,1},{2,10},{10... | collective-permute-start | bytes 786440 | tf_op jit(solution)/shard_map/ppermute | solution.py:144
  124.1 10.6 %collective-permute-start.11 = (bf16[2,4,8,2048]{3,2,1,0:T(8,128)(2,1)S(1)}, bf16[2,4,8,2048]{3,2,1,0:T(8,128)(2,1)S(1)}, u32[]{:S(2)}, u32[]{:S(2)}) collective-permute-start(bf16[2,4,8,2048]{3,2,1,0:T(8,128)(2,1)S(1)} %pad_maximum_fusion.3), channel_id=1, source_target_pairs={{0,16},{8,24},{16,0},{24,8},{1,17},{9,25},{17,1},{25,9},{2,18},{10... | collective-permute-start | bytes 786440 | tf_op jit(solution)/shard_map/ppermute | solution.py:144
  124.8 9.9 %collective-permute-start.12 = (bf16[2,4,8,2048]{3,2,1,0:T(8,128)(2,1)S(1)}, bf16[2,4,8,2048]{3,2,1,0:T(8,128)(2,1)S(1)}, u32[]{:S(2)}, u32[]{:S(2)}) collective-permute-start(bf16[2,4,8,2048]{3,2,1,0:T(8,128)(2,1)S(1)} %pad_maximum_fusion.4), channel_id=1, source_target_pairs={{0,24},{8,0},{16,8},{24,16},{1,25},{9,1},{17,9},{25,17},{2,26},{10... | collective-permute-start | bytes 786440 | tf_op jit(solution)/shard_map/ppermute | solution.py:144
  134.8 2.7 %collective-permute-start.13 = (bf16[2,4,4,8,2048]{4,3,2,1,0:T(8,128)(2,1)S(1)}, bf16[2,4,4,8,2048]{4,3,2,1,0:T(8,128)(2,1)S(1)}, u32[]{:S(2)}, u32[]{:S(2)}) collective-permute-start(bf16[2,4,4,8,2048]{4,3,2,1,0:T(8,128)(2,1)S(1)} %bitcast_dynamic-update-slice_fusion.2), channel_id=1, source_target_pairs={{0,1},{1,0},{2,3},{3,2},{4,5},{5,4},{6,7},{7,6},{8,9},{9,8},{10,11... | collective-permute-start | bytes 3145736 | tf_op jit(solution)/shard_map/ppermute | solution.py:134
  158.9 1.4 collective-permute-start.14
  161.3 22.1 %collective-permute-start.15 = (f32[2,4,8,128]{3,2,1,0:T(8,128)S(1)}, f32[2,4,8,128]{3,2,1,0:T(8,128)S(1)}, u32[]{:S(2)}, u32[]{:S(2)}) collective-permute-start(f32[2,4,8,128]{3,2,1,0:T(8,128)S(1)} %get-tuple-element.27), channel_id=1, source_target_pairs={{0,2},{1,3},{2,4},{3,5},{4,6},{5,7},{6,0},{7,1},{8,10},{9,11},{10,... | collective-permute-start | bytes 98312 | tf_op jit(solution)/shard_map/ppermute | solution.py:139
  164.2 19.2 %collective-permute-start.17 = (f32[2,4,8,128]{3,2,1,0:T(8,128)S(1)}, f32[2,4,8,128]{3,2,1,0:T(8,128)S(1)}, u32[]{:S(2)}, u32[]{:S(2)}) collective-permute-start(f32[2,4,8,128]{3,2,1,0:T(8,128)S(1)} %get-tuple-element.28), channel_id=1, source_target_pairs={{0,6},{1,7},{2,0},{3,1},{4,2},{5,3},{6,4},{7,5},{8,14},{9,15},{10,... | collective-permute-start | bytes 98312 | tf_op jit(solution)/shard_map/ppermute | solution.py:139
  167.1 16.3 %collective-permute-start.16 = (f32[2,4,8,128]{3,2,1,0:T(8,128)S(1)}, f32[2,4,8,128]{3,2,1,0:T(8,128)S(1)}, u32[]{:S(2)}, u32[]{:S(2)}) collective-permute-start(f32[2,4,8,128]{3,2,1,0:T(8,128)S(1)} %get-tuple-element.29), channel_id=1, source_target_pairs={{0,4},{1,5},{2,6},{3,7},{4,0},{5,1},{6,2},{7,3},{8,12},{9,13},{10,... | collective-permute-start | bytes 98312 | tf_op jit(solution)/shard_map/ppermute | solution.py:139
  183.5 21.7 %collective-permute-start.18 = (f32[2,8,128]{2,1,0:T(8,128)S(1)}, f32[2,8,128]{2,1,0:T(8,128)S(1)}, u32[]{:S(2)}, u32[]{:S(2)}) collective-permute-start(f32[2,8,128]{2,1,0:T(8,128)S(1)} %get-tuple-element.30), channel_id=1, source_target_pairs={{0,8},{8,16},{16,24},{24,0},{1,9},{9,17},{17,25},{25,1},{2,10},{10... | collective-permute-start | bytes 24584 | tf_op jit(solution)/shard_map/ppermute | solution.py:144
  185.3 19.9 %collective-permute-start.20 = (f32[2,8,128]{2,1,0:T(8,128)S(1)}, f32[2,8,128]{2,1,0:T(8,128)S(1)}, u32[]{:S(2)}, u32[]{:S(2)}) collective-permute-start(f32[2,8,128]{2,1,0:T(8,128)S(1)} %get-tuple-element.31), channel_id=1, source_target_pairs={{0,24},{8,0},{16,8},{24,16},{1,25},{9,1},{17,9},{25,17},{2,26},{10... | collective-permute-start | bytes 24584 | tf_op jit(solution)/shard_map/ppermute | solution.py:144
  186.4 18.7 %collective-permute-start.19 = (f32[2,8,128]{2,1,0:T(8,128)S(1)}, f32[2,8,128]{2,1,0:T(8,128)S(1)}, u32[]{:S(2)}, u32[]{:S(2)}) collective-permute-start(f32[2,8,128]{2,1,0:T(8,128)S(1)} %get-tuple-element.32), channel_id=1, source_target_pairs={{0,16},{8,24},{16,0},{24,8},{1,17},{9,25},{17,1},{25,9},{2,18},{10... | collective-permute-start | bytes 24584 | tf_op jit(solution)/shard_map/ppermute | solution.py:144

commit v2 on v0

v2 whole, which is shorter than its diff:
```python
import jax
import jax.numpy as jnp
from jax import lax
from jax.experimental import pallas as pl
from jax.experimental.pallas import tpu as pltpu
from jax.sharding import PartitionSpec as P

f32 = jnp.float32
bf16 = jnp.bfloat16
i32 = jnp.int32
LANES = 128
WIRE_SCALE = 128.0
VMEM_LIMIT = 56 << 20
NT = (((1,), (1,)), ((), ()))
TN = (((0,), (0,)), ((), ()))


def split(x):
    hi = x.astype(bf16)
    return hi, (x - hi.astype(f32)).astype(bf16)


def cost(flops, nbytes):
    return pl.CostEstimate(flops=int(flops), bytes_accessed=int(nbytes), transcendentals=0)


def params():
    return pltpu.CompilerParams(vmem_limit_bytes=VMEM_LIMIT)


def lay_out(features, idx_ref, val_ref, ids_ref, val_scr, pairs, zs):
    tokens = idx_ref.shape[1]
    rows = tokens // (pairs * zs * 2)
    p, feat = lax.axis_index("pair"), lax.axis_index("feat")
    first = feat * features

    def run(at, _):
        zr = at & (zs - 1)
        pr = (at // zs) & (pairs - 1)
        cr = at // (zs * pairs)
        block = (p ^ pr) * (zs * 2) + (feat ^ (zr * 2 + cr))
        ids_ref[0, pl.ds(at * rows, rows), :] = idx_ref[0, pl.ds(block * rows, rows), :] - first
        val_scr[pl.ds(at * rows, rows), :] = val_ref[0, pl.ds(block * rows, rows), :]
        return 0

    lax.fori_loop(0, tokens // rows, run, 0)


def build_acts(ids_ref, val_scr, acts_ref, rows_scr, hi_scr, lo_scr, vhi_scr, vlo_scr, span):
    _, tokens, active = ids_ref.shape
    blocks = acts_ref.shape[-1] // LANES
    pitch = 2 * blocks + 1
    iota_block = lax.broadcasted_iota(i32, (blocks, active), 0)
    iota_lane = lax.broadcasted_iota(i32, (LANES, active), 0)
    ids = ids_ref[0]
    vhi, vlo = split(val_scr[...])
    hi_scr[...] = ids >> 7
    lo_scr[...] = ids & 127
    vhi_scr[...] = vhi.astype(f32)
    vlo_scr[...] = vlo.astype(f32)
    empty = jnp.zeros((2 * blocks, active), bf16)

    def factors(at):
        def row(ref, count):
            return jnp.broadcast_to(ref[pl.ds(at, 1), :], (count, active))

        hit = row(hi_scr, blocks) == iota_block
        high = jnp.where(hit, row(vhi_scr, blocks), 0.0)
        low = jnp.where(hit, row(vlo_scr, blocks), 0.0)
        weights = jnp.concatenate([high, low], axis=0).astype(bf16)
        onehot = jnp.where(row(lo_scr, LANES) == iota_lane, 1.0, 0.0).astype(bf16)
        return weights, onehot

    def part(b, _):
        base = pl.multiple_of(b * span, span)
        for i in range(0, span, 2):
            w0, o0 = factors(base + i)
            w1, o1 = factors(base + i + 1)
            weights = jnp.concatenate(
                [jnp.concatenate([w0, empty], axis=1), jnp.concatenate([empty, w1], axis=1)], axis=0
            )
            onehot = jnp.concatenate([o0, o1], axis=1)
            got = lax.dot_general(weights, onehot, NT, preferred_element_type=f32)
            rows_scr[i * pitch:i * pitch + 2 * blocks, :] = got[:2 * blocks]
            rows_scr[(i + 1) * pitch:(i + 1) * pitch + 2 * blocks, :] = got[2 * blocks:]
        for h in range(blocks):
            lanes = slice(h * LANES, (h + 1) * LANES)
            high = rows_scr[pl.ds(h, span, stride=pitch), :]
            low = rows_scr[pl.ds(blocks + h, span, stride=pitch), :]
            acts_ref[0, pl.ds(base, span), lanes] = high.astype(bf16)
            acts_ref[0, pl.ds(tokens + base, span), lanes] = low.astype(bf16)
        return 0

    lax.fori_loop(0, tokens // span, part, 0)


def recon_kernel(pairs, zs, span, map_ref, idx_ref, val_ref, dec_ref, keep_ref, send_ref, acts_ref, ids_ref, val_scr, *scr):
    @pl.when(pl.program_id(1) == 0)
    def _():
        lay_out(acts_ref.shape[-1], idx_ref, val_ref, ids_ref, val_scr, pairs, zs)
        build_acts(ids_ref, val_scr, acts_ref, *scr, span)

    tokens = idx_ref.shape[1]
    dhi, dlo = split(dec_ref[0])
    both = jnp.dot(acts_ref[0], dhi, preferred_element_type=f32)
    low = jnp.dot(acts_ref[0, :tokens], dlo, preferred_element_type=f32)
    prod = both[:tokens] + both[tokens:] + low
    keep_ref[0] = prod[:tokens // 2]
    send_ref[0] = prod[tokens // 2:]


def recon_call(pair_map, indices, values, decoder, pairs, zs, tile=512, span=64):
    slots, features, width = decoder.shape
    layers, tokens, active = indices.shape
    tile = min(tile, width)
    blocks = features // LANES
    layer = pl.BlockSpec((1, tokens, active), lambda j, n, m: (jnp.minimum(m[j, 0], layers - 1), 0, 0))
    half = pl.BlockSpec((1, tokens // 2, tile), lambda j, n, m: (j, 0, n))

    def kernel(*refs):
        recon_kernel(pairs, zs, span, *refs)

    def slot(rows, cols):
        return pl.BlockSpec((1, rows, cols), lambda j, n, m: (j, 0, 0))

    return pl.pallas_call(
        kernel,
        out_shape=(
            jax.ShapeDtypeStruct((slots, tokens // 2, width), f32),
            jax.ShapeDtypeStruct((slots, tokens // 2, width), f32),
            jax.ShapeDtypeStruct((slots, 2 * tokens, features), bf16),
            jax.ShapeDtypeStruct((slots, tokens, active), i32),
        ),
        grid_spec=pltpu.PrefetchScalarGridSpec(
            num_scalar_prefetch=1,
            grid=(slots, width // tile),
            in_specs=[layer, layer, pl.BlockSpec((1, features, tile), lambda j, n, m: (j, 0, n))],
            out_specs=[half, half, slot(2 * tokens, features), slot(tokens, active)],
            scratch_shapes=[
                pltpu.VMEM((tokens, active), f32),
                pltpu.VMEM((span * (2 * blocks + 1) + 8, LANES), f32),
                pltpu.VMEM((tokens, active), i32),
                pltpu.VMEM((tokens, active), i32),
                pltpu.VMEM((tokens, active), f32),
                pltpu.VMEM((tokens, active), f32),
            ],
        ),
        compiler_params=params(),
        cost_estimate=cost(6 * slots * tokens * features * width, 4 * slots * features * width),
        name="recon",
    )(pair_map, indices, values, decoder)


def gather_errors(pieces, err_scr):
    at = 0
    for piece in pieces:
        rows = piece.shape[1]
        err_scr[at:at + rows] = piece[0]
        at += rows


def back_kernel(count, ids_ref, *refs):
    pieces, (dec_ref, keep_ref, send_ref, out_ref, err_scr) = refs[:count], refs[count:]
    n = pl.program_id(1)
    depth = dec_ref.shape[1]

    @pl.when(n == 0)
    def _():
        out_ref[...] = jnp.zeros_like(out_ref)
        gather_errors(pieces, err_scr)

    dhi, dlo = split(dec_ref[0])
    err = err_scr[...]
    grad = lax.dot_general(err, dhi, NT, preferred_element_type=f32)
    grad += lax.dot_general(err, dlo, NT, preferred_element_type=f32)
    ids = ids_ref[0] - n * depth
    block = ids >> 7
    lane = ids & 127
    total = out_ref[...]
    for c in range(depth // LANES):
        picked = jnp.take_along_axis(grad[:, c * LANES:(c + 1) * LANES], lane, axis=1)
        total = jnp.where(block == c, picked, total)
    out_ref[...] = total

    @pl.when(n == pl.num_programs(1) - 1)
    def _():
        half = total.shape[0] // 2
        keep_ref[0] = total[:half]
        send_ref[0] = total[half:]


def back_call(ids, pieces, decoder, depth=512):
    slots, features, width = decoder.shape
    _, tokens, active = ids.shape
    depth = min(depth, features)

    def kernel(*refs):
        back_kernel(len(pieces), *refs)

    return pl.pallas_call(
        kernel,
        out_shape=[jax.ShapeDtypeStruct((slots, tokens // 2, active), f32)] * 2,
        grid=(slots, features // depth),
        in_specs=[pl.BlockSpec((1, tokens, active), lambda j, n: (j, 0, 0))]
        + [pl.BlockSpec((1, x.shape[1], width), lambda j, n: (j, 0, 0)) for x in pieces]
        + [pl.BlockSpec((1, depth, width), lambda j, n: (j, n, 0))],
        out_specs=[pl.BlockSpec((1, tokens // 2, active), lambda j, n: (j, 0, 0))] * 2,
        scratch_shapes=[pltpu.VMEM((tokens, active), f32), pltpu.VMEM((tokens, width), bf16)],
        compiler_params=params(),
        cost_estimate=cost(4 * slots * tokens * features * width, 4 * slots * features * width),
        name="back",
    )(ids, *pieces, decoder)


def grad_kernel(count, acts_ref, *refs):
    pieces, (out_ref, err_scr) = refs[:count], refs[-2:]
    tokens = err_scr.shape[0] // 2

    @pl.when(pl.program_id(0) == 0)
    def _():
        gather_errors(pieces, err_scr)
        err_scr[tokens:] = err_scr[:tokens]

    out_ref[0] = lax.dot_general(acts_ref[0], err_scr[...], TN, preferred_element_type=f32)


def grad_call(acts, pieces, slot, earlier, depth=512):
    slots, rows, features = acts.shape
    width = pieces[0].shape[2]
    depth = min(depth, features)
    count = len(pieces)

    def kernel(*refs):
        grad_kernel(count, *refs)

    more = [] if earlier is None else [earlier]
    return pl.pallas_call(
        kernel,
        out_shape=jax.ShapeDtypeStruct((slots, features, width), f32),
        grid=(features // depth,),
        in_specs=[pl.BlockSpec((1, rows, depth), lambda n: (slot, 0, n))]
        + [pl.BlockSpec((1, x.shape[1], width), lambda n: (slot, 0, 0)) for x in pieces]
        + [pl.BlockSpec(memory_space=pl.ANY)] * len(more),
        out_specs=pl.BlockSpec((1, depth, width), lambda n: (slot, n, 0)),
        scratch_shapes=[pltpu.VMEM((rows, width), bf16)],
        input_output_aliases={count + 1: 0} if more else {},
        compiler_params=params(),
        cost_estimate=cost(2 * rows * features * width, 4 * features * width),
        name="grad",
    )(acts, *pieces, *more)


def layer_sums(tables, blocks, layers):
    shape = blocks[0].shape[1:]

    def kernel(table_ref, *refs):
        out_ref = refs[-1]
        out_ref[...] = jnp.zeros_like(out_ref)
        for m, ref in enumerate(refs[:-1]):
            for j in range(ref.shape[0]):
                goal = table_ref[m, j]

                @pl.when(goal < layers)
                def _():
                    out_ref[goal] = out_ref[goal] + ref[j]

    return pl.pallas_call(
        kernel,
        out_shape=jax.ShapeDtypeStruct((layers,) + shape, f32),
        in_specs=[pl.BlockSpec(memory_space=pltpu.SMEM)] + [pl.BlockSpec(memory_space=pltpu.VMEM)] * len(blocks),
        out_specs=pl.BlockSpec(memory_space=pltpu.VMEM),
        compiler_params=params(),
        name="layer_sums",
    )(jnp.stack(tables), *blocks)


def choose_layers(tables, errors, slots):
    layers, rows, width = errors[0].shape
    if rows % 8:
        column = jnp.concatenate(errors, axis=1)
        out = []
        for table in tables:
            picked = [
                sum(jnp.where(table[j] == layer, column[layer], jnp.zeros((), bf16)) for layer in range(layers))
                for j in range(slots)
            ]
            out.append(jnp.stack(picked))
        return out
    count = len(tables)
    total = len(errors) * rows

    def kernel(table_ref, *refs):
        for m, out_ref in enumerate(refs[len(errors):]):
            for j in range(slots):
                goal = table_ref[m, j]
                at = jnp.minimum(goal, layers - 1)
                live = jnp.where(goal < layers, 1.0, 0.0)
                wide = jnp.concatenate([ref[at].astype(f32) for ref in refs[:len(errors)]], axis=0)
                out_ref[j] = (wide * live).astype(bf16)

    return pl.pallas_call(
        kernel,
        out_shape=[jax.ShapeDtypeStruct((slots, total, width), bf16)] * count,
        in_specs=[pl.BlockSpec(memory_space=pltpu.SMEM)] + [pl.BlockSpec(memory_space=pltpu.VMEM)] * len(errors),
        out_specs=[pl.BlockSpec(memory_space=pltpu.VMEM)] * count,
        compiler_params=params(),
        name="choose_layers",
    )(jnp.stack(tables), *errors)


def swap_cores(x):
    return lax.ppermute(x, "feat", [(i, i ^ 1) for i in range(lax.axis_size("feat"))])


def swap_z(x, m):
    return lax.ppermute(x, "feat", [(i, i ^ (2 * m)) for i in range(lax.axis_size("feat"))])


def swap_pair(x, m):
    return lax.ppermute(x, "pair", [(i, i ^ m) for i in range(lax.axis_size("pair"))])


def pack(x):
    return (x * WIRE_SCALE).astype(jnp.float16)


def unpack(x):
    return x.astype(f32) * (1.0 / WIRE_SCALE)


def weigh(tables, blocks, layers):
    total = 0.0
    for table, block in zip(tables, blocks):
        for j in range(block.shape[0]):
            chosen = (jnp.arange(layers, dtype=i32) == table[j]).astype(f32)
            total = total + chosen[:, None, None] * block[j][None]
    return total


def sum_full(keep, send, pair_map, layers):
    pairs, zs = lax.axis_size("pair"), lax.axis_size("feat") // 2
    run = keep.shape[1] // pairs
    rows = run // zs
    got = swap_cores(send)
    halves = [keep[:, m * run:(m + 1) * run] + got[:, m * run:(m + 1) * run] for m in range(pairs)]
    packed = [pack(x) for x in halves[1:]]
    arrived = [None] + [swap_pair(packed[m - 1], m) for m in range(1, pairs)]
    pair_map, _ = lax.optimization_barrier((pair_map, packed[0]))
    maps = [pair_map] + [swap_pair(pair_map, m) for m in range(1, pairs)]
    sources = [x[:, 0] for x in maps]
    goals = [x[:, 1] for x in maps]
    parts = []
    for k in range(zs):
        cut = slice(k * rows, (k + 1) * rows)
        blocks = [halves[0][:, cut]] + [unpack(x[:, cut]) for x in arrived[1:]]
        parts.append(weigh(goals, blocks, layers))
    sent = [pack(x) for x in parts[1:]]
    full = parts[0]
    for m in range(1, zs):
        full = full + unpack(swap_z(sent[m - 1], m))
    return full, sources, goals


def spread_errors(error, goals, slots):
    pairs, zs = lax.axis_size("pair"), lax.axis_size("feat") // 2
    errors = [error] + [swap_z(error, m) for m in range(1, zs)]
    chosen = choose_layers(goals, errors, slots)
    own = [chosen[0]] + [swap_pair(chosen[m], m) for m in range(1, pairs)]
    return own + [swap_cores(x) for x in own]


def finish(keep, send, sources, layers, acts, pieces):
    pairs, zs = lax.axis_size("pair"), lax.axis_size("feat") // 2
    slots, half_rows, width = keep.shape
    rows = half_rows // (pairs * zs)
    half = (keep + swap_cores(send)).reshape(slots, pairs, zs, rows, width)
    arrived = [half[:, :, 0]] + [swap_z(half[:, :, m], m) for m in range(1, zs)]
    dec_grad = None
    for j in range(0, slots - 1):
        dec_grad = grad_call(acts, pieces, j, dec_grad)
    if dec_grad is not None:
        dec_grad, *arrived = lax.optimization_barrier((dec_grad, *arrived))
    column = sum(arrived)
    arrived = [column[:, 0]] + [swap_pair(column[:, m], m) for m in range(1, pairs)]
    dec_grad = grad_call(acts, pieces, slots - 1, dec_grad)
    dec_grad, *arrived = lax.optimization_barrier((dec_grad, *arrived))
    return dec_grad, layer_sums(sources, arrived, layers)


def body(decoder, pair_map, indices, values, target):
    slots = decoder.shape[0]
    layers = indices.shape[0]
    pairs, zs = lax.axis_size("pair"), lax.axis_size("feat") // 2
    keep, send, acts, ids = recon_call(pair_map, indices, values, decoder, pairs, zs)
    full, sources, goals = sum_full(keep, send, pair_map, layers)
    recon = full.astype(bf16)
    error = (full - target).astype(bf16)
    pieces = spread_errors(error, goals, slots)
    keep, send = back_call(ids, pieces, decoder)
    dec_grad, feat_grad = finish(keep, send, sources, layers, acts, pieces)
    return recon, dec_grad, feat_grad


def solution(mesh):
    in_specs = (P("pair", "feat", None), P("pair", None), P(), P(), P(None, ("pair", "feat"), None))
    out_specs = (
        P(None, ("pair", "feat"), None),
        P("pair", "feat", None),
        P(None, ("pair", "feat"), None),
    )
    return jax.shard_map(body, mesh=mesh, in_specs=in_specs, out_specs=out_specs, check_vma=False)
```

time: 815 us -> 148 us (0.18); the launches traced: 806 us -> 148 us
  matrix products: 496 us -> 0 us
  waiting for transfers between devices: 239 us -> 27.3 us
  Pallas kernels: 0 us -> 70.7 us
  starting transfers between devices: 0.16 us -> 31.3 us
  other arithmetic: 31.5 us -> 10.9 us
  between operations: 16.4 us -> 1.02 us
  blocking collectives: 9.47 us -> 0 us
    dot_general x12 -> x0, matrix products: 496 us -> none  [the longest x2 243 us: body(): jnp.einsum('tkf,tf->tk', matches, back, precision=lax.Precision.HIGHEST,...]
    reduce_scatter x2 -> x0, waiting for transfers between devices: 162 us -> none  [the longest x1 110 us: body(): lax.psum_scatter(feature_term, ('pair', 'feat'), scatter_dimension=1, til...]
    pallas_call x0 -> x6, Pallas kernels: none -> 70.7 us  [the longest x1 29.7 us: recon_call(): pl.pallas_call(kernel, out_shape=(jax.ShapeDtypeStruct((slots, tokens //...]
    unnamed x5 -> x0, waiting for transfers between devices: 49.6 us -> none
    ppermute x0 -> x27, starting transfers between devices: none -> 31.3 us  [the longest x9 15.1 us: swap_z(): lax.ppermute(x, 'feat', [(i, i ^ 2 * m) for i in range(lax.axis_size('fea...]
    ppermute x0 -> x27, waiting for transfers between devices: none -> 27.3 us  [the longest x12 10.8 us: swap_pair(): lax.ppermute(x, 'pair', [(i, i ^ m) for i in range(lax.axis_size('pair'))])]
    all_gather x1 -> x0, waiting for transfers between devices: 27.2 us -> none  [body(): gathered = lax.all_gather(chosen, 'feat', axis=1, tiled=True)]
    another operation x1 -> x2, other arithmetic: 23.3 us -> 1.19 us  [the longest x1 0.6 us: layer_sums(): jnp.stack(tables)]
  transfers between devices with their start and end apart: 4 -> 27, of which waited for: 4 -> 11; matrix products, arithmetic and copies ran while one was open for 3% -> 7% of each run, Pallas kernels for 0% -> 13%
where the time goes in v2:
time: 148 us
  Pallas kernels  70.7 us (48%)
  starting transfers between devices  31.3 us (21%)
  waiting for transfers between devices  27.3 us (18%)
  other arithmetic  10.9 us (7%)
  local copies, waits for them, and re-layouts  6.39 us (4%)
    pallas_call x1, Pallas kernels, recon_call(): pl.pallas_call(kernel, out_shape=(jax.ShapeDtypeStruct((slots, tokens //...  29.7 us
    pallas_call x2, Pallas kernels, grad_call(): pl.pallas_call(kernel, out_shape=jax.ShapeDtypeStruct((slots, features, w...  19 us
    pallas_call x1, Pallas kernels, back_call(): pl.pallas_call(kernel, out_shape=[jax.ShapeDtypeStruct((slots, tokens //...  18.4 us
    ppermute x9, starting transfers between devices, swap_z(): lax.ppermute(x, 'feat', [(i, i ^ 2 * m) for i in range(lax.axis_size('fea...  15.1 us
    ppermute x12, starting transfers between devices, swap_pair(): lax.ppermute(x, 'pair', [(i, i ^ m) for i in range(lax.axis_size('pair'))])  15 us
    ppermute x12, waiting for transfers between devices, swap_pair(): lax.ppermute(x, 'pair', [(i, i ^ m) for i in range(lax.axis_size('pair'))])  10.8 us
    ppermute x9, waiting for transfers between devices, swap_z(): lax.ppermute(x, 'feat', [(i, i ^ 2 * m) for i in range(lax.axis_size('fea...  10.4 us
    ppermute x6, waiting for transfers between devices, swap_cores(): lax.ppermute(x, 'feat', [(i, i ^ 1) for i in range(lax.axis_size('feat'))])  6.19 us
  transfers between devices with their start and end apart: 27, of which 11 were waited for; matrix products, arithmetic and copies ran while one was open for 7% of the time, Pallas kernels for 13%

profile of v2, /device:TPU:0, one launch (start us, length us, event | category | flops | bytes accessed | tf_op | source)
XLA Modules:
  0.0 147.5 jit_solution(7228919385676361739)
XLA Ops:
  0.6 29.7 %recon.1 = (f32[2,128,2048]{2,1,0:T(8,128)}, f32[2,128,2048]{2,1,0:T(8,128)}, bf16[2,512,2048]{2,1,0:T(8,128)(2,1)}, s32[2,256,128]{2,1,0:T(8,128)}) custom-call(s32[2,2]{1,0:T(2,128)} %refs_0_.1, s32[3,256,128]{2,1,0:T(8,128)} %refs_1_.1, f32[3,256,128]{2,1,0:T(8,128)} %refs_2_.1, f32[2,2048,2048]{2,1,0:T(8,128)} %refs_9_.1), custom_call_target="tpu_custom_call" | custom-call | flops 12884901888 | bytes 33554432 | tf_op jit(solution)/shard_map/recon/pallas_call | solution.py:126
  30.8 4.0 %collective-permute-done = f32[2,128,2048]{2,1,0:T(8,128)S(1)} collective-permute-done((f32[2,128,2048]{2,1,0:T(8,128)}, f32[2,128,2048]{2,1,0:T(8,128)S(1)}, u32[]{:S(2)}, u32[]{:S(2)}) %collective-permute-start) | collective-permute-done | bytes 2097184 | tf_op jit(solution)/shard_map/ppermute | solution.py:312
  34.8 1.9 %slice_add_fusion.2 = (f32[2,32,2048]{2,1,0:T(8,128)S(1)}, f16[2,32,2048]{2,1,0:T(8,128)(2,1)S(1)}, f16[2,32,2048]{2,1,0:T(8,128)(2,1)S(1)}, f16[2,32,2048]{2,1,0:T(8,128)(2,1)S(1)}) fusion(f32[2,128,2048]{2,1,0:T(8,128)S(1)} %collective-permute-done, f32[2,128,2048]{2,1,0:T(8,128)} %get-tuple-element.24), kind=kLoop, calls=%fused_computation.6 | loop fusion | flops 1310720 | bytes 5505024 | tf_op jit(solution)/shard_map/add | solution.py:345
  36.7 2.8 %collective-permute-start.1 = (s32[2,2]{1,0:T(2,128)S(1)}, s32[2,2]{1,0:T(2,128)S(1)}, u32[]{:S(2)}, u32[]{:S(2)}) collective-permute-start(s32[2,2]{1,0:T(2,128)S(1)} %copy-done.12), channel_id=1, source_target_pairs={{0,8},{8,0},{16,24},{24,16},{1,9},{9,1},{17,25},{25,17},{2,10},{10... | collective-permute-start | bytes 56 | tf_op jit(solution)/shard_map/ppermute | solution.py:320
  39.5 1.6 %collective-permute-start.3 = (s32[2,2]{1,0:T(2,128)S(1)}, s32[2,2]{1,0:T(2,128)S(1)}, u32[]{:S(2)}, u32[]{:S(2)}) collective-permute-start(s32[2,2]{1,0:T(2,128)S(1)} %copy-done.12), channel_id=1, source_target_pairs={{0,16},{8,24},{16,0},{24,8},{1,17},{9,25},{17,1},{25,9},{2,18},{10... | collective-permute-start | bytes 56 | tf_op jit(solution)/shard_map/ppermute | solution.py:320
  41.7 1.9 %collective-permute-start.2 = (f16[2,32,2048]{2,1,0:T(8,128)(2,1)S(1)}, f16[2,32,2048]{2,1,0:T(8,128)(2,1)S(1)}, u32[]{:S(2)}, u32[]{:S(2)}) collective-permute-start(f16[2,32,2048]{2,1,0:T(8,128)(2,1)S(1)} %get-tuple-element.58), channel_id=1, source_target_pairs={{0,8},{8,0},{16,24},{24,16},{1,9},{9,1},{17,25},{25,17},{2,10},{10... | collective-permute-start | bytes 786440 | tf_op jit(solution)/shard_map/ppermute | solution.py:320
  43.8 1.7 %collective-permute-start.4 = (f16[2,32,2048]{2,1,0:T(8,128)(2,1)S(1)}, f16[2,32,2048]{2,1,0:T(8,128)(2,1)S(1)}, u32[]{:S(2)}, u32[]{:S(2)}) collective-permute-start(f16[2,32,2048]{2,1,0:T(8,128)(2,1)S(1)} %get-tuple-element.57), channel_id=1, source_target_pairs={{0,16},{8,24},{16,0},{24,8},{1,17},{9,25},{17,1},{25,9},{2,18},{10... | collective-permute-start | bytes 786440 | tf_op jit(solution)/shard_map/ppermute | solution.py:320
  53.1 3.6 %collective-permute-done.4 = f16[2,32,2048]{2,1,0:T(8,128)(2,1)S(1)} collective-permute-done((f16[2,32,2048]{2,1,0:T(8,128)(2,1)S(1)}, f16[2,32,2048]{2,1,0:T(8,128)(2,1)S(1)}, u32[]{:S(2)}, u32[]{:S(2)}) %collective-permute-start.4) | collective-permute-done | bytes 262176 | tf_op jit(solution)/shard_map/ppermute | solution.py:320
  57.1 1.6 %collective-permute-start.7 = (f16[3,8,2048]{2,1,0:T(8,128)(2,1)S(1)}, f16[3,8,2048]{2,1,0:T(8,128)(2,1)S(1)}, u32[]{:S(2)}, u32[]{:S(2)}) collective-permute-start(f16[3,8,2048]{2,1,0:T(8,128)(2,1)S(1)} %multiply_convert_fusion.2), channel_id=1, source_target_pairs={{0,2},{1,3},{2,0},{3,1},{4,6},{5,7},{6,4},{7,5},{8,10},{9,11},{10,... | collective-permute-start | bytes 294920 | tf_op jit(solution)/shard_map/ppermute | solution.py:316
  59.1 2.7 %collective-permute-start.8 = (f16[3,8,2048]{2,1,0:T(8,128)(2,1)S(1)}, f16[3,8,2048]{2,1,0:T(8,128)(2,1)S(1)}, u32[]{:S(2)}, u32[]{:S(2)}) collective-permute-start(f16[3,8,2048]{2,1,0:T(8,128)(2,1)S(1)} %multiply_convert_fusion.1), channel_id=1, source_target_pairs={{0,4},{1,5},{2,6},{3,7},{4,0},{5,1},{6,2},{7,3},{8,12},{9,13},{10,... | collective-permute-start | bytes 294920 | tf_op jit(solution)/shard_map/ppermute | solution.py:316
  62.3 4.5 %collective-permute-done.8 = f16[3,8,2048]{2,1,0:T(8,128)(2,1)S(1)} collective-permute-done((f16[3,8,2048]{2,1,0:T(8,128)(2,1)S(1)}, f16[3,8,2048]{2,1,0:T(8,128)(2,1)S(1)}, u32[]{:S(2)}, u32[]{:S(2)}) %collective-permute-start.8) | collective-permute-done | bytes 98336 | tf_op jit(solution)/shard_map/ppermute | solution.py:316
  66.7 1.8 %collective-permute-done.9 = f16[3,8,2048]{2,1,0:T(8,128)(2,1)S(1)} collective-permute-done((f16[3,8,2048]{2,1,0:T(8,128)(2,1)S(1)}, f16[3,8,2048]{2,1,0:T(8,128)(2,1)S(1)}, u32[]{:S(2)}, u32[]{:S(2)}) %collective-permute-start.9) | collective-permute-done | bytes 98336 | tf_op jit(solution)/shard_map/ppermute | solution.py:316
  71.7 2.1 %collective-permute-start.12 = (bf16[3,8,2048]{2,1,0:T(8,128)(2,1)S(1)}, bf16[3,8,2048]{2,1,0:T(8,128)(2,1)S(1)}, u32[]{:S(2)}, u32[]{:S(2)}) collective-permute-start(bf16[3,8,2048]{2,1,0:T(8,128)(2,1)S(1)} %get-tuple-element.53.refs_0_), channel_id=1, source_target_pairs={{0,6},{1,7},{2,4},{3,5},{4,2},{5,3},{6,0},{7,1},{8,14},{9,15},{10,... | collective-permute-start | bytes 294920 | tf_op jit(solution)/shard_map/ppermute | solution.py:316
  75.3 3.2 %collective-permute-done.11.refs_2_ = bf16[3,8,2048]{2,1,0:T(8,128)(2,1)S(1)} collective-permute-done((bf16[3,8,2048]{2,1,0:T(8,128)(2,1)S(1)}, bf16[3,8,2048]{2,1,0:T(8,128)(2,1)S(1)}, u32[]{:S(2)}, u32[]{:S(2)}) %collective-permute-start.11) | collective-permute-done | bytes 98336 | tf_op jit(solution)/shard_map/ppermute | solution.py:316
  79.8 2.1 %choose_layers.1 = (bf16[2,32,2048]{2,1,0:T(8,128)(2,1)}, bf16[2,32,2048]{2,1,0:T(8,128)(2,1)}, bf16[2,32,2048]{2,1,0:T(8,128)(2,1)}, bf16[2,32,2048]{2,1,0:T(8,128)(2,1)}) custom-call(s32[4,2]{1,0:T(4,128)} %pad_add_fusion.table_ref, bf16[3,8,2048]{2,1,0:T(8,128)(2,1)} %copy-done.7, bf16[3,8,2048]{2,1,0:T(8,128)(2,1)} %copy-done.9, ...), custom_call_target="tpu_custom_call" | custom-call | tf_op jit(solution)/shard_map/choose_layers/pallas_call | solution.py:301
  83.3 2.0 %collective-permute-start.15 = (bf16[2,32,2048]{2,1,0:T(8,128)(2,1)}, bf16[2,32,2048]{2,1,0:T(8,128)(2,1)S(1)}, u32[]{:S(2)}, u32[]{:S(2)}) collective-permute-start(bf16[2,32,2048]{2,1,0:T(8,128)(2,1)} %get-tuple-element.31), channel_id=1, source_target_pairs={{0,24},{8,16},{16,8},{24,0},{1,25},{9,17},{17,9},{25,1},{2,26},{10... | collective-permute-start | bytes 786440 | tf_op jit(solution)/shard_map/ppermute | solution.py:320
  85.3 3.1 %collective-permute-done.13.refs_2_ = bf16[2,32,2048]{2,1,0:T(8,128)(2,1)S(1)} collective-permute-done((bf16[2,32,2048]{2,1,0:T(8,128)(2,1)}, bf16[2,32,2048]{2,1,0:T(8,128)(2,1)S(1)}, u32[]{:S(2)}, u32[]{:S(2)}) %collective-permute-start.13) | collective-permute-done | bytes 262176 | tf_op jit(solution)/shard_map/ppermute | solution.py:320
  88.4 4.0 %collective-permute-done.14.refs_3_ = bf16[2,32,2048]{2,1,0:T(8,128)(2,1)S(1)} collective-permute-done((bf16[2,32,2048]{2,1,0:T(8,128)(2,1)}, bf16[2,32,2048]{2,1,0:T(8,128)(2,1)S(1)}, u32[]{:S(2)}, u32[]{:S(2)}) %collective-permute-start.14) | collective-permute-done | bytes 262176 | tf_op jit(solution)/shard_map/ppermute | solution.py:320
  95.1 18.4 %back.1 = (f32[2,128,128]{2,1,0:T(8,128)}, f32[2,128,128]{2,1,0:T(8,128)}) custom-call(s32[2,256,128]{2,1,0:T(8,128)} %get-tuple-element.32.refs_0_, bf16[2,32,2048]{2,1,0:T(8,128)(2,1)} %get-tuple-element.28.refs_1_, bf16[2,32,2048]{2,1,0:T(8,128)(2,1)} %copy-done, bf16[2,32,2048]{2,1,0:T(8,128)(2,1)} %copy-done.1, bf16[2,32,2048]{2,1,0:T(8,128)(2,1)} %copy-done.2, ...), custom_call_target="tpu_custom_call" | custom-call | flops 8589934592 | bytes 33554432 | tf_op jit(solution)/shard_map/back/pallas_call | solution.py:200
  116.1 2.8 %collective-permute-start.21 = (f32[2,4,8,128]{3,2,0,1:T(8,128)S(1)}, f32[2,4,8,128]{3,2,0,1:T(8,128)S(1)}, u32[]{:S(2)}, u32[]{:S(2)}) collective-permute-start(f32[2,4,8,128]{3,2,0,1:T(8,128)S(1)} %bitcast.103), channel_id=1, source_target_pairs={{0,2},{1,3},{2,0},{3,1},{4,6},{5,7},{6,4},{7,5},{8,10},{9,11},{10,... | collective-permute-start | bytes 98312 | tf_op jit(solution)/shard_map/ppermute | solution.py:316
  118.9 1.8 %collective-permute-start.22 = (f32[2,4,8,128]{3,2,0,1:T(8,128)S(1)}, f32[2,4,8,128]{3,2,0,1:T(8,128)S(1)}, u32[]{:S(2)}, u32[]{:S(2)}) collective-permute-start(f32[2,4,8,128]{3,2,0,1:T(8,128)S(1)} %bitcast.104), channel_id=1, source_target_pairs={{0,4},{1,5},{2,6},{3,7},{4,0},{5,1},{6,2},{7,3},{8,12},{9,13},{10,... | collective-permute-start | bytes 98312 | tf_op jit(solution)/shard_map/ppermute | solution.py:316
  122.2 9.5 %grad.2.refs_9_ = f32[2,2048,2048]{2,1,0:T(8,128)} custom-call(bf16[2,512,2048]{2,1,0:T(8,128)(2,1)} %get-tuple-element.27.refs_0_, bf16[2,32,2048]{2,1,0:T(8,128)(2,1)} %get-tuple-element.28.refs_1_, bf16[2,32,2048]{2,1,0:T(8,128)(2,1)} %copy-done, bf16[2,32,2048]{2,1,0:T(8,128)(2,1)} %copy-done.1, bf16[2,32,2048]{2,1,0:T(8,128)(2,1)} %copy-done.2, ...), custom_call_target="tpu_custom_call" | custom-call | flops 4294967296 | bytes 16777216 | tf_op jit(solution)/shard_map/grad/pallas_call | solution.py:237
  133.8 2.1 %collective-permute-start.26 = (f32[2,8,128]{2,1,0:T(8,128)S(1)}, f32[2,8,128]{2,1,0:T(8,128)S(1)}, u32[]{:S(2)}, u32[]{:S(2)}) collective-permute-start(f32[2,8,128]{2,1,0:T(8,128)S(1)} %get-tuple-element.107), channel_id=1, source_target_pairs={{0,24},{8,16},{16,8},{24,0},{1,25},{9,17},{17,9},{25,1},{2,26},{10... | collective-permute-start | bytes 24584 | tf_op jit(solution)/shard_map/ppermute | solution.py:320
  135.9 9.5 %grad.3 = f32[2,2048,2048]{2,1,0:T(8,128)} custom-call(bf16[2,512,2048]{2,1,0:T(8,128)(2,1)} %get-tuple-element.27.refs_0_, bf16[2,32,2048]{2,1,0:T(8,128)(2,1)} %get-tuple-element.28.refs_1_, bf16[2,32,2048]{2,1,0:T(8,128)(2,1)} %copy-done, bf16[2,32,2048]{2,1,0:T(8,128)(2,1)} %copy-done.1, ...), custom_call_target="tpu_custom_call", output_to_operand_aliasing={{}: (9, {})} | custom-call | flops 4294967296 | bytes 16777216 | tf_op jit(solution)/shard_map/grad/pallas_call | solution.py:237
  (106 shorter events, 28.1 us)
Async XLA Ops:
  30.3 4.5 %collective-permute-start = (f32[2,128,2048]{2,1,0:T(8,128)}, f32[2,128,2048]{2,1,0:T(8,128)S(1)}, u32[]{:S(2)}, u32[]{:S(2)}) collective-permute-start(f32[2,128,2048]{2,1,0:T(8,128)} %get-tuple-element.25), channel_id=1, source_target_pairs={{0,1},{1,0},{2,3},{3,2},{4,5},{5,4},{6,7},{7,6},{8,9},{9,8},{10,11... | collective-permute-start | bytes 6291464 | tf_op jit(solution)/shard_map/ppermute | solution.py:312
  36.7 10.1 %collective-permute-start.1 = (s32[2,2]{1,0:T(2,128)S(1)}, s32[2,2]{1,0:T(2,128)S(1)}, u32[]{:S(2)}, u32[]{:S(2)}) collective-permute-start(s32[2,2]{1,0:T(2,128)S(1)} %copy-done.12), channel_id=1, source_target_pairs={{0,8},{8,0},{16,24},{24,16},{1,9},{9,1},{17,25},{25,17},{2,10},{10... | collective-permute-start | bytes 56 | tf_op jit(solution)/shard_map/ppermute | solution.py:320
  39.5 9.2 %collective-permute-start.3 = (s32[2,2]{1,0:T(2,128)S(1)}, s32[2,2]{1,0:T(2,128)S(1)}, u32[]{:S(2)}, u32[]{:S(2)}) collective-permute-start(s32[2,2]{1,0:T(2,128)S(1)} %copy-done.12), channel_id=1, source_target_pairs={{0,16},{8,24},{16,0},{24,8},{1,17},{9,25},{17,1},{25,9},{2,18},{10... | collective-permute-start | bytes 56 | tf_op jit(solution)/shard_map/ppermute | solution.py:320
  41.1 9.7 %collective-permute-start.5 = (s32[2,2]{1,0:T(2,128)S(1)}, s32[2,2]{1,0:T(2,128)S(1)}, u32[]{:S(2)}, u32[]{:S(2)}) collective-permute-start(s32[2,2]{1,0:T(2,128)S(1)} %copy-done.12), channel_id=1, source_target_pairs={{0,24},{8,16},{16,8},{24,0},{1,25},{9,17},{17,9},{25,1},{2,26},{10... | collective-permute-start | bytes 56 | tf_op jit(solution)/shard_map/ppermute | solution.py:320
  41.7 15.0 %collective-permute-start.2 = (f16[2,32,2048]{2,1,0:T(8,128)(2,1)S(1)}, f16[2,32,2048]{2,1,0:T(8,128)(2,1)S(1)}, u32[]{:S(2)}, u32[]{:S(2)}) collective-permute-start(f16[2,32,2048]{2,1,0:T(8,128)(2,1)S(1)} %get-tuple-element.58), channel_id=1, source_target_pairs={{0,8},{8,0},{16,24},{24,16},{1,9},{9,1},{17,25},{25,17},{2,10},{10... | collective-permute-start | bytes 786440 | tf_op jit(solution)/shard_map/ppermute | solution.py:320
  43.8 12.9 %collective-permute-start.4 = (f16[2,32,2048]{2,1,0:T(8,128)(2,1)S(1)}, f16[2,32,2048]{2,1,0:T(8,128)(2,1)S(1)}, u32[]{:S(2)}, u32[]{:S(2)}) collective-permute-start(f16[2,32,2048]{2,1,0:T(8,128)(2,1)S(1)} %get-tuple-element.57), channel_id=1, source_target_pairs={{0,16},{8,24},{16,0},{24,8},{1,17},{9,25},{17,1},{25,9},{2,18},{10... | collective-permute-start | bytes 786440 | tf_op jit(solution)/shard_map/ppermute | solution.py:320
  46.8 10.1 %collective-permute-start.6 = (f16[2,32,2048]{2,1,0:T(8,128)(2,1)S(1)}, f16[2,32,2048]{2,1,0:T(8,128)(2,1)S(1)}, u32[]{:S(2)}, u32[]{:S(2)}) collective-permute-start(f16[2,32,2048]{2,1,0:T(8,128)(2,1)S(1)} %get-tuple-element.56), channel_id=1, source_target_pairs={{0,24},{8,16},{16,8},{24,0},{1,25},{9,17},{17,9},{25,1},{2,26},{10... | collective-permute-start | bytes 786440 | tf_op jit(solution)/shard_map/ppermute | solution.py:320
  57.1 5.1 %collective-permute-start.7 = (f16[3,8,2048]{2,1,0:T(8,128)(2,1)S(1)}, f16[3,8,2048]{2,1,0:T(8,128)(2,1)S(1)}, u32[]{:S(2)}, u32[]{:S(2)}) collective-permute-start(f16[3,8,2048]{2,1,0:T(8,128)(2,1)S(1)} %multiply_convert_fusion.2), channel_id=1, source_target_pairs={{0,2},{1,3},{2,0},{3,1},{4,6},{5,7},{6,4},{7,5},{8,10},{9,11},{10,... | collective-permute-start | bytes 294920 | tf_op jit(solution)/shard_map/ppermute | solution.py:316
  59.1 7.7 %collective-permute-start.8 = (f16[3,8,2048]{2,1,0:T(8,128)(2,1)S(1)}, f16[3,8,2048]{2,1,0:T(8,128)(2,1)S(1)}, u32[]{:S(2)}, u32[]{:S(2)}) collective-permute-start(f16[3,8,2048]{2,1,0:T(8,128)(2,1)S(1)} %multiply_convert_fusion.1), channel_id=1, source_target_pairs={{0,4},{1,5},{2,6},{3,7},{4,0},{5,1},{6,2},{7,3},{8,12},{9,13},{10,... | collective-permute-start | bytes 294920 | tf_op jit(solution)/shard_map/ppermute | solution.py:316
  61.9 6.6 %collective-permute-start.9 = (f16[3,8,2048]{2,1,0:T(8,128)(2,1)S(1)}, f16[3,8,2048]{2,1,0:T(8,128)(2,1)S(1)}, u32[]{:S(2)}, u32[]{:S(2)}) collective-permute-start(f16[3,8,2048]{2,1,0:T(8,128)(2,1)S(1)} %multiply_convert_fusion), channel_id=1, source_target_pairs={{0,6},{1,7},{2,4},{3,5},{4,2},{5,3},{6,0},{7,1},{8,14},{9,15},{10,... | collective-permute-start | bytes 294920 | tf_op jit(solution)/shard_map/ppermute | solution.py:316
  69.4 5.9 %collective-permute-start.10 = (bf16[3,8,2048]{2,1,0:T(8,128)(2,1)S(1)}, bf16[3,8,2048]{2,1,0:T(8,128)(2,1)S(1)}, u32[]{:S(2)}, u32[]{:S(2)}) collective-permute-start(bf16[3,8,2048]{2,1,0:T(8,128)(2,1)S(1)} %get-tuple-element.53.refs_0_), channel_id=1, source_target_pairs={{0,2},{1,3},{2,0},{3,1},{4,6},{5,7},{6,4},{7,5},{8,10},{9,11},{10,... | collective-permute-start | bytes 294920 | tf_op jit(solution)/shard_map/ppermute | solution.py:316
  70.3 8.2 %collective-permute-start.11 = (bf16[3,8,2048]{2,1,0:T(8,128)(2,1)S(1)}, bf16[3,8,2048]{2,1,0:T(8,128)(2,1)S(1)}, u32[]{:S(2)}, u32[]{:S(2)}) collective-permute-start(bf16[3,8,2048]{2,1,0:T(8,128)(2,1)S(1)} %get-tuple-element.53.refs_0_), channel_id=1, source_target_pairs={{0,4},{1,5},{2,6},{3,7},{4,0},{5,1},{6,2},{7,3},{8,12},{9,13},{10,... | collective-permute-start | bytes 294920 | tf_op jit(solution)/shard_map/ppermute | solution.py:316
  71.7 6.8 %collective-permute-start.12 = (bf16[3,8,2048]{2,1,0:T(8,128)(2,1)S(1)}, bf16[3,8,2048]{2,1,0:T(8,128)(2,1)S(1)}, u32[]{:S(2)}, u32[]{:S(2)}) collective-permute-start(bf16[3,8,2048]{2,1,0:T(8,128)(2,1)S(1)} %get-tuple-element.53.refs_0_), channel_id=1, source_target_pairs={{0,6},{1,7},{2,4},{3,5},{4,2},{5,3},{6,0},{7,1},{8,14},{9,15},{10,... | collective-permute-start | bytes 294920 | tf_op jit(solution)/shard_map/ppermute | solution.py:316
  81.8 6.6 %collective-permute-start.13 = (bf16[2,32,2048]{2,1,0:T(8,128)(2,1)}, bf16[2,32,2048]{2,1,0:T(8,128)(2,1)S(1)}, u32[]{:S(2)}, u32[]{:S(2)}) collective-permute-start(bf16[2,32,2048]{2,1,0:T(8,128)(2,1)} %get-tuple-element.29), channel_id=1, source_target_pairs={{0,8},{8,0},{16,24},{24,16},{1,9},{9,1},{17,25},{25,17},{2,10},{10... | collective-permute-start | bytes 786440 | tf_op jit(solution)/shard_map/ppermute | solution.py:320
  83.1 9.4 %collective-permute-start.14 = (bf16[2,32,2048]{2,1,0:T(8,128)(2,1)}, bf16[2,32,2048]{2,1,0:T(8,128)(2,1)S(1)}, u32[]{:S(2)}, u32[]{:S(2)}) collective-permute-start(bf16[2,32,2048]{2,1,0:T(8,128)(2,1)} %get-tuple-element.30), channel_id=1, source_target_pairs={{0,16},{8,24},{16,0},{24,8},{1,17},{9,25},{17,1},{25,9},{2,18},{10... | collective-permute-start | bytes 786440 | tf_op jit(solution)/shard_map/ppermute | solution.py:320
  83.3 9.2 %collective-permute-start.15 = (bf16[2,32,2048]{2,1,0:T(8,128)(2,1)}, bf16[2,32,2048]{2,1,0:T(8,128)(2,1)S(1)}, u32[]{:S(2)}, u32[]{:S(2)}) collective-permute-start(bf16[2,32,2048]{2,1,0:T(8,128)(2,1)} %get-tuple-element.31), channel_id=1, source_target_pairs={{0,24},{8,16},{16,8},{24,0},{1,25},{9,17},{17,9},{25,1},{2,26},{10... | collective-permute-start | bytes 786440 | tf_op jit(solution)/shard_map/ppermute | solution.py:320
  85.3 7.7 %collective-permute-start.16 = (bf16[2,32,2048]{2,1,0:T(8,128)(2,1)}, bf16[2,32,2048]{2,1,0:T(8,128)(2,1)S(1)}, u32[]{:S(2)}, u32[]{:S(2)}) collective-permute-start(bf16[2,32,2048]{2,1,0:T(8,128)(2,1)} %get-tuple-element.28.refs_1_), channel_id=1, source_target_pairs={{0,1},{1,0},{2,3},{3,2},{4,5},{5,4},{6,7},{7,6},{8,9},{9,8},{10,11... | collective-permute-start | bytes 786440 | tf_op jit(solution)/shard_map/ppermute | solution.py:312
  88.4 4.6 %collective-permute-start.17 = (bf16[2,32,2048]{2,1,0:T(8,128)(2,1)S(1)}, bf16[2,32,2048]{2,1,0:T(8,128)(2,1)S(1)}, u32[]{:S(2)}, u32[]{:S(2)}) collective-permute-start(bf16[2,32,2048]{2,1,0:T(8,128)(2,1)S(1)} %collective-permute-done.13.refs_2_), channel_id=1, source_target_pairs={{0,1},{1,0},{2,3},{3,2},{4,5},{5,4},{6,7},{7,6},{8,9},{9,8},{10,11... | collective-permute-start | bytes 786440 | tf_op jit(solution)/shard_map/ppermute | solution.py:312
  116.1 15.6 %collective-permute-start.21 = (f32[2,4,8,128]{3,2,0,1:T(8,128)S(1)}, f32[2,4,8,128]{3,2,0,1:T(8,128)S(1)}, u32[]{:S(2)}, u32[]{:S(2)}) collective-permute-start(f32[2,4,8,128]{3,2,0,1:T(8,128)S(1)} %bitcast.103), channel_id=1, source_target_pairs={{0,2},{1,3},{2,0},{3,1},{4,6},{5,7},{6,4},{7,5},{8,10},{9,11},{10,... | collective-permute-start | bytes 98312 | tf_op jit(solution)/shard_map/ppermute | solution.py:316
  118.9 12.8 %collective-permute-start.22 = (f32[2,4,8,128]{3,2,0,1:T(8,128)S(1)}, f32[2,4,8,128]{3,2,0,1:T(8,128)S(1)}, u32[]{:S(2)}, u32[]{:S(2)}) collective-permute-start(f32[2,4,8,128]{3,2,0,1:T(8,128)S(1)} %bitcast.104), channel_id=1, source_target_pairs={{0,4},{1,5},{2,6},{3,7},{4,0},{5,1},{6,2},{7,3},{8,12},{9,13},{10,... | collective-permute-start | bytes 98312 | tf_op jit(solution)/shard_map/ppermute | solution.py:316
  120.8 11.0 %collective-permute-start.23 = (f32[2,4,8,128]{3,2,0,1:T(8,128)S(1)}, f32[2,4,8,128]{3,2,0,1:T(8,128)S(1)}, u32[]{:S(2)}, u32[]{:S(2)}) collective-permute-start(f32[2,4,8,128]{3,2,0,1:T(8,128)S(1)} %bitcast.105), channel_id=1, source_target_pairs={{0,6},{1,7},{2,4},{3,5},{4,2},{5,3},{6,0},{7,1},{8,14},{9,15},{10,... | collective-permute-start | bytes 98312 | tf_op jit(solution)/shard_map/ppermute | solution.py:316
  132.4 13.0 %collective-permute-start.24 = (f32[2,8,128]{2,1,0:T(8,128)S(1)}, f32[2,8,128]{2,1,0:T(8,128)S(1)}, u32[]{:S(2)}, u32[]{:S(2)}) collective-permute-start(f32[2,8,128]{2,1,0:T(8,128)S(1)} %get-tuple-element.109), channel_id=1, source_target_pairs={{0,8},{8,0},{16,24},{24,16},{1,9},{9,1},{17,25},{25,17},{2,10},{10... | collective-permute-start | bytes 24584 | tf_op jit(solution)/shard_map/ppermute | solution.py:320
  132.7 12.7 %collective-permute-start.25 = (f32[2,8,128]{2,1,0:T(8,128)S(1)}, f32[2,8,128]{2,1,0:T(8,128)S(1)}, u32[]{:S(2)}, u32[]{:S(2)}) collective-permute-start(f32[2,8,128]{2,1,0:T(8,128)S(1)} %get-tuple-element.108), channel_id=1, source_target_pairs={{0,16},{8,24},{16,0},{24,8},{1,17},{9,25},{17,1},{25,9},{2,18},{10... | collective-permute-start | bytes 24584 | tf_op jit(solution)/shard_map/ppermute | solution.py:320
  133.8 11.6 %collective-permute-start.26 = (f32[2,8,128]{2,1,0:T(8,128)S(1)}, f32[2,8,128]{2,1,0:T(8,128)S(1)}, u32[]{:S(2)}, u32[]{:S(2)}) collective-permute-start(f32[2,8,128]{2,1,0:T(8,128)S(1)} %get-tuple-element.107), channel_id=1, source_target_pairs={{0,24},{8,16},{16,8},{24,0},{1,25},{9,17},{17,9},{25,1},{2,26},{10... | collective-permute-start | bytes 24584 | tf_op jit(solution)/shard_map/ppermute | solution.py:320
  (19 other events, 47.9 us)

commit v3 on v2

--- a/solution.py
+++ b/solution.py
@@ -11,6 +11,7 @@
 LANES = 128
 WIRE_SCALE = 128.0
 VMEM_LIMIT = 56 << 20
+BACK_DEPTH = 1024
 NT = (((1,), (1,)), ((), ()))
 TN = (((0,), (0,)), ((), ()))
 
@@ -109,7 +110,7 @@
     send_ref[0] = prod[tokens // 2:]
 
 
-def recon_call(pair_map, indices, values, decoder, pairs, zs, tile=512, span=64):
+def recon_call(pair_map, indices, values, decoder, pairs, zs, tile=1024, span=64):
     slots, features, width = decoder.shape
     layers, tokens, active = indices.shape
     tile = min(tile, width)
@@ -152,102 +153,118 @@
 
 
 def gather_errors(pieces, err_scr):
-    at = 0
-    for piece in pieces:
-        rows = piece.shape[1]
-        err_scr[at:at + rows] = piece[0]
-        at += rows
-
-
-def back_kernel(count, ids_ref, *refs):
-    pieces, (dec_ref, keep_ref, send_ref, out_ref, err_scr) = refs[:count], refs[count:]
-    n = pl.program_id(1)
-    depth = dec_ref.shape[1]
+    for j in range(err_scr.shape[0]):
+        at = 0
+        for piece in pieces:
+            rows = piece.shape[1]
+            err_scr[j, at:at + rows] = piece[j]
+            at += rows
+
+
+def acts_grad(acts_ref, err):
+    return lax.dot_general(acts_ref[0], err, TN, preferred_element_type=f32)
+
+
+def back_kernel(count, slot_steps, ids_ref, acts_ref, dec_ref, *refs):
+    pieces, (keep_ref, send_ref, grad_ref, total_scr, err_scr) = refs[:count], refs[count:]
+    i = pl.program_id(0)
+    j, n = i // slot_steps, lax.rem(i, slot_steps)
+    depth, grad_depth = dec_ref.shape[1], grad_ref.shape[1]
+
+    @pl.when(i == 0)
+    def _():
+        gather_errors(pieces, err_scr)
 
     @pl.when(n == 0)
     def _():
-        out_ref[...] = jnp.zeros_like(out_ref)
-        gather_errors(pieces, err_scr)
-
-    dhi, dlo = split(dec_ref[0])
-    err = err_scr[...]
-    grad = lax.dot_general(err, dhi, NT, preferred_element_type=f32)
-    grad += lax.dot_general(err, dlo, NT, preferred_element_type=f32)
+        total_scr[...] = jnp.zeros_like(total_scr)
+
+    back = lax.dot_general(err_scr[j], dec_ref[0].astype(bf16), NT, preferred_element_type=f32)
+    grad_ref[0] = acts_grad(acts_ref, err_scr[i * grad_depth // (slot_steps * depth)])
     ids = ids_ref[0] - n * depth
     block = ids >> 7
     lane = ids & 127
-    total = out_ref[...]
+    total = total_scr[...]
     for c in range(depth // LANES):
-        picked = jnp.take_along_axis(grad[:, c * LANES:(c + 1) * LANES], lane, axis=1)
+        picked = jnp.take_along_axis(back[:, c * LANES:(c + 1) * LANES], lane, axis=1)
         total = jnp.where(block == c, picked, total)
-    out_ref[...] = total
-
-    @pl.when(n == pl.num_programs(1) - 1)
+    total_scr[...] = total
+
+    @pl.when(n == slot_steps - 1)
     def _():
         half = total.shape[0] // 2
         keep_ref[0] = total[:half]
         send_ref[0] = total[half:]
 
 
-def back_call(ids, pieces, decoder, depth=512):
+def back_call(ids, acts, pieces, decoder, depth=BACK_DEPTH):
     slots, features, width = decoder.shape
     _, tokens, active = ids.shape
     depth = min(depth, features)
+    grad_depth = depth // 2
+    slot_steps = features // depth
+    slot_parts = features // grad_depth
+    count = len(pieces)
 
     def kernel(*refs):
-        back_kernel(len(pieces), *refs)
-
+        back_kernel(count, slot_steps, *refs)
+
+    half = pl.BlockSpec((1, tokens // 2, active), lambda i: (i // slot_steps, 0, 0))
     return pl.pallas_call(
         kernel,
-        out_shape=[jax.ShapeDtypeStruct((slots, tokens // 2, active), f32)] * 2,
-        grid=(slots, features // depth),
-        in_specs=[pl.BlockSpec((1, tokens, active), lambda j, n: (j, 0, 0))]
-        + [pl.BlockSpec((1, x.shape[1], width), lambda j, n: (j, 0, 0)) for x in pieces]
-        + [pl.BlockSpec((1, depth, width), lambda j, n: (j, n, 0))],
-        out_specs=[pl.BlockSpec((1, tokens // 2, active), lambda j, n: (j, 0, 0))] * 2,
-        scratch_shapes=[pltpu.VMEM((tokens, active), f32), pltpu.VMEM((tokens, width), bf16)],
+        out_shape=[jax.ShapeDtypeStruct((slots, tokens // 2, active), f32)] * 2
+        + [jax.ShapeDtypeStruct((slots, features, width), f32)],
+        grid=(slots * slot_steps,),
+        in_specs=[
+            pl.BlockSpec((1, tokens, active), lambda i: (i // slot_steps, 0, 0)),
+            pl.BlockSpec((1, tokens, grad_depth), lambda i: (i // slot_parts, 0, i % slot_parts)),
+            pl.BlockSpec((1, depth, width), lambda i: (i // slot_steps, i % slot_steps, 0)),
+        ]
+        + [pl.BlockSpec(x.shape, lambda i: (0, 0, 0)) for x in pieces],
+        out_specs=[half, half, pl.BlockSpec((1, grad_depth, width), lambda i: (i // slot_parts, i % slot_parts, 0))],
+        scratch_shapes=[pltpu.VMEM((tokens, active), f32), pltpu.VMEM((slots, tokens, width), bf16)],
         compiler_params=params(),
-        cost_estimate=cost(4 * slots * tokens * features * width, 4 * slots * features * width),
+        cost_estimate=cost(3 * slots * tokens * features * width, 6 * slots * features * width),
         name="back",
-    )(ids, *pieces, decoder)
+    )(ids, acts, decoder, *pieces)
 
 
 def grad_kernel(count, acts_ref, *refs):
-    pieces, (out_ref, err_scr) = refs[:count], refs[-2:]
-    tokens = err_scr.shape[0] // 2
+    pieces, (grad_ref, err_scr) = refs[:count], refs[-2:]
 
     @pl.when(pl.program_id(0) == 0)
     def _():
         gather_errors(pieces, err_scr)
-        err_scr[tokens:] = err_scr[:tokens]
-
-    out_ref[0] = lax.dot_general(acts_ref[0], err_scr[...], TN, preferred_element_type=f32)
-
-
-def grad_call(acts, pieces, slot, earlier, depth=512):
+
+    grad_ref[0] = acts_grad(acts_ref, err_scr[0])
+
+
+def grad_call(acts, pieces, quarter, earlier, depth=512):
     slots, rows, features = acts.shape
+    tokens = rows // 2
     width = pieces[0].shape[2]
-    depth = min(depth, features)
+    span = slots * features // 4
+    slot, first = quarter * span // features, quarter * span % features
+    depth = min(depth, span)
     count = len(pieces)
 
     def kernel(*refs):
         grad_kernel(count, *refs)
 
-    more = [] if earlier is None else [earlier]
     return pl.pallas_call(
         kernel,
         out_shape=jax.ShapeDtypeStruct((slots, features, width), f32),
-        grid=(features // depth,),
-        in_specs=[pl.BlockSpec((1, rows, depth), lambda n: (slot, 0, n))]
-        + [pl.BlockSpec((1, x.shape[1], width), lambda n: (slot, 0, 0)) for x in pieces]
-        + [pl.BlockSpec(memory_space=pl.ANY)] * len(more),
-        out_specs=pl.BlockSpec((1, depth, width), lambda n: (slot, n, 0)),
-        scratch_shapes=[pltpu.VMEM((rows, width), bf16)],
-        input_output_aliases={count + 1: 0} if more else {},
+        grid=(span // depth,),
+        in_specs=[pl.BlockSpec((1, tokens, depth), lambda i: (slot, 0, first // depth + i))]
+        + [pl.BlockSpec((1, x.shape[1], width), lambda i: (slot, 0, 0)) for x in pieces]
+        + [pl.BlockSpec(memory_space=pl.ANY)],
+        out_specs=pl.BlockSpec((1, depth, width), lambda i: (slot, first // depth + i, 0)),
+        scratch_shapes=[pltpu.VMEM((1, tokens, width), bf16)],
+        input_output_aliases={count + 1: 0},
         compiler_params=params(),
-        cost_estimate=cost(2 * rows * features * width, 4 * features * width),
+        cost_estimate=cost(2 * span * tokens * width, 4 * span * width),
         name="grad",
-    )(acts, *pieces, *more)
+    )(acts, *pieces, earlier)
 
 
 def layer_sums(tables, blocks, layers):
@@ -271,7 +288,7 @@
         out_specs=pl.BlockSpec(memory_space=pltpu.VMEM),
         compiler_params=params(),
         name="layer_sums",
-    )(jnp.stack(tables), *blocks)
+    )(tables, *blocks)
 
 
 def choose_layers(tables, errors, slots):
@@ -286,7 +303,7 @@
             ]
             out.append(jnp.stack(picked))
         return out
-    count = len(tables)
+    count = tables.shape[0]
     total = len(errors) * rows
 
     def kernel(table_ref, *refs):
@@ -305,7 +322,7 @@
         out_specs=[pl.BlockSpec(memory_space=pltpu.VMEM)] * count,
         compiler_params=params(),
         name="choose_layers",
-    )(jnp.stack(tables), *errors)
+    )(tables, *errors)
 
 
 def swap_cores(x):
@@ -328,12 +345,11 @@
     return x.astype(f32) * (1.0 / WIRE_SCALE)
 
 
-def weigh(tables, blocks, layers):
+def weigh(chosen, blocks):
     total = 0.0
-    for table, block in zip(tables, blocks):
+    for m, block in enumerate(blocks):
         for j in range(block.shape[0]):
-            chosen = (jnp.arange(layers, dtype=i32) == table[j]).astype(f32)
-            total = total + chosen[:, None, None] * block[j][None]
+            total = total + chosen[m, j][:, None, None] * block[j][None]
     return total
 
 
@@ -342,18 +358,20 @@
     run = keep.shape[1] // pairs
     rows = run // zs
     got = swap_cores(send)
+    pair_map, _ = lax.optimization_barrier((pair_map, keep))
+    maps = [pair_map] + [swap_pair(pair_map, m) for m in range(1, pairs)]
     halves = [keep[:, m * run:(m + 1) * run] + got[:, m * run:(m + 1) * run] for m in range(pairs)]
     packed = [pack(x) for x in halves[1:]]
     arrived = [None] + [swap_pair(packed[m - 1], m) for m in range(1, pairs)]
-    pair_map, _ = lax.optimization_barrier((pair_map, packed[0]))
-    maps = [pair_map] + [swap_pair(pair_map, m) for m in range(1, pairs)]
-    sources = [x[:, 0] for x in maps]
-    goals = [x[:, 1] for x in maps]
+    maps, _ = lax.optimization_barrier((jnp.stack(maps), packed))
+    sources, goals = maps[:, :, 0], maps[:, :, 1]
+    chosen = (goals[:, :, None] == jnp.arange(layers, dtype=i32)).astype(f32)
+    chosen, sources, goals = lax.optimization_barrier((chosen, sources, goals))
     parts = []
     for k in range(zs):
         cut = slice(k * rows, (k + 1) * rows)
         blocks = [halves[0][:, cut]] + [unpack(x[:, cut]) for x in arrived[1:]]
-        parts.append(weigh(goals, blocks, layers))
+        parts.append(weigh(chosen, blocks))
     sent = [pack(x) for x in parts[1:]]
     full = parts[0]
     for m in range(1, zs):
@@ -369,20 +387,17 @@
     return own + [swap_cores(x) for x in own]
 
 
-def finish(keep, send, sources, layers, acts, pieces):
+def finish(keep, send, sources, layers, acts, pieces, dec_grad):
     pairs, zs = lax.axis_size("pair"), lax.axis_size("feat") // 2
     slots, half_rows, width = keep.shape
     rows = half_rows // (pairs * zs)
     half = (keep + swap_cores(send)).reshape(slots, pairs, zs, rows, width)
     arrived = [half[:, :, 0]] + [swap_z(half[:, :, m], m) for m in range(1, zs)]
-    dec_grad = None
-    for j in range(0, slots - 1):
-        dec_grad = grad_call(acts, pieces, j, dec_grad)
-    if dec_grad is not None:
-        dec_grad, *arrived = lax.optimization_barrier((dec_grad, *arrived))
+    dec_grad = grad_call(acts, pieces, 2, dec_grad)
+    dec_grad, *arrived = lax.optimization_barrier((dec_grad, *arrived))
     column = sum(arrived)
     arrived = [column[:, 0]] + [swap_pair(column[:, m], m) for m in range(1, pairs)]
-    dec_grad = grad_call(acts, pieces, slots - 1, dec_grad)
+    dec_grad = grad_call(acts, pieces, 3, dec_grad)
     dec_grad, *arrived = lax.optimization_barrier((dec_grad, *arrived))
     return dec_grad, layer_sums(sources, arrived, layers)
 
@@ -396,8 +411,8 @@
     recon = full.astype(bf16)
     error = (full - target).astype(bf16)
     pieces = spread_errors(error, goals, slots)
-    keep, send = back_call(ids, pieces, decoder)
-    dec_grad, feat_grad = finish(keep, send, sources, layers, acts, pieces)
+    keep, send, dec_grad = back_call(ids, acts, pieces, decoder)
+    dec_grad, feat_grad = finish(keep, send, sources, layers, acts, pieces, dec_grad)
     return recon, dec_grad, feat_grad
 
 

time: 148 us -> 135 us (0.912)
  Pallas kernels: 70.7 us -> 62.5 us
  other arithmetic: 10.9 us -> 4.55 us
  waiting for transfers between devices: 27.3 us -> 32.4 us
  starting transfers between devices: 31.3 us -> 29.3 us
    ppermute x12, waiting for transfers between devices: 10.8 us -> 20.6 us  [swap_pair(): lax.ppermute(x, 'pair', [(i, i ^ m) for i in range(lax.axis_size('pair'))])]
    pallas_call x2, Pallas kernels: 19 us -> 11 us  [grad_call(): pl.pallas_call(kernel, out_shape=jax.ShapeDtypeStruct((slots, features, w...]
    convert_element_type x4 -> x1, other arithmetic: 5.18 us -> 0.07 us  [sum_full(): chosen = (goals[:, :, None] == jnp.arange(layers, dtype=i32)).astype(f32)]
    ppermute x6, waiting for transfers between devices: 6.19 us -> 2.12 us  [swap_cores(): lax.ppermute(x, 'feat', [(i, i ^ 1) for i in range(lax.axis_size('feat'))])]
    slice x8 -> x3, local copies, waits for them, and re-layouts: 3.04 us -> 0.27 us  [sum_full(): sources, goals = (maps[:, :, 0], maps[:, :, 1])]
    ppermute x9, starting transfers between devices: 15.1 us -> 13.4 us  [swap_z(): lax.ppermute(x, 'feat', [(i, i ^ 2 * m) for i in range(lax.axis_size('fea...]
  transfers between devices with their start and end apart: 27 -> 27, of which waited for: 11 -> 12; matrix products, arithmetic and copies ran while one was open for 7% -> 2% of each run, Pallas kernels for 13% -> 8%
where the time goes in v3:
time: 135 us
  Pallas kernels  62.5 us (46%)
  waiting for transfers between devices  32.4 us (24%)
  starting transfers between devices  29.3 us (22%)
  local copies, waits for them, and re-layouts  5.07 us (4%)
  other arithmetic  4.55 us (3%)
    pallas_call x1, Pallas kernels, recon_call(): pl.pallas_call(kernel, out_shape=(jax.ShapeDtypeStruct((slots, tokens //...  28.9 us
    ppermute x12, waiting for transfers between devices, swap_pair(): lax.ppermute(x, 'pair', [(i, i ^ m) for i in range(lax.axis_size('pair'))])  20.6 us
    pallas_call x1, Pallas kernels, back_call(): pl.pallas_call(kernel, out_shape=[jax.ShapeDtypeStruct((slots, tokens //...  19 us
    ppermute x12, starting transfers between devices, swap_pair(): lax.ppermute(x, 'pair', [(i, i ^ m) for i in range(lax.axis_size('pair'))])  14.8 us
    ppermute x9, starting transfers between devices, swap_z(): lax.ppermute(x, 'feat', [(i, i ^ 2 * m) for i in range(lax.axis_size('fea...  13.4 us
    pallas_call x2, Pallas kernels, grad_call(): pl.pallas_call(kernel, out_shape=jax.ShapeDtypeStruct((slots, features, w...  11 us
    ppermute x9, waiting for transfers between devices, swap_z(): lax.ppermute(x, 'feat', [(i, i ^ 2 * m) for i in range(lax.axis_size('fea...  9.66 us
  transfers between devices with their start and end apart: 27, of which 12 were waited for; matrix products, arithmetic and copies ran while one was open for 2% of the time, Pallas kernels for 8%

profile of v3, /device:TPU:0, one launch (start us, length us, event | category | flops | bytes accessed | tf_op | source)
XLA Modules:
  0.0 134.7 jit_solution(3539214305212578131)
XLA Ops:
  0.6 28.9 %recon.1 = (f32[2,128,2048]{2,1,0:T(8,128)}, f32[2,128,2048]{2,1,0:T(8,128)}, bf16[2,512,2048]{2,1,0:T(8,128)(2,1)}, s32[2,256,128]{2,1,0:T(8,128)}) custom-call(s32[2,2]{1,0:T(2,128)} %refs_0_.1, s32[3,256,128]{2,1,0:T(8,128)} %refs_1_.1, f32[3,256,128]{2,1,0:T(8,128)} %refs_2_.2, f32[2,2048,2048]{2,1,0:T(8,128)} %refs_2_.3), custom_call_target="tpu_custom_call" | custom-call | flops 12884901888 | bytes 33554432 | tf_op jit(solution)/shard_map/recon/pallas_call | solution.py:127
  30.0 2.7 %collective-permute-start = (s32[2,2]{1,0:T(2,128)S(1)}, s32[2,2]{1,0:T(2,128)S(1)}, u32[]{:S(2)}, u32[]{:S(2)}) collective-permute-start(s32[2,2]{1,0:T(2,128)S(1)} %copy-done.15), channel_id=1, source_target_pairs={{0,8},{8,0},{16,24},{24,16},{1,9},{9,1},{17,25},{25,17},{2,10},{10... | collective-permute-start | bytes 56 | tf_op jit(solution)/shard_map/ppermute | solution.py:337
  32.7 1.5 %collective-permute-start.1 = (s32[2,2]{1,0:T(2,128)S(1)}, s32[2,2]{1,0:T(2,128)S(1)}, u32[]{:S(2)}, u32[]{:S(2)}) collective-permute-start(s32[2,2]{1,0:T(2,128)S(1)} %copy-done.15), channel_id=1, source_target_pairs={{0,16},{8,24},{16,0},{24,8},{1,17},{9,25},{17,1},{25,9},{2,18},{10... | collective-permute-start | bytes 56 | tf_op jit(solution)/shard_map/ppermute | solution.py:337
  34.3 2.0 %collective-permute-done.1 = s32[2,2]{1,0:T(2,128)S(1)} collective-permute-done((s32[2,2]{1,0:T(2,128)S(1)}, s32[2,2]{1,0:T(2,128)S(1)}, u32[]{:S(2)}, u32[]{:S(2)}) %collective-permute-start.1) | collective-permute-done | bytes 48 | tf_op jit(solution)/shard_map/ppermute | solution.py:337
  36.3 2.4 %collective-permute-done.2 = s32[2,2]{1,0:T(2,128)S(1)} collective-permute-done((s32[2,2]{1,0:T(2,128)S(1)}, s32[2,2]{1,0:T(2,128)S(1)}, u32[]{:S(2)}, u32[]{:S(2)}) %collective-permute-start.2) | collective-permute-done | bytes 48 | tf_op jit(solution)/shard_map/ppermute | solution.py:337
  38.7 1.9 %slice_add_fusion = (f32[2,32,2048]{2,1,0:T(8,128)S(1)}, f16[2,32,2048]{2,1,0:T(8,128)(2,1)S(1)}, f16[2,32,2048]{2,1,0:T(8,128)(2,1)S(1)}, f16[2,32,2048]{2,1,0:T(8,128)(2,1)S(1)}) fusion(f32[2,128,2048]{2,1,0:T(8,128)S(1)} %collective-permute-done.3, f32[2,128,2048]{2,1,0:T(8,128)} %get-tuple-element.29), kind=kLoop, calls=%fused_computation | loop fusion | flops 1310720 | bytes 5505024 | tf_op jit(solution)/shard_map/add | solution.py:363
  41.2 1.5 %collective-permute-start.6 = (f16[2,32,2048]{2,1,0:T(8,128)(2,1)S(1)}, f16[2,32,2048]{2,1,0:T(8,128)(2,1)S(1)}, u32[]{:S(2)}, u32[]{:S(2)}) collective-permute-start(f16[2,32,2048]{2,1,0:T(8,128)(2,1)S(1)} %get-tuple-element.58), channel_id=1, source_target_pairs={{0,24},{8,16},{16,8},{24,0},{1,25},{9,17},{17,9},{25,1},{2,26},{10... | collective-permute-start | bytes 786440 | tf_op jit(solution)/shard_map/ppermute | solution.py:337
  44.6 8.6 %collective-permute-done.5 = f16[2,32,2048]{2,1,0:T(8,128)(2,1)S(1)} collective-permute-done((f16[2,32,2048]{2,1,0:T(8,128)(2,1)S(1)}, f16[2,32,2048]{2,1,0:T(8,128)(2,1)S(1)}, u32[]{:S(2)}, u32[]{:S(2)}) %collective-permute-start.5) | collective-permute-done | bytes 262176 | tf_op jit(solution)/shard_map/ppermute | solution.py:337
  54.8 1.6 %collective-permute-start.7 = (f16[3,8,2048]{2,1,0:T(8,128)(2,1)S(1)}, f16[3,8,2048]{2,1,0:T(8,128)(2,1)S(1)}, u32[]{:S(2)}, u32[]{:S(2)}) collective-permute-start(f16[3,8,2048]{2,1,0:T(8,128)(2,1)S(1)} %multiply_convert_fusion.2), channel_id=1, source_target_pairs={{0,2},{1,3},{2,0},{3,1},{4,6},{5,7},{6,4},{7,5},{8,10},{9,11},{10,... | collective-permute-start | bytes 294920 | tf_op jit(solution)/shard_map/ppermute | solution.py:333
  56.8 2.7 %collective-permute-start.8 = (f16[3,8,2048]{2,1,0:T(8,128)(2,1)S(1)}, f16[3,8,2048]{2,1,0:T(8,128)(2,1)S(1)}, u32[]{:S(2)}, u32[]{:S(2)}) collective-permute-start(f16[3,8,2048]{2,1,0:T(8,128)(2,1)S(1)} %multiply_convert_fusion.1), channel_id=1, source_target_pairs={{0,4},{1,5},{2,6},{3,7},{4,0},{5,1},{6,2},{7,3},{8,12},{9,13},{10,... | collective-permute-start | bytes 294920 | tf_op jit(solution)/shard_map/ppermute | solution.py:333
  60.0 4.4 %collective-permute-done.8 = f16[3,8,2048]{2,1,0:T(8,128)(2,1)S(1)} collective-permute-done((f16[3,8,2048]{2,1,0:T(8,128)(2,1)S(1)}, f16[3,8,2048]{2,1,0:T(8,128)(2,1)S(1)}, u32[]{:S(2)}, u32[]{:S(2)}) %collective-permute-start.8) | collective-permute-done | bytes 98336 | tf_op jit(solution)/shard_map/ppermute | solution.py:333
  64.4 1.8 %collective-permute-done.9 = f16[3,8,2048]{2,1,0:T(8,128)(2,1)S(1)} collective-permute-done((f16[3,8,2048]{2,1,0:T(8,128)(2,1)S(1)}, f16[3,8,2048]{2,1,0:T(8,128)(2,1)S(1)}, u32[]{:S(2)}, u32[]{:S(2)}) %collective-permute-start.9) | collective-permute-done | bytes 98336 | tf_op jit(solution)/shard_map/ppermute | solution.py:333
  69.0 2.5 %collective-permute-start.12 = (bf16[3,8,2048]{2,1,0:T(8,128)(2,1)S(1)}, bf16[3,8,2048]{2,1,0:T(8,128)(2,1)S(1)}, u32[]{:S(2)}, u32[]{:S(2)}) collective-permute-start(bf16[3,8,2048]{2,1,0:T(8,128)(2,1)S(1)} %get-tuple-element.55.refs_0_), channel_id=1, source_target_pairs={{0,6},{1,7},{2,4},{3,5},{4,2},{5,3},{6,0},{7,1},{8,14},{9,15},{10,... | collective-permute-start | bytes 294920 | tf_op jit(solution)/shard_map/ppermute | solution.py:333
  72.2 3.4 %collective-permute-done.11.refs_2_ = bf16[3,8,2048]{2,1,0:T(8,128)(2,1)S(1)} collective-permute-done((bf16[3,8,2048]{2,1,0:T(8,128)(2,1)S(1)}, bf16[3,8,2048]{2,1,0:T(8,128)(2,1)S(1)}, u32[]{:S(2)}, u32[]{:S(2)}) %collective-permute-start.11) | collective-permute-done | bytes 98336 | tf_op jit(solution)/shard_map/ppermute | solution.py:333
  76.9 2.1 %choose_layers.1 = (bf16[2,32,2048]{2,1,0:T(8,128)(2,1)}, bf16[2,32,2048]{2,1,0:T(8,128)(2,1)}, bf16[2,32,2048]{2,1,0:T(8,128)(2,1)}, bf16[2,32,2048]{2,1,0:T(8,128)(2,1)}) custom-call(s32[4,2]{1,0:T(4,128)} %copy.18.table_ref, bf16[3,8,2048]{2,1,0:T(8,128)(2,1)} %copy-done.7, bf16[3,8,2048]{2,1,0:T(8,128)(2,1)} %copy-done.9, ...), custom_call_target="tpu_custom_call" | custom-call | tf_op jit(solution)/shard_map/choose_layers/pallas_call | solution.py:318
  79.6 2.8 %collective-permute-start.15 = (bf16[2,32,2048]{2,1,0:T(8,128)(2,1)}, bf16[2,32,2048]{2,1,0:T(8,128)(2,1)S(1)}, u32[]{:S(2)}, u32[]{:S(2)}) collective-permute-start(bf16[2,32,2048]{2,1,0:T(8,128)(2,1)} %get-tuple-element.39), channel_id=1, source_target_pairs={{0,24},{8,16},{16,8},{24,0},{1,25},{9,17},{17,9},{25,1},{2,26},{10... | collective-permute-start | bytes 786440 | tf_op jit(solution)/shard_map/ppermute | solution.py:337
  82.4 3.1 %collective-permute-done.13.refs_4_.refs_2_ = bf16[2,32,2048]{2,1,0:T(8,128)(2,1)S(1)} collective-permute-done((bf16[2,32,2048]{2,1,0:T(8,128)(2,1)}, bf16[2,32,2048]{2,1,0:T(8,128)(2,1)S(1)}, u32[]{:S(2)}, u32[]{:S(2)}) %collective-permute-start.13) | collective-permute-done | bytes 262176 | tf_op jit(solution)/shard_map/ppermute | solution.py:337
  85.5 3.3 %collective-permute-done.14.refs_5_.refs_3_ = bf16[2,32,2048]{2,1,0:T(8,128)(2,1)S(1)} collective-permute-done((bf16[2,32,2048]{2,1,0:T(8,128)(2,1)}, bf16[2,32,2048]{2,1,0:T(8,128)(2,1)S(1)}, u32[]{:S(2)}, u32[]{:S(2)}) %collective-permute-start.14) | collective-permute-done | bytes 262176 | tf_op jit(solution)/shard_map/ppermute | solution.py:337
  91.4 19.0 %back.1 = (f32[2,128,128]{2,1,0:T(8,128)}, f32[2,128,128]{2,1,0:T(8,128)}, f32[2,2048,2048]{2,1,0:T(8,128)}) custom-call(s32[2,256,128]{2,1,0:T(8,128)} %get-tuple-element.40.refs_0_, bf16[2,512,2048]{2,1,0:T(8,128)(2,1)} %get-tuple-element.34.refs_1_.refs_0_, f32[2,2048,2048]{2,1,0:T(8,128)} %refs_2_.3, ...), custom_call_target="tpu_custom_call" | custom-call | flops 6442450944 | bytes 50331648 | tf_op jit(solution)/shard_map/back/pallas_call | solution.py:213
  115.5 1.9 %collective-permute-start.23 = (f32[2,4,8,128]{3,2,0,1:T(8,128)S(1)}, f32[2,4,8,128]{3,2,0,1:T(8,128)S(1)}, u32[]{:S(2)}, u32[]{:S(2)}) collective-permute-start(f32[2,4,8,128]{3,2,0,1:T(8,128)S(1)} %bitcast.111), channel_id=1, source_target_pairs={{0,6},{1,7},{2,4},{3,5},{4,2},{5,3},{6,0},{7,1},{8,14},{9,15},{10,... | collective-permute-start | bytes 98312 | tf_op jit(solution)/shard_map/ppermute | solution.py:333
  117.4 5.5 %grad.2.refs_9_ = f32[2,2048,2048]{2,1,0:T(8,128)} custom-call(bf16[2,512,2048]{2,1,0:T(8,128)(2,1)} %get-tuple-element.34.refs_1_.refs_0_, bf16[2,32,2048]{2,1,0:T(8,128)(2,1)} %get-tuple-element.36.refs_3_.refs_1_, bf16[2,32,2048]{2,1,0:T(8,128)(2,1)} %copy-done, bf16[2,32,2048]{2,1,0:T(8,128)(2,1)} %copy-done.1, ...), custom_call_target="tpu_custom_call", output_to_operand_aliasing={{}: (9, {})} | custom-call | flops 1073741824 | bytes 8388608 | tf_op jit(solution)/shard_map/grad/pallas_call | solution.py:254
  123.6 1.5 %collective-permute-start.24 = (f32[2,8,128]{2,1,0:T(8,128)S(1)}, f32[2,8,128]{2,1,0:T(8,128)S(1)}, u32[]{:S(2)}, u32[]{:S(2)}) collective-permute-start(f32[2,8,128]{2,1,0:T(8,128)S(1)} %get-tuple-element.111), channel_id=1, source_target_pairs={{0,8},{8,0},{16,24},{24,16},{1,9},{9,1},{17,25},{25,17},{2,10},{10... | collective-permute-start | bytes 24584 | tf_op jit(solution)/shard_map/ppermute | solution.py:337
  127.1 5.5 %grad.3 = f32[2,2048,2048]{2,1,0:T(8,128)} custom-call(bf16[2,512,2048]{2,1,0:T(8,128)(2,1)} %get-tuple-element.34.refs_1_.refs_0_, bf16[2,32,2048]{2,1,0:T(8,128)(2,1)} %get-tuple-element.36.refs_3_.refs_1_, bf16[2,32,2048]{2,1,0:T(8,128)(2,1)} %copy-done, bf16[2,32,2048]{2,1,0:T(8,128)(2,1)} %copy-done.1, ...), custom_call_target="tpu_custom_call", output_to_operand_aliasing={{}: (9, {})} | custom-call | flops 1073741824 | bytes 8388608 | tf_op jit(solution)/shard_map/grad/pallas_call | solution.py:254
  133.2 1.5 %layer_sums.1 = f32[3,8,128]{2,1,0:T(8,128)} custom-call(s32[4,2]{1,0:T(4,128)} %copy.23.table_ref, f32[2,8,128]{2,1,0:T(8,128)} %get-tuple-element.51.refs_0_, f32[2,8,128]{2,1,0:T(8,128)} %copy-done.12, f32[2,8,128]{2,1,0:T(8,128)} %copy-done.13, f32[2,8,128]{2,1,0:T(8,128)} %copy-done.14), custom_call_target="tpu_custom_call" | custom-call | tf_op jit(solution)/shard_map/layer_sums/pallas_call | solution.py:284
  (101 shorter events, 21.6 us)
Async XLA Ops:
  29.6 9.1 %collective-permute-start.3 = (f32[2,128,2048]{2,1,0:T(8,128)}, f32[2,128,2048]{2,1,0:T(8,128)S(1)}, u32[]{:S(2)}, u32[]{:S(2)}) collective-permute-start(f32[2,128,2048]{2,1,0:T(8,128)} %get-tuple-element.31), channel_id=1, source_target_pairs={{0,1},{1,0},{2,3},{3,2},{4,5},{5,4},{6,7},{7,6},{8,9},{9,8},{10,11... | collective-permute-start | bytes 6291464 | tf_op jit(solution)/shard_map/ppermute | solution.py:329
  30.0 4.2 %collective-permute-start = (s32[2,2]{1,0:T(2,128)S(1)}, s32[2,2]{1,0:T(2,128)S(1)}, u32[]{:S(2)}, u32[]{:S(2)}) collective-permute-start(s32[2,2]{1,0:T(2,128)S(1)} %copy-done.15), channel_id=1, source_target_pairs={{0,8},{8,0},{16,24},{24,16},{1,9},{9,1},{17,25},{25,17},{2,10},{10... | collective-permute-start | bytes 56 | tf_op jit(solution)/shard_map/ppermute | solution.py:337
  32.7 3.6 %collective-permute-start.1 = (s32[2,2]{1,0:T(2,128)S(1)}, s32[2,2]{1,0:T(2,128)S(1)}, u32[]{:S(2)}, u32[]{:S(2)}) collective-permute-start(s32[2,2]{1,0:T(2,128)S(1)} %copy-done.15), channel_id=1, source_target_pairs={{0,16},{8,24},{16,0},{24,8},{1,17},{9,25},{17,1},{25,9},{2,18},{10... | collective-permute-start | bytes 56 | tf_op jit(solution)/shard_map/ppermute | solution.py:337
  34.2 4.5 %collective-permute-start.2 = (s32[2,2]{1,0:T(2,128)S(1)}, s32[2,2]{1,0:T(2,128)S(1)}, u32[]{:S(2)}, u32[]{:S(2)}) collective-permute-start(s32[2,2]{1,0:T(2,128)S(1)} %copy-done.15), channel_id=1, source_target_pairs={{0,24},{8,16},{16,8},{24,0},{1,25},{9,17},{17,9},{25,1},{2,26},{10... | collective-permute-start | bytes 56 | tf_op jit(solution)/shard_map/ppermute | solution.py:337
  40.6 12.6 %collective-permute-start.5 = (f16[2,32,2048]{2,1,0:T(8,128)(2,1)S(1)}, f16[2,32,2048]{2,1,0:T(8,128)(2,1)S(1)}, u32[]{:S(2)}, u32[]{:S(2)}) collective-permute-start(f16[2,32,2048]{2,1,0:T(8,128)(2,1)S(1)} %get-tuple-element.59), channel_id=1, source_target_pairs={{0,16},{8,24},{16,0},{24,8},{1,17},{9,25},{17,1},{25,9},{2,18},{10... | collective-permute-start | bytes 786440 | tf_op jit(solution)/shard_map/ppermute | solution.py:337
  41.2 13.4 %collective-permute-start.6 = (f16[2,32,2048]{2,1,0:T(8,128)(2,1)S(1)}, f16[2,32,2048]{2,1,0:T(8,128)(2,1)S(1)}, u32[]{:S(2)}, u32[]{:S(2)}) collective-permute-start(f16[2,32,2048]{2,1,0:T(8,128)(2,1)S(1)} %get-tuple-element.58), channel_id=1, source_target_pairs={{0,24},{8,16},{16,8},{24,0},{1,25},{9,17},{17,9},{25,1},{2,26},{10... | collective-permute-start | bytes 786440 | tf_op jit(solution)/shard_map/ppermute | solution.py:337
  42.7 11.8 %collective-permute-start.4 = (f16[2,32,2048]{2,1,0:T(8,128)(2,1)S(1)}, f16[2,32,2048]{2,1,0:T(8,128)(2,1)S(1)}, u32[]{:S(2)}, u32[]{:S(2)}) collective-permute-start(f16[2,32,2048]{2,1,0:T(8,128)(2,1)S(1)} %get-tuple-element.60), channel_id=1, source_target_pairs={{0,8},{8,0},{16,24},{24,16},{1,9},{9,1},{17,25},{25,17},{2,10},{10... | collective-permute-start | bytes 786440 | tf_op jit(solution)/shard_map/ppermute | solution.py:337
  54.8 5.1 %collective-permute-start.7 = (f16[3,8,2048]{2,1,0:T(8,128)(2,1)S(1)}, f16[3,8,2048]{2,1,0:T(8,128)(2,1)S(1)}, u32[]{:S(2)}, u32[]{:S(2)}) collective-permute-start(f16[3,8,2048]{2,1,0:T(8,128)(2,1)S(1)} %multiply_convert_fusion.2), channel_id=1, source_target_pairs={{0,2},{1,3},{2,0},{3,1},{4,6},{5,7},{6,4},{7,5},{8,10},{9,11},{10,... | collective-permute-start | bytes 294920 | tf_op jit(solution)/shard_map/ppermute | solution.py:333
  56.8 7.6 %collective-permute-start.8 = (f16[3,8,2048]{2,1,0:T(8,128)(2,1)S(1)}, f16[3,8,2048]{2,1,0:T(8,128)(2,1)S(1)}, u32[]{:S(2)}, u32[]{:S(2)}) collective-permute-start(f16[3,8,2048]{2,1,0:T(8,128)(2,1)S(1)} %multiply_convert_fusion.1), channel_id=1, source_target_pairs={{0,4},{1,5},{2,6},{3,7},{4,0},{5,1},{6,2},{7,3},{8,12},{9,13},{10,... | collective-permute-start | bytes 294920 | tf_op jit(solution)/shard_map/ppermute | solution.py:333
  59.6 6.6 %collective-permute-start.9 = (f16[3,8,2048]{2,1,0:T(8,128)(2,1)S(1)}, f16[3,8,2048]{2,1,0:T(8,128)(2,1)S(1)}, u32[]{:S(2)}, u32[]{:S(2)}) collective-permute-start(f16[3,8,2048]{2,1,0:T(8,128)(2,1)S(1)} %multiply_convert_fusion), channel_id=1, source_target_pairs={{0,6},{1,7},{2,4},{3,5},{4,2},{5,3},{6,0},{7,1},{8,14},{9,15},{10,... | collective-permute-start | bytes 294920 | tf_op jit(solution)/shard_map/ppermute | solution.py:333
  67.1 5.1 %collective-permute-start.10 = (bf16[3,8,2048]{2,1,0:T(8,128)(2,1)S(1)}, bf16[3,8,2048]{2,1,0:T(8,128)(2,1)S(1)}, u32[]{:S(2)}, u32[]{:S(2)}) collective-permute-start(bf16[3,8,2048]{2,1,0:T(8,128)(2,1)S(1)} %get-tuple-element.55.refs_0_), channel_id=1, source_target_pairs={{0,2},{1,3},{2,0},{3,1},{4,6},{5,7},{6,4},{7,5},{8,10},{9,11},{10,... | collective-permute-start | bytes 294920 | tf_op jit(solution)/shard_map/ppermute | solution.py:333
  68.0 7.6 %collective-permute-start.11 = (bf16[3,8,2048]{2,1,0:T(8,128)(2,1)S(1)}, bf16[3,8,2048]{2,1,0:T(8,128)(2,1)S(1)}, u32[]{:S(2)}, u32[]{:S(2)}) collective-permute-start(bf16[3,8,2048]{2,1,0:T(8,128)(2,1)S(1)} %get-tuple-element.55.refs_0_), channel_id=1, source_target_pairs={{0,4},{1,5},{2,6},{3,7},{4,0},{5,1},{6,2},{7,3},{8,12},{9,13},{10,... | collective-permute-start | bytes 294920 | tf_op jit(solution)/shard_map/ppermute | solution.py:333
  69.0 6.6 %collective-permute-start.12 = (bf16[3,8,2048]{2,1,0:T(8,128)(2,1)S(1)}, bf16[3,8,2048]{2,1,0:T(8,128)(2,1)S(1)}, u32[]{:S(2)}, u32[]{:S(2)}) collective-permute-start(bf16[3,8,2048]{2,1,0:T(8,128)(2,1)S(1)} %get-tuple-element.55.refs_0_), channel_id=1, source_target_pairs={{0,6},{1,7},{2,4},{3,5},{4,2},{5,3},{6,0},{7,1},{8,14},{9,15},{10,... | collective-permute-start | bytes 294920 | tf_op jit(solution)/shard_map/ppermute | solution.py:333
  78.9 6.6 %collective-permute-start.13 = (bf16[2,32,2048]{2,1,0:T(8,128)(2,1)}, bf16[2,32,2048]{2,1,0:T(8,128)(2,1)S(1)}, u32[]{:S(2)}, u32[]{:S(2)}) collective-permute-start(bf16[2,32,2048]{2,1,0:T(8,128)(2,1)} %get-tuple-element.37), channel_id=1, source_target_pairs={{0,8},{8,0},{16,24},{24,16},{1,9},{9,1},{17,25},{25,17},{2,10},{10... | collective-permute-start | bytes 786440 | tf_op jit(solution)/shard_map/ppermute | solution.py:337
  79.4 9.4 %collective-permute-start.14 = (bf16[2,32,2048]{2,1,0:T(8,128)(2,1)}, bf16[2,32,2048]{2,1,0:T(8,128)(2,1)S(1)}, u32[]{:S(2)}, u32[]{:S(2)}) collective-permute-start(bf16[2,32,2048]{2,1,0:T(8,128)(2,1)} %get-tuple-element.38), channel_id=1, source_target_pairs={{0,16},{8,24},{16,0},{24,8},{1,17},{9,25},{17,1},{25,9},{2,18},{10... | collective-permute-start | bytes 786440 | tf_op jit(solution)/shard_map/ppermute | solution.py:337
  79.6 9.2 %collective-permute-start.15 = (bf16[2,32,2048]{2,1,0:T(8,128)(2,1)}, bf16[2,32,2048]{2,1,0:T(8,128)(2,1)S(1)}, u32[]{:S(2)}, u32[]{:S(2)}) collective-permute-start(bf16[2,32,2048]{2,1,0:T(8,128)(2,1)} %get-tuple-element.39), channel_id=1, source_target_pairs={{0,24},{8,16},{16,8},{24,0},{1,25},{9,17},{17,9},{25,1},{2,26},{10... | collective-permute-start | bytes 786440 | tf_op jit(solution)/shard_map/ppermute | solution.py:337
  82.4 6.9 %collective-permute-start.16 = (bf16[2,32,2048]{2,1,0:T(8,128)(2,1)}, bf16[2,32,2048]{2,1,0:T(8,128)(2,1)S(1)}, u32[]{:S(2)}, u32[]{:S(2)}) collective-permute-start(bf16[2,32,2048]{2,1,0:T(8,128)(2,1)} %get-tuple-element.36.refs_3_.refs_1_), channel_id=1, source_target_pairs={{0,1},{1,0},{2,3},{3,2},{4,5},{5,4},{6,7},{7,6},{8,9},{9,8},{10,11... | collective-permute-start | bytes 786440 | tf_op jit(solution)/shard_map/ppermute | solution.py:329
  85.5 3.8 %collective-permute-start.17 = (bf16[2,32,2048]{2,1,0:T(8,128)(2,1)S(1)}, bf16[2,32,2048]{2,1,0:T(8,128)(2,1)S(1)}, u32[]{:S(2)}, u32[]{:S(2)}) collective-permute-start(bf16[2,32,2048]{2,1,0:T(8,128)(2,1)S(1)} %collective-permute-done.13.refs_4_.refs_2_), channel_id=1, source_target_pairs={{0,1},{1,0},{2,3},{3,2},{4,5},{5,4},{6,7},{7,6},{8,9},{9,8},{10,11... | collective-permute-start | bytes 786440 | tf_op jit(solution)/shard_map/ppermute | solution.py:329
  113.0 10.0 %collective-permute-start.21 = (f32[2,4,8,128]{3,2,0,1:T(8,128)S(1)}, f32[2,4,8,128]{3,2,0,1:T(8,128)S(1)}, u32[]{:S(2)}, u32[]{:S(2)}) collective-permute-start(f32[2,4,8,128]{3,2,0,1:T(8,128)S(1)} %bitcast.109), channel_id=1, source_target_pairs={{0,2},{1,3},{2,0},{3,1},{4,6},{5,7},{6,4},{7,5},{8,10},{9,11},{10,... | collective-permute-start | bytes 98312 | tf_op jit(solution)/shard_map/ppermute | solution.py:333
  114.0 8.9 %collective-permute-start.22 = (f32[2,4,8,128]{3,2,0,1:T(8,128)S(1)}, f32[2,4,8,128]{3,2,0,1:T(8,128)S(1)}, u32[]{:S(2)}, u32[]{:S(2)}) collective-permute-start(f32[2,4,8,128]{3,2,0,1:T(8,128)S(1)} %bitcast.110), channel_id=1, source_target_pairs={{0,4},{1,5},{2,6},{3,7},{4,0},{5,1},{6,2},{7,3},{8,12},{9,13},{10,... | collective-permute-start | bytes 98312 | tf_op jit(solution)/shard_map/ppermute | solution.py:333
  115.5 7.5 %collective-permute-start.23 = (f32[2,4,8,128]{3,2,0,1:T(8,128)S(1)}, f32[2,4,8,128]{3,2,0,1:T(8,128)S(1)}, u32[]{:S(2)}, u32[]{:S(2)}) collective-permute-start(f32[2,4,8,128]{3,2,0,1:T(8,128)S(1)} %bitcast.111), channel_id=1, source_target_pairs={{0,6},{1,7},{2,4},{3,5},{4,2},{5,3},{6,0},{7,1},{8,14},{9,15},{10,... | collective-permute-start | bytes 98312 | tf_op jit(solution)/shard_map/ppermute | solution.py:333
  123.6 9.0 %collective-permute-start.24 = (f32[2,8,128]{2,1,0:T(8,128)S(1)}, f32[2,8,128]{2,1,0:T(8,128)S(1)}, u32[]{:S(2)}, u32[]{:S(2)}) collective-permute-start(f32[2,8,128]{2,1,0:T(8,128)S(1)} %get-tuple-element.111), channel_id=1, source_target_pairs={{0,8},{8,0},{16,24},{24,16},{1,9},{9,1},{17,25},{25,17},{2,10},{10... | collective-permute-start | bytes 24584 | tf_op jit(solution)/shard_map/ppermute | solution.py:337
  125.1 7.5 %collective-permute-start.25 = (f32[2,8,128]{2,1,0:T(8,128)S(1)}, f32[2,8,128]{2,1,0:T(8,128)S(1)}, u32[]{:S(2)}, u32[]{:S(2)}) collective-permute-start(f32[2,8,128]{2,1,0:T(8,128)S(1)} %get-tuple-element.110), channel_id=1, source_target_pairs={{0,16},{8,24},{16,0},{24,8},{1,17},{9,25},{17,1},{25,9},{2,18},{10... | collective-permute-start | bytes 24584 | tf_op jit(solution)/shard_map/ppermute | solution.py:337
  125.6 7.0 %collective-permute-start.26 = (f32[2,8,128]{2,1,0:T(8,128)S(1)}, f32[2,8,128]{2,1,0:T(8,128)S(1)}, u32[]{:S(2)}, u32[]{:S(2)}) collective-permute-start(f32[2,8,128]{2,1,0:T(8,128)S(1)} %get-tuple-element.109), channel_id=1, source_target_pairs={{0,24},{8,16},{16,8},{24,0},{1,25},{9,17},{17,9},{25,1},{2,26},{10... | collective-permute-start | bytes 24584 | tf_op jit(solution)/shard_map/ppermute | solution.py:337
  (19 other events, 84.4 us)

commit v4 on v3

--- a/solution.py
+++ b/solution.py
@@ -10,8 +10,8 @@
 i32 = jnp.int32
 LANES = 128
 WIRE_SCALE = 128.0
-VMEM_LIMIT = 56 << 20
 BACK_DEPTH = 1024
+RECON_TILE = 512
 NT = (((1,), (1,)), ((), ()))
 TN = (((0,), (0,)), ((), ()))
 
@@ -25,11 +25,12 @@
     return pl.CostEstimate(flops=int(flops), bytes_accessed=int(nbytes), transcendentals=0)
 
 
-def params():
-    return pltpu.CompilerParams(vmem_limit_bytes=VMEM_LIMIT)
-
-
-def lay_out(features, idx_ref, val_ref, ids_ref, val_scr, pairs, zs):
+def params(mib):
+    return pltpu.CompilerParams(vmem_limit_bytes=mib << 20)
+
+
+def prepare(slot, layer, refs, pairs, zs, features):
+    idx_ref, val_ref, ids_ref, val_scr, hi_scr, lo_scr, vhi_scr, vlo_scr = refs
     tokens = idx_ref.shape[1]
     rows = tokens // (pairs * zs * 2)
     p, feat = lax.axis_index("pair"), lax.axis_index("feat")
@@ -40,26 +41,27 @@
         pr = (at // zs) & (pairs - 1)
         cr = at // (zs * pairs)
         block = (p ^ pr) * (zs * 2) + (feat ^ (zr * 2 + cr))
-        ids_ref[0, pl.ds(at * rows, rows), :] = idx_ref[0, pl.ds(block * rows, rows), :] - first
-        val_scr[pl.ds(at * rows, rows), :] = val_ref[0, pl.ds(block * rows, rows), :]
+        ids_ref[slot, pl.ds(at * rows, rows), :] = idx_ref[layer, pl.ds(block * rows, rows), :] - first
+        val_scr[pl.ds(at * rows, rows), :] = val_ref[layer, pl.ds(block * rows, rows), :]
         return 0
 
     lax.fori_loop(0, tokens // rows, run, 0)
-
-
-def build_acts(ids_ref, val_scr, acts_ref, rows_scr, hi_scr, lo_scr, vhi_scr, vlo_scr, span):
-    _, tokens, active = ids_ref.shape
-    blocks = acts_ref.shape[-1] // LANES
-    pitch = 2 * blocks + 1
-    iota_block = lax.broadcasted_iota(i32, (blocks, active), 0)
-    iota_lane = lax.broadcasted_iota(i32, (LANES, active), 0)
-    ids = ids_ref[0]
+    ids = ids_ref[slot]
     vhi, vlo = split(val_scr[...])
     hi_scr[...] = ids >> 7
     lo_scr[...] = ids & 127
     vhi_scr[...] = vhi.astype(f32)
     vlo_scr[...] = vlo.astype(f32)
+
+
+def build_span(part, span, high_ref, low_ref, rows_scr, hi_scr, lo_scr, vhi_scr, vlo_scr):
+    active = hi_scr.shape[1]
+    blocks = high_ref.shape[-1] // LANES
+    pitch = 2 * blocks + 1
+    iota_block = lax.broadcasted_iota(i32, (blocks, active), 0)
+    iota_lane = lax.broadcasted_iota(i32, (LANES, active), 0)
     empty = jnp.zeros((2 * blocks, active), bf16)
+    base = pl.multiple_of(part * span, span)
 
     def factors(at):
         def row(ref, count):
@@ -72,81 +74,111 @@
         onehot = jnp.where(row(lo_scr, LANES) == iota_lane, 1.0, 0.0).astype(bf16)
         return weights, onehot
 
-    def part(b, _):
-        base = pl.multiple_of(b * span, span)
-        for i in range(0, span, 2):
-            w0, o0 = factors(base + i)
-            w1, o1 = factors(base + i + 1)
-            weights = jnp.concatenate(
-                [jnp.concatenate([w0, empty], axis=1), jnp.concatenate([empty, w1], axis=1)], axis=0
-            )
-            onehot = jnp.concatenate([o0, o1], axis=1)
-            got = lax.dot_general(weights, onehot, NT, preferred_element_type=f32)
-            rows_scr[i * pitch:i * pitch + 2 * blocks, :] = got[:2 * blocks]
-            rows_scr[(i + 1) * pitch:(i + 1) * pitch + 2 * blocks, :] = got[2 * blocks:]
-        for h in range(blocks):
-            lanes = slice(h * LANES, (h + 1) * LANES)
-            high = rows_scr[pl.ds(h, span, stride=pitch), :]
-            low = rows_scr[pl.ds(blocks + h, span, stride=pitch), :]
-            acts_ref[0, pl.ds(base, span), lanes] = high.astype(bf16)
-            acts_ref[0, pl.ds(tokens + base, span), lanes] = low.astype(bf16)
-        return 0
-
-    lax.fori_loop(0, tokens // span, part, 0)
-
-
-def recon_kernel(pairs, zs, span, map_ref, idx_ref, val_ref, dec_ref, keep_ref, send_ref, acts_ref, ids_ref, val_scr, *scr):
-    @pl.when(pl.program_id(1) == 0)
+    for i in range(0, span, 2):
+        w0, o0 = factors(base + i)
+        w1, o1 = factors(base + i + 1)
+        weights = jnp.concatenate(
+            [jnp.concatenate([w0, empty], axis=1), jnp.concatenate([empty, w1], axis=1)], axis=0
+        )
+        onehot = jnp.concatenate([o0, o1], axis=1)
+        got = lax.dot_general(weights, onehot, NT, preferred_element_type=f32)
+        rows_scr[i * pitch:i * pitch + 2 * blocks, :] = got[:2 * blocks]
+        rows_scr[(i + 1) * pitch:(i + 1) * pitch + 2 * blocks, :] = got[2 * blocks:]
+    for h in range(blocks):
+        lanes = slice(h * LANES, (h + 1) * LANES)
+        high = rows_scr[pl.ds(h, span, stride=pitch), :]
+        low = rows_scr[pl.ds(blocks + h, span, stride=pitch), :]
+        high_ref[pl.ds(base, span), lanes] = high.astype(bf16)
+        low_ref[pl.ds(base, span), lanes] = low.astype(bf16)
+
+
+def recon_kernel(slots, layers, pairs, zs, span, map_ref, idx_ref, val_ref, dec_ref, keep_ref, send_ref, acts_ref, ids_ref, *scr):
+    lows, (rows_scr, val_scr, *split_scr) = scr[:slots], scr[slots:]
+    _, tokens, features = acts_ref.shape
+    j, n = pl.program_id(0), pl.program_id(1)
+    steps = tokens // span
+    share = -(-steps // pl.num_programs(1))
+
+    def start(slot):
+        layer = jnp.minimum(map_ref[slot, 0], layers - 1)
+        prepare(slot, layer, (idx_ref, val_ref, ids_ref, val_scr, *split_scr), pairs, zs, features)
+
+    def build(slot, part):
+        build_span(part, span, acts_ref.at[slot], lows[slot], rows_scr, *split_scr)
+
+    def multiply(slot):
+        dhi, dlo = split(dec_ref[0])
+        prod = jnp.dot(acts_ref[slot], dhi, preferred_element_type=f32)
+        prod += jnp.dot(lows[slot][...], dhi, preferred_element_type=f32)
+        prod += jnp.dot(acts_ref[slot], dlo, preferred_element_type=f32)
+        keep_ref[0] = prod[:tokens // 2]
+        send_ref[0] = prod[tokens // 2:]
+
+    @pl.when((j == 0) & (n == 0))
     def _():
-        lay_out(acts_ref.shape[-1], idx_ref, val_ref, ids_ref, val_scr, pairs, zs)
-        build_acts(ids_ref, val_scr, acts_ref, *scr, span)
-
-    tokens = idx_ref.shape[1]
-    dhi, dlo = split(dec_ref[0])
-    both = jnp.dot(acts_ref[0], dhi, preferred_element_type=f32)
-    low = jnp.dot(acts_ref[0, :tokens], dlo, preferred_element_type=f32)
-    prod = both[:tokens] + both[tokens:] + low
-    keep_ref[0] = prod[:tokens // 2]
-    send_ref[0] = prod[tokens // 2:]
-
-
-def recon_call(pair_map, indices, values, decoder, pairs, zs, tile=1024, span=64):
+        start(0)
+
+        def part(b, _):
+            build(0, b)
+            return 0
+
+        lax.fori_loop(0, steps, part, 0)
+
+    for slot in range(slots):
+        if slot + 1 < slots:
+            @pl.when((j == slot) & (n == 0))
+            def _():
+                start(slot + 1)
+
+        @pl.when(j == slot)
+        def _():
+            if slot + 1 < slots:
+                for q in range(share):
+                    build(slot + 1, jnp.minimum(n * share + q, steps - 1))
+            multiply(slot)
+
+
+def recon_call(pair_map, indices, values, decoder, pairs, zs, tile=RECON_TILE, span=64):
     slots, features, width = decoder.shape
     layers, tokens, active = indices.shape
     tile = min(tile, width)
     blocks = features // LANES
-    layer = pl.BlockSpec((1, tokens, active), lambda j, n, m: (jnp.minimum(m[j, 0], layers - 1), 0, 0))
     half = pl.BlockSpec((1, tokens // 2, tile), lambda j, n, m: (j, 0, n))
 
     def kernel(*refs):
-        recon_kernel(pairs, zs, span, *refs)
-
-    def slot(rows, cols):
-        return pl.BlockSpec((1, rows, cols), lambda j, n, m: (j, 0, 0))
+        recon_kernel(slots, layers, pairs, zs, span, *refs)
+
+    def whole(*shape):
+        return pl.BlockSpec(shape, lambda j, n, m: (0, 0, 0))
 
     return pl.pallas_call(
         kernel,
         out_shape=(
             jax.ShapeDtypeStruct((slots, tokens // 2, width), f32),
             jax.ShapeDtypeStruct((slots, tokens // 2, width), f32),
-            jax.ShapeDtypeStruct((slots, 2 * tokens, features), bf16),
+            jax.ShapeDtypeStruct((slots, tokens, features), bf16),
             jax.ShapeDtypeStruct((slots, tokens, active), i32),
         ),
         grid_spec=pltpu.PrefetchScalarGridSpec(
             num_scalar_prefetch=1,
             grid=(slots, width // tile),
-            in_specs=[layer, layer, pl.BlockSpec((1, features, tile), lambda j, n, m: (j, 0, n))],
-            out_specs=[half, half, slot(2 * tokens, features), slot(tokens, active)],
-            scratch_shapes=[
+            in_specs=[
+                whole(layers, tokens, active),
+                whole(layers, tokens, active),
+                pl.BlockSpec((1, features, tile), lambda j, n, m: (j, 0, n)),
+            ],
+            out_specs=[half, half, whole(slots, tokens, features), whole(slots, tokens, active)],
+            scratch_shapes=[pltpu.VMEM((tokens, features), bf16)] * slots
+            + [
+                pltpu.VMEM((span * (2 * blocks + 1) + 8, LANES), f32),
                 pltpu.VMEM((tokens, active), f32),
-                pltpu.VMEM((span * (2 * blocks + 1) + 8, LANES), f32),
                 pltpu.VMEM((tokens, active), i32),
                 pltpu.VMEM((tokens, active), i32),
                 pltpu.VMEM((tokens, active), f32),
                 pltpu.VMEM((tokens, active), f32),
             ],
         ),
-        compiler_params=params(),
+        compiler_params=params(30),
         cost_estimate=cost(6 * slots * tokens * features * width, 4 * slots * features * width),
         name="recon",
     )(pair_map, indices, values, decoder)
@@ -223,7 +255,7 @@
         + [pl.BlockSpec(x.shape, lambda i: (0, 0, 0)) for x in pieces],
         out_specs=[half, half, pl.BlockSpec((1, grad_depth, width), lambda i: (i // slot_parts, i % slot_parts, 0))],
         scratch_shapes=[pltpu.VMEM((tokens, active), f32), pltpu.VMEM((slots, tokens, width), bf16)],
-        compiler_params=params(),
+        compiler_params=params(46),
         cost_estimate=cost(3 * slots * tokens * features * width, 6 * slots * features * width),
         name="back",
     )(ids, acts, decoder, *pieces)
@@ -240,8 +272,7 @@
 
 
 def grad_call(acts, pieces, quarter, earlier, depth=512):
-    slots, rows, features = acts.shape
-    tokens = rows // 2
+    slots, tokens, features = acts.shape
     width = pieces[0].shape[2]
     span = slots * features // 4
     slot, first = quarter * span // features, quarter * span % features
@@ -261,7 +292,7 @@
         out_specs=pl.BlockSpec((1, depth, width), lambda i: (slot, first // depth + i, 0)),
         scratch_shapes=[pltpu.VMEM((1, tokens, width), bf16)],
         input_output_aliases={count + 1: 0},
-        compiler_params=params(),
+        compiler_params=params(56),
         cost_estimate=cost(2 * span * tokens * width, 4 * span * width),
         name="grad",
     )(acts, *pieces, earlier)
@@ -286,7 +317,7 @@
         out_shape=jax.ShapeDtypeStruct((layers,) + shape, f32),
         in_specs=[pl.BlockSpec(memory_space=pltpu.SMEM)] + [pl.BlockSpec(memory_space=pltpu.VMEM)] * len(blocks),
         out_specs=pl.BlockSpec(memory_space=pltpu.VMEM),
-        compiler_params=params(),
+        compiler_params=params(8),
         name="layer_sums",
     )(tables, *blocks)
 
@@ -320,7 +351,7 @@
         out_shape=[jax.ShapeDtypeStruct((slots, total, width), bf16)] * count,
         in_specs=[pl.BlockSpec(memory_space=pltpu.SMEM)] + [pl.BlockSpec(memory_space=pltpu.VMEM)] * len(errors),
         out_specs=[pl.BlockSpec(memory_space=pltpu.VMEM)] * count,
-        compiler_params=params(),
+        compiler_params=params(12),
         name="choose_layers",
     )(tables, *errors)
 

time: 135 us -> 129 us (0.956)
  Pallas kernels: 62.5 us -> 57 us
  other arithmetic: 4.55 us -> 2.87 us
    pallas_call x1, Pallas kernels: 28.9 us -> 26 us  [recon_call(): pl.pallas_call(kernel, out_shape=(jax.ShapeDtypeStruct((slots, tokens //...]
    unnamed x36 -> x46, local copies, waits for them, and re-layouts: 2.59 us -> 3.79 us
  transfers between devices with their start and end apart: 27 -> 27, of which waited for: 12 -> 14; matrix products, arithmetic and copies ran while one was open for 2% -> 2% of each run, Pallas kernels for 8% -> 9%
where the time goes in v4:
time: 129 us; the launch traced here: 128 us
  Pallas kernels  57 us (44%)
  waiting for transfers between devices  32.9 us (26%)
  starting transfers between devices  29.4 us (23%)
  local copies, waits for them, and re-layouts  5.21 us (4%)
  other arithmetic  2.87 us (2%)
    pallas_call x1, Pallas kernels, recon_call(): pl.pallas_call(kernel, out_shape=(jax.ShapeDtypeStruct((slots, tokens //...  26 us
    ppermute x12, waiting for transfers between devices, swap_pair(): lax.ppermute(x, 'pair', [(i, i ^ m) for i in range(lax.axis_size('pair'))])  20 us
    pallas_call x1, Pallas kernels, back_call(): pl.pallas_call(kernel, out_shape=[jax.ShapeDtypeStruct((slots, tokens //...  18.1 us
    ppermute x12, starting transfers between devices, swap_pair(): lax.ppermute(x, 'pair', [(i, i ^ m) for i in range(lax.axis_size('pair'))])  14.7 us
    ppermute x9, starting transfers between devices, swap_z(): lax.ppermute(x, 'feat', [(i, i ^ 2 * m) for i in range(lax.axis_size('fea...  13.4 us
    pallas_call x2, Pallas kernels, grad_call(): pl.pallas_call(kernel, out_shape=jax.ShapeDtypeStruct((slots, features, w...  11 us
    ppermute x9, waiting for transfers between devices, swap_z(): lax.ppermute(x, 'feat', [(i, i ^ 2 * m) for i in range(lax.axis_size('fea...  10.3 us
    unnamed x46, local copies, waits for them, and re-layouts  3.79 us
  transfers between devices with their start and end apart: 27, of which 14 were waited for; matrix products, arithmetic and copies ran while one was open for 2% of the time, Pallas kernels for 9%

profile of v4, /device:TPU:0, one launch (start us, length us, event | category | flops | bytes accessed | tf_op | source)
XLA Modules:
  0.0 128.4 jit_solution(1097377290625273818)
XLA Ops:
  3.3 26.0 %recon.1 = (f32[2,128,2048]{2,1,0:T(8,128)S(1)}, f32[2,128,2048]{2,1,0:T(8,128)S(1)}, bf16[2,256,2048]{2,1,0:T(8,128)(2,1)S(1)}, s32[2,256,128]{2,1,0:T(8,128)S(1)}) custom-call(s32[2,2]{1,0:T(2,128)S(1)} %copy-done.11, s32[3,256,128]{2,1,0:T(8,128)S(1)} %copy-done.12, f32[3,256,128]{2,1,0:T(8,128)S(1)} %copy-done.13, f32[2,2048,2048]{2,1,0:T(8,128)} %refs_2_.3), custom_call_target="tpu_custom_call" | custom-call | flops 12884901888 | bytes 33554432 | tf_op jit(solution)/shard_map/recon/pallas_call | solution.py:154
  29.8 2.6 %collective-permute-start = (s32[2,2]{1,0:T(2,128)S(1)}, s32[2,2]{1,0:T(2,128)S(1)}, u32[]{:S(2)}, u32[]{:S(2)}) collective-permute-start(s32[2,2]{1,0:T(2,128)S(1)} %copy-done.11), channel_id=1, source_target_pairs={{0,8},{8,0},{16,24},{24,16},{1,9},{9,1},{17,25},{25,17},{2,10},{10... | collective-permute-start | bytes 56 | tf_op jit(solution)/shard_map/ppermute | solution.py:368
  32.4 1.5 %collective-permute-start.1 = (s32[2,2]{1,0:T(2,128)S(1)}, s32[2,2]{1,0:T(2,128)S(1)}, u32[]{:S(2)}, u32[]{:S(2)}) collective-permute-start(s32[2,2]{1,0:T(2,128)S(1)} %copy-done.11), channel_id=1, source_target_pairs={{0,16},{8,24},{16,0},{24,8},{1,17},{9,25},{17,1},{25,9},{2,18},{10... | collective-permute-start | bytes 56 | tf_op jit(solution)/shard_map/ppermute | solution.py:368
  33.9 2.0 %collective-permute-done.1 = s32[2,2]{1,0:T(2,128)S(1)} collective-permute-done((s32[2,2]{1,0:T(2,128)S(1)}, s32[2,2]{1,0:T(2,128)S(1)}, u32[]{:S(2)}, u32[]{:S(2)}) %collective-permute-start.1) | collective-permute-done | bytes 48 | tf_op jit(solution)/shard_map/ppermute | solution.py:368
  36.0 2.4 %collective-permute-done.2 = s32[2,2]{1,0:T(2,128)S(1)} collective-permute-done((s32[2,2]{1,0:T(2,128)S(1)}, s32[2,2]{1,0:T(2,128)S(1)}, u32[]{:S(2)}, u32[]{:S(2)}) %collective-permute-start.2) | collective-permute-done | bytes 48 | tf_op jit(solution)/shard_map/ppermute | solution.py:368
  40.0 1.5 %collective-permute-start.6 = (f16[2,32,2048]{2,1,0:T(8,128)(2,1)}, f16[2,32,2048]{2,1,0:T(8,128)(2,1)S(1)}, u32[]{:S(2)}, u32[]{:S(2)}) collective-permute-start(f16[2,32,2048]{2,1,0:T(8,128)(2,1)} %get-tuple-element.58), channel_id=1, source_target_pairs={{0,24},{8,16},{16,8},{24,0},{1,25},{9,17},{17,9},{25,1},{2,26},{10... | collective-permute-start | bytes 786440 | tf_op jit(solution)/shard_map/ppermute | solution.py:368
  41.5 1.5 %collective-permute-start.4 = (f16[2,32,2048]{2,1,0:T(8,128)(2,1)}, f16[2,32,2048]{2,1,0:T(8,128)(2,1)S(1)}, u32[]{:S(2)}, u32[]{:S(2)}) collective-permute-start(f16[2,32,2048]{2,1,0:T(8,128)(2,1)} %get-tuple-element.60), channel_id=1, source_target_pairs={{0,8},{8,0},{16,24},{24,16},{1,9},{9,1},{17,25},{25,17},{2,10},{10... | collective-permute-start | bytes 786440 | tf_op jit(solution)/shard_map/ppermute | solution.py:368
  44.2 8.1 %collective-permute-done.5 = f16[2,32,2048]{2,1,0:T(8,128)(2,1)S(1)} collective-permute-done((f16[2,32,2048]{2,1,0:T(8,128)(2,1)}, f16[2,32,2048]{2,1,0:T(8,128)(2,1)S(1)}, u32[]{:S(2)}, u32[]{:S(2)}) %collective-permute-start.5) | collective-permute-done | bytes 262176 | tf_op jit(solution)/shard_map/ppermute | solution.py:368
  54.0 1.6 %collective-permute-start.7 = (f16[3,8,2048]{2,1,0:T(8,128)(2,1)S(1)}, f16[3,8,2048]{2,1,0:T(8,128)(2,1)S(1)}, u32[]{:S(2)}, u32[]{:S(2)}) collective-permute-start(f16[3,8,2048]{2,1,0:T(8,128)(2,1)S(1)} %multiply_convert_fusion.2), channel_id=1, source_target_pairs={{0,2},{1,3},{2,0},{3,1},{4,6},{5,7},{6,4},{7,5},{8,10},{9,11},{10,... | collective-permute-start | bytes 294920 | tf_op jit(solution)/shard_map/ppermute | solution.py:364
  55.9 2.7 %collective-permute-start.8 = (f16[3,8,2048]{2,1,0:T(8,128)(2,1)S(1)}, f16[3,8,2048]{2,1,0:T(8,128)(2,1)S(1)}, u32[]{:S(2)}, u32[]{:S(2)}) collective-permute-start(f16[3,8,2048]{2,1,0:T(8,128)(2,1)S(1)} %multiply_convert_fusion.1), channel_id=1, source_target_pairs={{0,4},{1,5},{2,6},{3,7},{4,0},{5,1},{6,2},{7,3},{8,12},{9,13},{10,... | collective-permute-start | bytes 294920 | tf_op jit(solution)/shard_map/ppermute | solution.py:364
  59.1 4.4 %collective-permute-done.8 = f16[3,8,2048]{2,1,0:T(8,128)(2,1)S(1)} collective-permute-done((f16[3,8,2048]{2,1,0:T(8,128)(2,1)S(1)}, f16[3,8,2048]{2,1,0:T(8,128)(2,1)S(1)}, u32[]{:S(2)}, u32[]{:S(2)}) %collective-permute-start.8) | collective-permute-done | bytes 98336 | tf_op jit(solution)/shard_map/ppermute | solution.py:364
  63.5 1.8 %collective-permute-done.9 = f16[3,8,2048]{2,1,0:T(8,128)(2,1)S(1)} collective-permute-done((f16[3,8,2048]{2,1,0:T(8,128)(2,1)S(1)}, f16[3,8,2048]{2,1,0:T(8,128)(2,1)S(1)}, u32[]{:S(2)}, u32[]{:S(2)}) %collective-permute-start.9) | collective-permute-done | bytes 98336 | tf_op jit(solution)/shard_map/ppermute | solution.py:364
  68.3 2.4 %collective-permute-start.12 = (bf16[3,8,2048]{2,1,0:T(8,128)(2,1)S(1)}, bf16[3,8,2048]{2,1,0:T(8,128)(2,1)S(1)}, u32[]{:S(2)}, u32[]{:S(2)}) collective-permute-start(bf16[3,8,2048]{2,1,0:T(8,128)(2,1)S(1)} %get-tuple-element.55.refs_0_), channel_id=1, source_target_pairs={{0,6},{1,7},{2,4},{3,5},{4,2},{5,3},{6,0},{7,1},{8,14},{9,15},{10,... | collective-permute-start | bytes 294920 | tf_op jit(solution)/shard_map/ppermute | solution.py:364
  71.2 2.5 %collective-permute-done.11.refs_2_ = bf16[3,8,2048]{2,1,0:T(8,128)(2,1)S(1)} collective-permute-done((bf16[3,8,2048]{2,1,0:T(8,128)(2,1)S(1)}, bf16[3,8,2048]{2,1,0:T(8,128)(2,1)S(1)}, u32[]{:S(2)}, u32[]{:S(2)}) %collective-permute-start.11) | collective-permute-done | bytes 98336 | tf_op jit(solution)/shard_map/ppermute | solution.py:364
  76.5 2.5 %collective-permute-start.15 = (bf16[2,32,2048]{2,1,0:T(8,128)(2,1)S(1)}, bf16[2,32,2048]{2,1,0:T(8,128)(2,1)S(1)}, u32[]{:S(2)}, u32[]{:S(2)}) collective-permute-start(bf16[2,32,2048]{2,1,0:T(8,128)(2,1)S(1)} %get-tuple-element.39), channel_id=1, source_target_pairs={{0,24},{8,16},{16,8},{24,0},{1,25},{9,17},{17,9},{25,1},{2,26},{10... | collective-permute-start | bytes 786440 | tf_op jit(solution)/shard_map/ppermute | solution.py:368
  79.1 2.9 %collective-permute-done.13.refs_4_.refs_2_ = bf16[2,32,2048]{2,1,0:T(8,128)(2,1)S(1)} collective-permute-done((bf16[2,32,2048]{2,1,0:T(8,128)(2,1)S(1)}, bf16[2,32,2048]{2,1,0:T(8,128)(2,1)S(1)}, u32[]{:S(2)}, u32[]{:S(2)}) %collective-permute-start.13) | collective-permute-done | bytes 262176 | tf_op jit(solution)/shard_map/ppermute | solution.py:368
  82.0 3.3 %collective-permute-done.14.refs_5_.refs_3_ = bf16[2,32,2048]{2,1,0:T(8,128)(2,1)S(1)} collective-permute-done((bf16[2,32,2048]{2,1,0:T(8,128)(2,1)S(1)}, bf16[2,32,2048]{2,1,0:T(8,128)(2,1)S(1)}, u32[]{:S(2)}, u32[]{:S(2)}) %collective-permute-start.14) | collective-permute-done | bytes 262176 | tf_op jit(solution)/shard_map/ppermute | solution.py:368
  88.3 18.1 %back.1 = (f32[2,128,128]{2,1,0:T(8,128)S(1)}, f32[2,128,128]{2,1,0:T(8,128)}, f32[2,2048,2048]{2,1,0:T(8,128)}) custom-call(s32[2,256,128]{2,1,0:T(8,128)S(1)} %copy-done.10, bf16[2,256,2048]{2,1,0:T(8,128)(2,1)S(1)} %get-tuple-element.34.refs_1_.refs_0_, f32[2,2048,2048]{2,1,0:T(8,128)} %refs_2_.3, ...), custom_call_target="tpu_custom_call" | custom-call | flops 6442450944 | bytes 50331648 | tf_op jit(solution)/shard_map/back/pallas_call | solution.py:245
  108.1 1.6 %collective-permute-start.21 = (f32[2,4,8,128]{3,2,0,1:T(8,128)S(1)}, f32[2,4,8,128]{3,2,0,1:T(8,128)S(1)}, u32[]{:S(2)}, u32[]{:S(2)}) collective-permute-start(f32[2,4,8,128]{3,2,0,1:T(8,128)S(1)} %bitcast.110), channel_id=1, source_target_pairs={{0,2},{1,3},{2,0},{3,1},{4,6},{5,7},{6,4},{7,5},{8,10},{9,11},{10,... | collective-permute-start | bytes 98312 | tf_op jit(solution)/shard_map/ppermute | solution.py:364
  111.1 1.4 %collective-permute-start.23 = (f32[2,4,8,128]{3,2,0,1:T(8,128)S(1)}, f32[2,4,8,128]{3,2,0,1:T(8,128)S(1)}, u32[]{:S(2)}, u32[]{:S(2)}) collective-permute-start(f32[2,4,8,128]{3,2,0,1:T(8,128)S(1)} %bitcast.112), channel_id=1, source_target_pairs={{0,6},{1,7},{2,4},{3,5},{4,2},{5,3},{6,0},{7,1},{8,14},{9,15},{10,... | collective-permute-start | bytes 98312 | tf_op jit(solution)/shard_map/ppermute | solution.py:364
  112.5 5.5 %grad.2.refs_9_ = f32[2,2048,2048]{2,1,0:T(8,128)} custom-call(bf16[2,256,2048]{2,1,0:T(8,128)(2,1)} %copy-done, bf16[2,32,2048]{2,1,0:T(8,128)(2,1)} %copy-done.1, bf16[2,32,2048]{2,1,0:T(8,128)(2,1)} %copy-done.2, bf16[2,32,2048]{2,1,0:T(8,128)(2,1)} %copy-done.3, bf16[2,32,2048]{2,1,0:T(8,128)(2,1)} %copy-done.4, ...), custom_call_target="tpu_custom_call", output_to_operand_aliasing={{}: (9, {})} | custom-call | flops 1073741824 | bytes 8388608 | tf_op jit(solution)/shard_map/grad/pallas_call | solution.py:285
  118.1 1.6 %collective-permute-start.24 = (f32[2,8,128]{2,1,0:T(8,128)S(1)}, f32[2,8,128]{2,1,0:T(8,128)S(1)}, u32[]{:S(2)}, u32[]{:S(2)}) collective-permute-start(f32[2,8,128]{2,1,0:T(8,128)S(1)} %get-tuple-element.111), channel_id=1, source_target_pairs={{0,8},{8,0},{16,24},{24,16},{1,9},{9,1},{17,25},{25,17},{2,10},{10... | collective-permute-start | bytes 24584 | tf_op jit(solution)/shard_map/ppermute | solution.py:368
  120.1 1.6 %collective-permute-start.26 = (f32[2,8,128]{2,1,0:T(8,128)S(1)}, f32[2,8,128]{2,1,0:T(8,128)S(1)}, u32[]{:S(2)}, u32[]{:S(2)}) collective-permute-start(f32[2,8,128]{2,1,0:T(8,128)S(1)} %get-tuple-element.109), channel_id=1, source_target_pairs={{0,24},{8,16},{16,8},{24,0},{1,25},{9,17},{17,9},{25,1},{2,26},{10... | collective-permute-start | bytes 24584 | tf_op jit(solution)/shard_map/ppermute | solution.py:368
  121.7 5.5 %grad.3 = f32[2,2048,2048]{2,1,0:T(8,128)} custom-call(bf16[2,256,2048]{2,1,0:T(8,128)(2,1)} %copy-done, bf16[2,32,2048]{2,1,0:T(8,128)(2,1)} %copy-done.1, bf16[2,32,2048]{2,1,0:T(8,128)(2,1)} %copy-done.2, bf16[2,32,2048]{2,1,0:T(8,128)(2,1)} %copy-done.3, bf16[2,32,2048]{2,1,0:T(8,128)(2,1)} %copy-done.4, ...), custom_call_target="tpu_custom_call", output_to_operand_aliasing={{}: (9, {})} | custom-call | flops 1073741824 | bytes 8388608 | tf_op jit(solution)/shard_map/grad/pallas_call | solution.py:285
  (111 shorter events, 22.4 us)
Async XLA Ops:
  29.3 9.1 %collective-permute-start.3 = (f32[2,128,2048]{2,1,0:T(8,128)S(1)}, f32[2,128,2048]{2,1,0:T(8,128)S(1)}, u32[]{:S(2)}, u32[]{:S(2)}) collective-permute-start(f32[2,128,2048]{2,1,0:T(8,128)S(1)} %get-tuple-element.31), channel_id=1, source_target_pairs={{0,1},{1,0},{2,3},{3,2},{4,5},{5,4},{6,7},{7,6},{8,9},{9,8},{10,11... | collective-permute-start | bytes 6291464 | tf_op jit(solution)/shard_map/ppermute | solution.py:360
  29.8 4.1 %collective-permute-start = (s32[2,2]{1,0:T(2,128)S(1)}, s32[2,2]{1,0:T(2,128)S(1)}, u32[]{:S(2)}, u32[]{:S(2)}) collective-permute-start(s32[2,2]{1,0:T(2,128)S(1)} %copy-done.11), channel_id=1, source_target_pairs={{0,8},{8,0},{16,24},{24,16},{1,9},{9,1},{17,25},{25,17},{2,10},{10... | collective-permute-start | bytes 56 | tf_op jit(solution)/shard_map/ppermute | solution.py:368
  32.4 3.6 %collective-permute-start.1 = (s32[2,2]{1,0:T(2,128)S(1)}, s32[2,2]{1,0:T(2,128)S(1)}, u32[]{:S(2)}, u32[]{:S(2)}) collective-permute-start(s32[2,2]{1,0:T(2,128)S(1)} %copy-done.11), channel_id=1, source_target_pairs={{0,16},{8,24},{16,0},{24,8},{1,17},{9,25},{17,1},{25,9},{2,18},{10... | collective-permute-start | bytes 56 | tf_op jit(solution)/shard_map/ppermute | solution.py:368
  33.9 4.5 %collective-permute-start.2 = (s32[2,2]{1,0:T(2,128)S(1)}, s32[2,2]{1,0:T(2,128)S(1)}, u32[]{:S(2)}, u32[]{:S(2)}) collective-permute-start(s32[2,2]{1,0:T(2,128)S(1)} %copy-done.11), channel_id=1, source_target_pairs={{0,24},{8,16},{16,8},{24,0},{1,25},{9,17},{17,9},{25,1},{2,26},{10... | collective-permute-start | bytes 56 | tf_op jit(solution)/shard_map/ppermute | solution.py:368
  39.5 12.8 %collective-permute-start.5 = (f16[2,32,2048]{2,1,0:T(8,128)(2,1)}, f16[2,32,2048]{2,1,0:T(8,128)(2,1)S(1)}, u32[]{:S(2)}, u32[]{:S(2)}) collective-permute-start(f16[2,32,2048]{2,1,0:T(8,128)(2,1)} %get-tuple-element.59), channel_id=1, source_target_pairs={{0,16},{8,24},{16,0},{24,8},{1,17},{9,25},{17,1},{25,9},{2,18},{10... | collective-permute-start | bytes 786440 | tf_op jit(solution)/shard_map/ppermute | solution.py:368
  40.0 13.6 %collective-permute-start.6 = (f16[2,32,2048]{2,1,0:T(8,128)(2,1)}, f16[2,32,2048]{2,1,0:T(8,128)(2,1)S(1)}, u32[]{:S(2)}, u32[]{:S(2)}) collective-permute-start(f16[2,32,2048]{2,1,0:T(8,128)(2,1)} %get-tuple-element.58), channel_id=1, source_target_pairs={{0,24},{8,16},{16,8},{24,0},{1,25},{9,17},{17,9},{25,1},{2,26},{10... | collective-permute-start | bytes 786440 | tf_op jit(solution)/shard_map/ppermute | solution.py:368
  41.5 12.0 %collective-permute-start.4 = (f16[2,32,2048]{2,1,0:T(8,128)(2,1)}, f16[2,32,2048]{2,1,0:T(8,128)(2,1)S(1)}, u32[]{:S(2)}, u32[]{:S(2)}) collective-permute-start(f16[2,32,2048]{2,1,0:T(8,128)(2,1)} %get-tuple-element.60), channel_id=1, source_target_pairs={{0,8},{8,0},{16,24},{24,16},{1,9},{9,1},{17,25},{25,17},{2,10},{10... | collective-permute-start | bytes 786440 | tf_op jit(solution)/shard_map/ppermute | solution.py:368
  54.0 5.1 %collective-permute-start.7 = (f16[3,8,2048]{2,1,0:T(8,128)(2,1)S(1)}, f16[3,8,2048]{2,1,0:T(8,128)(2,1)S(1)}, u32[]{:S(2)}, u32[]{:S(2)}) collective-permute-start(f16[3,8,2048]{2,1,0:T(8,128)(2,1)S(1)} %multiply_convert_fusion.2), channel_id=1, source_target_pairs={{0,2},{1,3},{2,0},{3,1},{4,6},{5,7},{6,4},{7,5},{8,10},{9,11},{10,... | collective-permute-start | bytes 294920 | tf_op jit(solution)/shard_map/ppermute | solution.py:364
  55.9 7.6 %collective-permute-start.8 = (f16[3,8,2048]{2,1,0:T(8,128)(2,1)S(1)}, f16[3,8,2048]{2,1,0:T(8,128)(2,1)S(1)}, u32[]{:S(2)}, u32[]{:S(2)}) collective-permute-start(f16[3,8,2048]{2,1,0:T(8,128)(2,1)S(1)} %multiply_convert_fusion.1), channel_id=1, source_target_pairs={{0,4},{1,5},{2,6},{3,7},{4,0},{5,1},{6,2},{7,3},{8,12},{9,13},{10,... | collective-permute-start | bytes 294920 | tf_op jit(solution)/shard_map/ppermute | solution.py:364
  58.8 6.6 %collective-permute-start.9 = (f16[3,8,2048]{2,1,0:T(8,128)(2,1)S(1)}, f16[3,8,2048]{2,1,0:T(8,128)(2,1)S(1)}, u32[]{:S(2)}, u32[]{:S(2)}) collective-permute-start(f16[3,8,2048]{2,1,0:T(8,128)(2,1)S(1)} %multiply_convert_fusion), channel_id=1, source_target_pairs={{0,6},{1,7},{2,4},{3,5},{4,2},{5,3},{6,0},{7,1},{8,14},{9,15},{10,... | collective-permute-start | bytes 294920 | tf_op jit(solution)/shard_map/ppermute | solution.py:364
  66.3 4.9 %collective-permute-start.10 = (bf16[3,8,2048]{2,1,0:T(8,128)(2,1)S(1)}, bf16[3,8,2048]{2,1,0:T(8,128)(2,1)S(1)}, u32[]{:S(2)}, u32[]{:S(2)}) collective-permute-start(bf16[3,8,2048]{2,1,0:T(8,128)(2,1)S(1)} %get-tuple-element.55.refs_0_), channel_id=1, source_target_pairs={{0,2},{1,3},{2,0},{3,1},{4,6},{5,7},{6,4},{7,5},{8,10},{9,11},{10,... | collective-permute-start | bytes 294920 | tf_op jit(solution)/shard_map/ppermute | solution.py:364
  67.1 6.6 %collective-permute-start.11 = (bf16[3,8,2048]{2,1,0:T(8,128)(2,1)S(1)}, bf16[3,8,2048]{2,1,0:T(8,128)(2,1)S(1)}, u32[]{:S(2)}, u32[]{:S(2)}) collective-permute-start(bf16[3,8,2048]{2,1,0:T(8,128)(2,1)S(1)} %get-tuple-element.55.refs_0_), channel_id=1, source_target_pairs={{0,4},{1,5},{2,6},{3,7},{4,0},{5,1},{6,2},{7,3},{8,12},{9,13},{10,... | collective-permute-start | bytes 294920 | tf_op jit(solution)/shard_map/ppermute | solution.py:364
  68.3 6.5 %collective-permute-start.12 = (bf16[3,8,2048]{2,1,0:T(8,128)(2,1)S(1)}, bf16[3,8,2048]{2,1,0:T(8,128)(2,1)S(1)}, u32[]{:S(2)}, u32[]{:S(2)}) collective-permute-start(bf16[3,8,2048]{2,1,0:T(8,128)(2,1)S(1)} %get-tuple-element.55.refs_0_), channel_id=1, source_target_pairs={{0,6},{1,7},{2,4},{3,5},{4,2},{5,3},{6,0},{7,1},{8,14},{9,15},{10,... | collective-permute-start | bytes 294920 | tf_op jit(solution)/shard_map/ppermute | solution.py:364
  75.5 6.4 %collective-permute-start.13 = (bf16[2,32,2048]{2,1,0:T(8,128)(2,1)S(1)}, bf16[2,32,2048]{2,1,0:T(8,128)(2,1)S(1)}, u32[]{:S(2)}, u32[]{:S(2)}) collective-permute-start(bf16[2,32,2048]{2,1,0:T(8,128)(2,1)S(1)} %get-tuple-element.37), channel_id=1, source_target_pairs={{0,8},{8,0},{16,24},{24,16},{1,9},{9,1},{17,25},{25,17},{2,10},{10... | collective-permute-start | bytes 786440 | tf_op jit(solution)/shard_map/ppermute | solution.py:368
  76.1 9.2 %collective-permute-start.14 = (bf16[2,32,2048]{2,1,0:T(8,128)(2,1)S(1)}, bf16[2,32,2048]{2,1,0:T(8,128)(2,1)S(1)}, u32[]{:S(2)}, u32[]{:S(2)}) collective-permute-start(bf16[2,32,2048]{2,1,0:T(8,128)(2,1)S(1)} %get-tuple-element.38), channel_id=1, source_target_pairs={{0,16},{8,24},{16,0},{24,8},{1,17},{9,25},{17,1},{25,9},{2,18},{10... | collective-permute-start | bytes 786440 | tf_op jit(solution)/shard_map/ppermute | solution.py:368
  76.5 8.8 %collective-permute-start.15 = (bf16[2,32,2048]{2,1,0:T(8,128)(2,1)S(1)}, bf16[2,32,2048]{2,1,0:T(8,128)(2,1)S(1)}, u32[]{:S(2)}, u32[]{:S(2)}) collective-permute-start(bf16[2,32,2048]{2,1,0:T(8,128)(2,1)S(1)} %get-tuple-element.39), channel_id=1, source_target_pairs={{0,24},{8,16},{16,8},{24,0},{1,25},{9,17},{17,9},{25,1},{2,26},{10... | collective-permute-start | bytes 786440 | tf_op jit(solution)/shard_map/ppermute | solution.py:368
  79.1 6.7 %collective-permute-start.16 = (bf16[2,32,2048]{2,1,0:T(8,128)(2,1)S(1)}, bf16[2,32,2048]{2,1,0:T(8,128)(2,1)S(1)}, u32[]{:S(2)}, u32[]{:S(2)}) collective-permute-start(bf16[2,32,2048]{2,1,0:T(8,128)(2,1)S(1)} %get-tuple-element.36.refs_3_.refs_1_), channel_id=1, source_target_pairs={{0,1},{1,0},{2,3},{3,2},{4,5},{5,4},{6,7},{7,6},{8,9},{9,8},{10,11... | collective-permute-start | bytes 786440 | tf_op jit(solution)/shard_map/ppermute | solution.py:360
  82.0 3.9 %collective-permute-start.17 = (bf16[2,32,2048]{2,1,0:T(8,128)(2,1)S(1)}, bf16[2,32,2048]{2,1,0:T(8,128)(2,1)S(1)}, u32[]{:S(2)}, u32[]{:S(2)}) collective-permute-start(bf16[2,32,2048]{2,1,0:T(8,128)(2,1)S(1)} %collective-permute-done.13.refs_4_.refs_2_), channel_id=1, source_target_pairs={{0,1},{1,0},{2,3},{3,2},{4,5},{5,4},{6,7},{7,6},{8,9},{9,8},{10,11... | collective-permute-start | bytes 786440 | tf_op jit(solution)/shard_map/ppermute | solution.py:360
  108.1 10.0 %collective-permute-start.21 = (f32[2,4,8,128]{3,2,0,1:T(8,128)S(1)}, f32[2,4,8,128]{3,2,0,1:T(8,128)S(1)}, u32[]{:S(2)}, u32[]{:S(2)}) collective-permute-start(f32[2,4,8,128]{3,2,0,1:T(8,128)S(1)} %bitcast.110), channel_id=1, source_target_pairs={{0,2},{1,3},{2,0},{3,1},{4,6},{5,7},{6,4},{7,5},{8,10},{9,11},{10,... | collective-permute-start | bytes 98312 | tf_op jit(solution)/shard_map/ppermute | solution.py:364
  109.7 8.3 %collective-permute-start.22 = (f32[2,4,8,128]{3,2,0,1:T(8,128)S(1)}, f32[2,4,8,128]{3,2,0,1:T(8,128)S(1)}, u32[]{:S(2)}, u32[]{:S(2)}) collective-permute-start(f32[2,4,8,128]{3,2,0,1:T(8,128)S(1)} %bitcast.111), channel_id=1, source_target_pairs={{0,4},{1,5},{2,6},{3,7},{4,0},{5,1},{6,2},{7,3},{8,12},{9,13},{10,... | collective-permute-start | bytes 98312 | tf_op jit(solution)/shard_map/ppermute | solution.py:364
  111.1 7.0 %collective-permute-start.23 = (f32[2,4,8,128]{3,2,0,1:T(8,128)S(1)}, f32[2,4,8,128]{3,2,0,1:T(8,128)S(1)}, u32[]{:S(2)}, u32[]{:S(2)}) collective-permute-start(f32[2,4,8,128]{3,2,0,1:T(8,128)S(1)} %bitcast.112), channel_id=1, source_target_pairs={{0,6},{1,7},{2,4},{3,5},{4,2},{5,3},{6,0},{7,1},{8,14},{9,15},{10,... | collective-permute-start | bytes 98312 | tf_op jit(solution)/shard_map/ppermute | solution.py:364
  118.1 9.1 %collective-permute-start.24 = (f32[2,8,128]{2,1,0:T(8,128)S(1)}, f32[2,8,128]{2,1,0:T(8,128)S(1)}, u32[]{:S(2)}, u32[]{:S(2)}) collective-permute-start(f32[2,8,128]{2,1,0:T(8,128)S(1)} %get-tuple-element.111), channel_id=1, source_target_pairs={{0,8},{8,0},{16,24},{24,16},{1,9},{9,1},{17,25},{25,17},{2,10},{10... | collective-permute-start | bytes 24584 | tf_op jit(solution)/shard_map/ppermute | solution.py:368
  119.7 7.5 %collective-permute-start.25 = (f32[2,8,128]{2,1,0:T(8,128)S(1)}, f32[2,8,128]{2,1,0:T(8,128)S(1)}, u32[]{:S(2)}, u32[]{:S(2)}) collective-permute-start(f32[2,8,128]{2,1,0:T(8,128)S(1)} %get-tuple-element.110), channel_id=1, source_target_pairs={{0,16},{8,24},{16,0},{24,8},{1,17},{9,25},{17,1},{25,9},{2,18},{10... | collective-permute-start | bytes 24584 | tf_op jit(solution)/shard_map/ppermute | solution.py:368
  120.1 7.1 %collective-permute-start.26 = (f32[2,8,128]{2,1,0:T(8,128)S(1)}, f32[2,8,128]{2,1,0:T(8,128)S(1)}, u32[]{:S(2)}, u32[]{:S(2)}) collective-permute-start(f32[2,8,128]{2,1,0:T(8,128)S(1)} %get-tuple-element.109), channel_id=1, source_target_pairs={{0,24},{8,16},{16,8},{24,0},{1,25},{9,17},{17,9},{25,1},{2,26},{10... | collective-permute-start | bytes 24584 | tf_op jit(solution)/shard_map/ppermute | solution.py:368
  (24 other events, 299.3 us)

commit v5 on v4

--- a/solution.py
+++ b/solution.py
@@ -170,7 +170,7 @@
             out_specs=[half, half, whole(slots, tokens, features), whole(slots, tokens, active)],
             scratch_shapes=[pltpu.VMEM((tokens, features), bf16)] * slots
             + [
-                pltpu.VMEM((span * (2 * blocks + 1) + 8, LANES), f32),
+                pltpu.VMEM(((span + 1) * (2 * blocks + 1) + 8, LANES), f32),
                 pltpu.VMEM((tokens, active), f32),
                 pltpu.VMEM((tokens, active), i32),
                 pltpu.VMEM((tokens, active), i32),

time: 129 us -> 129 us (level)
  no operation moved by 1% of the time
where the time goes in v5:
time: 129 us; the launch traced here: 128 us
  Pallas kernels  57 us (44%)
  waiting for transfers between devices  33 us (26%)
  starting transfers between devices  29.4 us (23%)
  local copies, waits for them, and re-layouts  5.21 us (4%)
  other arithmetic  2.87 us (2%)
    pallas_call x1, Pallas kernels, recon_call(): pl.pallas_call(kernel, out_shape=(jax.ShapeDtypeStruct((slots, tokens //...  25.9 us
    ppermute x12, waiting for transfers between devices, swap_pair(): lax.ppermute(x, 'pair', [(i, i ^ m) for i in range(lax.axis_size('pair'))])  20 us
    pallas_call x1, Pallas kernels, back_call(): pl.pallas_call(kernel, out_shape=[jax.ShapeDtypeStruct((slots, tokens //...  18.1 us
    ppermute x12, starting transfers between devices, swap_pair(): lax.ppermute(x, 'pair', [(i, i ^ m) for i in range(lax.axis_size('pair'))])  14.7 us
    ppermute x9, starting transfers between devices, swap_z(): lax.ppermute(x, 'feat', [(i, i ^ 2 * m) for i in range(lax.axis_size('fea...  13.4 us
    pallas_call x2, Pallas kernels, grad_call(): pl.pallas_call(kernel, out_shape=jax.ShapeDtypeStruct((slots, features, w...  11 us
    ppermute x9, waiting for transfers between devices, swap_z(): lax.ppermute(x, 'feat', [(i, i ^ 2 * m) for i in range(lax.axis_size('fea...  10.3 us
    unnamed x46, local copies, waits for them, and re-layouts  3.79 us
  transfers between devices with their start and end apart: 27, of which 14 were waited for; matrix products, arithmetic and copies ran while one was open for 2% of the time, Pallas kernels for 9%

profile of v5, /device:TPU:0, one launch (start us, length us, event | category | flops | bytes accessed | tf_op | source)
XLA Modules:
  0.0 128.4 jit_solution(5203108859050072300)
XLA Ops:
  3.3 25.9 %recon.1 = (f32[2,128,2048]{2,1,0:T(8,128)S(1)}, f32[2,128,2048]{2,1,0:T(8,128)S(1)}, bf16[2,256,2048]{2,1,0:T(8,128)(2,1)S(1)}, s32[2,256,128]{2,1,0:T(8,128)S(1)}) custom-call(s32[2,2]{1,0:T(2,128)S(1)} %copy-done.11, s32[3,256,128]{2,1,0:T(8,128)S(1)} %copy-done.12, f32[3,256,128]{2,1,0:T(8,128)S(1)} %copy-done.13, f32[2,2048,2048]{2,1,0:T(8,128)} %refs_2_.3), custom_call_target="tpu_custom_call" | custom-call | flops 12884901888 | bytes 33554432 | tf_op jit(solution)/shard_map/recon/pallas_call | solution.py:154
  29.8 2.6 %collective-permute-start = (s32[2,2]{1,0:T(2,128)S(1)}, s32[2,2]{1,0:T(2,128)S(1)}, u32[]{:S(2)}, u32[]{:S(2)}) collective-permute-start(s32[2,2]{1,0:T(2,128)S(1)} %copy-done.11), channel_id=1, source_target_pairs={{0,8},{8,0},{16,24},{24,16},{1,9},{9,1},{17,25},{25,17},{2,10},{10... | collective-permute-start | bytes 56 | tf_op jit(solution)/shard_map/ppermute | solution.py:368
  32.4 1.5 %collective-permute-start.1 = (s32[2,2]{1,0:T(2,128)S(1)}, s32[2,2]{1,0:T(2,128)S(1)}, u32[]{:S(2)}, u32[]{:S(2)}) collective-permute-start(s32[2,2]{1,0:T(2,128)S(1)} %copy-done.11), channel_id=1, source_target_pairs={{0,16},{8,24},{16,0},{24,8},{1,17},{9,25},{17,1},{25,9},{2,18},{10... | collective-permute-start | bytes 56 | tf_op jit(solution)/shard_map/ppermute | solution.py:368
  33.9 2.0 %collective-permute-done.1 = s32[2,2]{1,0:T(2,128)S(1)} collective-permute-done((s32[2,2]{1,0:T(2,128)S(1)}, s32[2,2]{1,0:T(2,128)S(1)}, u32[]{:S(2)}, u32[]{:S(2)}) %collective-permute-start.1) | collective-permute-done | bytes 48 | tf_op jit(solution)/shard_map/ppermute | solution.py:368
  35.9 2.4 %collective-permute-done.2 = s32[2,2]{1,0:T(2,128)S(1)} collective-permute-done((s32[2,2]{1,0:T(2,128)S(1)}, s32[2,2]{1,0:T(2,128)S(1)}, u32[]{:S(2)}, u32[]{:S(2)}) %collective-permute-start.2) | collective-permute-done | bytes 48 | tf_op jit(solution)/shard_map/ppermute | solution.py:368
  40.0 1.5 %collective-permute-start.6 = (f16[2,32,2048]{2,1,0:T(8,128)(2,1)}, f16[2,32,2048]{2,1,0:T(8,128)(2,1)S(1)}, u32[]{:S(2)}, u32[]{:S(2)}) collective-permute-start(f16[2,32,2048]{2,1,0:T(8,128)(2,1)} %get-tuple-element.58), channel_id=1, source_target_pairs={{0,24},{8,16},{16,8},{24,0},{1,25},{9,17},{17,9},{25,1},{2,26},{10... | collective-permute-start | bytes 786440 | tf_op jit(solution)/shard_map/ppermute | solution.py:368
  41.5 1.5 %collective-permute-start.4 = (f16[2,32,2048]{2,1,0:T(8,128)(2,1)}, f16[2,32,2048]{2,1,0:T(8,128)(2,1)S(1)}, u32[]{:S(2)}, u32[]{:S(2)}) collective-permute-start(f16[2,32,2048]{2,1,0:T(8,128)(2,1)} %get-tuple-element.60), channel_id=1, source_target_pairs={{0,8},{8,0},{16,24},{24,16},{1,9},{9,1},{17,25},{25,17},{2,10},{10... | collective-permute-start | bytes 786440 | tf_op jit(solution)/shard_map/ppermute | solution.py:368
  44.1 8.1 %collective-permute-done.5 = f16[2,32,2048]{2,1,0:T(8,128)(2,1)S(1)} collective-permute-done((f16[2,32,2048]{2,1,0:T(8,128)(2,1)}, f16[2,32,2048]{2,1,0:T(8,128)(2,1)S(1)}, u32[]{:S(2)}, u32[]{:S(2)}) %collective-permute-start.5) | collective-permute-done | bytes 262176 | tf_op jit(solution)/shard_map/ppermute | solution.py:368
  53.9 1.6 %collective-permute-start.7 = (f16[3,8,2048]{2,1,0:T(8,128)(2,1)S(1)}, f16[3,8,2048]{2,1,0:T(8,128)(2,1)S(1)}, u32[]{:S(2)}, u32[]{:S(2)}) collective-permute-start(f16[3,8,2048]{2,1,0:T(8,128)(2,1)S(1)} %multiply_convert_fusion.2), channel_id=1, source_target_pairs={{0,2},{1,3},{2,0},{3,1},{4,6},{5,7},{6,4},{7,5},{8,10},{9,11},{10,... | collective-permute-start | bytes 294920 | tf_op jit(solution)/shard_map/ppermute | solution.py:364
  55.9 2.7 %collective-permute-start.8 = (f16[3,8,2048]{2,1,0:T(8,128)(2,1)S(1)}, f16[3,8,2048]{2,1,0:T(8,128)(2,1)S(1)}, u32[]{:S(2)}, u32[]{:S(2)}) collective-permute-start(f16[3,8,2048]{2,1,0:T(8,128)(2,1)S(1)} %multiply_convert_fusion.1), channel_id=1, source_target_pairs={{0,4},{1,5},{2,6},{3,7},{4,0},{5,1},{6,2},{7,3},{8,12},{9,13},{10,... | collective-permute-start | bytes 294920 | tf_op jit(solution)/shard_map/ppermute | solution.py:364
  59.1 4.4 %collective-permute-done.8 = f16[3,8,2048]{2,1,0:T(8,128)(2,1)S(1)} collective-permute-done((f16[3,8,2048]{2,1,0:T(8,128)(2,1)S(1)}, f16[3,8,2048]{2,1,0:T(8,128)(2,1)S(1)}, u32[]{:S(2)}, u32[]{:S(2)}) %collective-permute-start.8) | collective-permute-done | bytes 98336 | tf_op jit(solution)/shard_map/ppermute | solution.py:364
  63.5 1.8 %collective-permute-done.9 = f16[3,8,2048]{2,1,0:T(8,128)(2,1)S(1)} collective-permute-done((f16[3,8,2048]{2,1,0:T(8,128)(2,1)S(1)}, f16[3,8,2048]{2,1,0:T(8,128)(2,1)S(1)}, u32[]{:S(2)}, u32[]{:S(2)}) %collective-permute-start.9) | collective-permute-done | bytes 98336 | tf_op jit(solution)/shard_map/ppermute | solution.py:364
  68.3 2.4 %collective-permute-start.12 = (bf16[3,8,2048]{2,1,0:T(8,128)(2,1)S(1)}, bf16[3,8,2048]{2,1,0:T(8,128)(2,1)S(1)}, u32[]{:S(2)}, u32[]{:S(2)}) collective-permute-start(bf16[3,8,2048]{2,1,0:T(8,128)(2,1)S(1)} %get-tuple-element.55.refs_0_), channel_id=1, source_target_pairs={{0,6},{1,7},{2,4},{3,5},{4,2},{5,3},{6,0},{7,1},{8,14},{9,15},{10,... | collective-permute-start | bytes 294920 | tf_op jit(solution)/shard_map/ppermute | solution.py:364
  71.1 2.5 %collective-permute-done.11.refs_2_ = bf16[3,8,2048]{2,1,0:T(8,128)(2,1)S(1)} collective-permute-done((bf16[3,8,2048]{2,1,0:T(8,128)(2,1)S(1)}, bf16[3,8,2048]{2,1,0:T(8,128)(2,1)S(1)}, u32[]{:S(2)}, u32[]{:S(2)}) %collective-permute-start.11) | collective-permute-done | bytes 98336 | tf_op jit(solution)/shard_map/ppermute | solution.py:364
  76.5 2.5 %collective-permute-start.15 = (bf16[2,32,2048]{2,1,0:T(8,128)(2,1)S(1)}, bf16[2,32,2048]{2,1,0:T(8,128)(2,1)S(1)}, u32[]{:S(2)}, u32[]{:S(2)}) collective-permute-start(bf16[2,32,2048]{2,1,0:T(8,128)(2,1)S(1)} %get-tuple-element.39), channel_id=1, source_target_pairs={{0,24},{8,16},{16,8},{24,0},{1,25},{9,17},{17,9},{25,1},{2,26},{10... | collective-permute-start | bytes 786440 | tf_op jit(solution)/shard_map/ppermute | solution.py:368
  79.1 2.9 %collective-permute-done.13.refs_4_.refs_2_ = bf16[2,32,2048]{2,1,0:T(8,128)(2,1)S(1)} collective-permute-done((bf16[2,32,2048]{2,1,0:T(8,128)(2,1)S(1)}, bf16[2,32,2048]{2,1,0:T(8,128)(2,1)S(1)}, u32[]{:S(2)}, u32[]{:S(2)}) %collective-permute-start.13) | collective-permute-done | bytes 262176 | tf_op jit(solution)/shard_map/ppermute | solution.py:368
  82.0 3.3 %collective-permute-done.14.refs_5_.refs_3_ = bf16[2,32,2048]{2,1,0:T(8,128)(2,1)S(1)} collective-permute-done((bf16[2,32,2048]{2,1,0:T(8,128)(2,1)S(1)}, bf16[2,32,2048]{2,1,0:T(8,128)(2,1)S(1)}, u32[]{:S(2)}, u32[]{:S(2)}) %collective-permute-start.14) | collective-permute-done | bytes 262176 | tf_op jit(solution)/shard_map/ppermute | solution.py:368
  88.3 18.1 %back.1 = (f32[2,128,128]{2,1,0:T(8,128)S(1)}, f32[2,128,128]{2,1,0:T(8,128)}, f32[2,2048,2048]{2,1,0:T(8,128)}) custom-call(s32[2,256,128]{2,1,0:T(8,128)S(1)} %copy-done.10, bf16[2,256,2048]{2,1,0:T(8,128)(2,1)S(1)} %get-tuple-element.34.refs_1_.refs_0_, f32[2,2048,2048]{2,1,0:T(8,128)} %refs_2_.3, ...), custom_call_target="tpu_custom_call" | custom-call | flops 6442450944 | bytes 50331648 | tf_op jit(solution)/shard_map/back/pallas_call | solution.py:245
  108.1 1.6 %collective-permute-start.21 = (f32[2,4,8,128]{3,2,0,1:T(8,128)S(1)}, f32[2,4,8,128]{3,2,0,1:T(8,128)S(1)}, u32[]{:S(2)}, u32[]{:S(2)}) collective-permute-start(f32[2,4,8,128]{3,2,0,1:T(8,128)S(1)} %bitcast.110), channel_id=1, source_target_pairs={{0,2},{1,3},{2,0},{3,1},{4,6},{5,7},{6,4},{7,5},{8,10},{9,11},{10,... | collective-permute-start | bytes 98312 | tf_op jit(solution)/shard_map/ppermute | solution.py:364
  111.1 1.4 %collective-permute-start.23 = (f32[2,4,8,128]{3,2,0,1:T(8,128)S(1)}, f32[2,4,8,128]{3,2,0,1:T(8,128)S(1)}, u32[]{:S(2)}, u32[]{:S(2)}) collective-permute-start(f32[2,4,8,128]{3,2,0,1:T(8,128)S(1)} %bitcast.112), channel_id=1, source_target_pairs={{0,6},{1,7},{2,4},{3,5},{4,2},{5,3},{6,0},{7,1},{8,14},{9,15},{10,... | collective-permute-start | bytes 98312 | tf_op jit(solution)/shard_map/ppermute | solution.py:364
  112.5 5.5 %grad.2.refs_9_ = f32[2,2048,2048]{2,1,0:T(8,128)} custom-call(bf16[2,256,2048]{2,1,0:T(8,128)(2,1)} %copy-done, bf16[2,32,2048]{2,1,0:T(8,128)(2,1)} %copy-done.1, bf16[2,32,2048]{2,1,0:T(8,128)(2,1)} %copy-done.2, bf16[2,32,2048]{2,1,0:T(8,128)(2,1)} %copy-done.3, bf16[2,32,2048]{2,1,0:T(8,128)(2,1)} %copy-done.4, ...), custom_call_target="tpu_custom_call", output_to_operand_aliasing={{}: (9, {})} | custom-call | flops 1073741824 | bytes 8388608 | tf_op jit(solution)/shard_map/grad/pallas_call | solution.py:285
  118.1 1.5 %collective-permute-start.24 = (f32[2,8,128]{2,1,0:T(8,128)S(1)}, f32[2,8,128]{2,1,0:T(8,128)S(1)}, u32[]{:S(2)}, u32[]{:S(2)}) collective-permute-start(f32[2,8,128]{2,1,0:T(8,128)S(1)} %get-tuple-element.111), channel_id=1, source_target_pairs={{0,8},{8,0},{16,24},{24,16},{1,9},{9,1},{17,25},{25,17},{2,10},{10... | collective-permute-start | bytes 24584 | tf_op jit(solution)/shard_map/ppermute | solution.py:368
  120.1 1.6 %collective-permute-start.26 = (f32[2,8,128]{2,1,0:T(8,128)S(1)}, f32[2,8,128]{2,1,0:T(8,128)S(1)}, u32[]{:S(2)}, u32[]{:S(2)}) collective-permute-start(f32[2,8,128]{2,1,0:T(8,128)S(1)} %get-tuple-element.109), channel_id=1, source_target_pairs={{0,24},{8,16},{16,8},{24,0},{1,25},{9,17},{17,9},{25,1},{2,26},{10... | collective-permute-start | bytes 24584 | tf_op jit(solution)/shard_map/ppermute | solution.py:368
  121.7 5.5 %grad.3 = f32[2,2048,2048]{2,1,0:T(8,128)} custom-call(bf16[2,256,2048]{2,1,0:T(8,128)(2,1)} %copy-done, bf16[2,32,2048]{2,1,0:T(8,128)(2,1)} %copy-done.1, bf16[2,32,2048]{2,1,0:T(8,128)(2,1)} %copy-done.2, bf16[2,32,2048]{2,1,0:T(8,128)(2,1)} %copy-done.3, bf16[2,32,2048]{2,1,0:T(8,128)(2,1)} %copy-done.4, ...), custom_call_target="tpu_custom_call", output_to_operand_aliasing={{}: (9, {})} | custom-call | flops 1073741824 | bytes 8388608 | tf_op jit(solution)/shard_map/grad/pallas_call | solution.py:285
  (111 shorter events, 22.4 us)
Async XLA Ops:
  29.3 9.1 %collective-permute-start.3 = (f32[2,128,2048]{2,1,0:T(8,128)S(1)}, f32[2,128,2048]{2,1,0:T(8,128)S(1)}, u32[]{:S(2)}, u32[]{:S(2)}) collective-permute-start(f32[2,128,2048]{2,1,0:T(8,128)S(1)} %get-tuple-element.31), channel_id=1, source_target_pairs={{0,1},{1,0},{2,3},{3,2},{4,5},{5,4},{6,7},{7,6},{8,9},{9,8},{10,11... | collective-permute-start | bytes 6291464 | tf_op jit(solution)/shard_map/ppermute | solution.py:360
  29.8 4.1 %collective-permute-start = (s32[2,2]{1,0:T(2,128)S(1)}, s32[2,2]{1,0:T(2,128)S(1)}, u32[]{:S(2)}, u32[]{:S(2)}) collective-permute-start(s32[2,2]{1,0:T(2,128)S(1)} %copy-done.11), channel_id=1, source_target_pairs={{0,8},{8,0},{16,24},{24,16},{1,9},{9,1},{17,25},{25,17},{2,10},{10... | collective-permute-start | bytes 56 | tf_op jit(solution)/shard_map/ppermute | solution.py:368
  32.4 3.6 %collective-permute-start.1 = (s32[2,2]{1,0:T(2,128)S(1)}, s32[2,2]{1,0:T(2,128)S(1)}, u32[]{:S(2)}, u32[]{:S(2)}) collective-permute-start(s32[2,2]{1,0:T(2,128)S(1)} %copy-done.11), channel_id=1, source_target_pairs={{0,16},{8,24},{16,0},{24,8},{1,17},{9,25},{17,1},{25,9},{2,18},{10... | collective-permute-start | bytes 56 | tf_op jit(solution)/shard_map/ppermute | solution.py:368
  33.9 4.5 %collective-permute-start.2 = (s32[2,2]{1,0:T(2,128)S(1)}, s32[2,2]{1,0:T(2,128)S(1)}, u32[]{:S(2)}, u32[]{:S(2)}) collective-permute-start(s32[2,2]{1,0:T(2,128)S(1)} %copy-done.11), channel_id=1, source_target_pairs={{0,24},{8,16},{16,8},{24,0},{1,25},{9,17},{17,9},{25,1},{2,26},{10... | collective-permute-start | bytes 56 | tf_op jit(solution)/shard_map/ppermute | solution.py:368
  39.5 12.8 %collective-permute-start.5 = (f16[2,32,2048]{2,1,0:T(8,128)(2,1)}, f16[2,32,2048]{2,1,0:T(8,128)(2,1)S(1)}, u32[]{:S(2)}, u32[]{:S(2)}) collective-permute-start(f16[2,32,2048]{2,1,0:T(8,128)(2,1)} %get-tuple-element.59), channel_id=1, source_target_pairs={{0,16},{8,24},{16,0},{24,8},{1,17},{9,25},{17,1},{25,9},{2,18},{10... | collective-permute-start | bytes 786440 | tf_op jit(solution)/shard_map/ppermute | solution.py:368
  40.0 13.6 %collective-permute-start.6 = (f16[2,32,2048]{2,1,0:T(8,128)(2,1)}, f16[2,32,2048]{2,1,0:T(8,128)(2,1)S(1)}, u32[]{:S(2)}, u32[]{:S(2)}) collective-permute-start(f16[2,32,2048]{2,1,0:T(8,128)(2,1)} %get-tuple-element.58), channel_id=1, source_target_pairs={{0,24},{8,16},{16,8},{24,0},{1,25},{9,17},{17,9},{25,1},{2,26},{10... | collective-permute-start | bytes 786440 | tf_op jit(solution)/shard_map/ppermute | solution.py:368
  41.5 12.0 %collective-permute-start.4 = (f16[2,32,2048]{2,1,0:T(8,128)(2,1)}, f16[2,32,2048]{2,1,0:T(8,128)(2,1)S(1)}, u32[]{:S(2)}, u32[]{:S(2)}) collective-permute-start(f16[2,32,2048]{2,1,0:T(8,128)(2,1)} %get-tuple-element.60), channel_id=1, source_target_pairs={{0,8},{8,0},{16,24},{24,16},{1,9},{9,1},{17,25},{25,17},{2,10},{10... | collective-permute-start | bytes 786440 | tf_op jit(solution)/shard_map/ppermute | solution.py:368
  53.9 5.1 %collective-permute-start.7 = (f16[3,8,2048]{2,1,0:T(8,128)(2,1)S(1)}, f16[3,8,2048]{2,1,0:T(8,128)(2,1)S(1)}, u32[]{:S(2)}, u32[]{:S(2)}) collective-permute-start(f16[3,8,2048]{2,1,0:T(8,128)(2,1)S(1)} %multiply_convert_fusion.2), channel_id=1, source_target_pairs={{0,2},{1,3},{2,0},{3,1},{4,6},{5,7},{6,4},{7,5},{8,10},{9,11},{10,... | collective-permute-start | bytes 294920 | tf_op jit(solution)/shard_map/ppermute | solution.py:364
  55.9 7.6 %collective-permute-start.8 = (f16[3,8,2048]{2,1,0:T(8,128)(2,1)S(1)}, f16[3,8,2048]{2,1,0:T(8,128)(2,1)S(1)}, u32[]{:S(2)}, u32[]{:S(2)}) collective-permute-start(f16[3,8,2048]{2,1,0:T(8,128)(2,1)S(1)} %multiply_convert_fusion.1), channel_id=1, source_target_pairs={{0,4},{1,5},{2,6},{3,7},{4,0},{5,1},{6,2},{7,3},{8,12},{9,13},{10,... | collective-permute-start | bytes 294920 | tf_op jit(solution)/shard_map/ppermute | solution.py:364
  58.7 6.6 %collective-permute-start.9 = (f16[3,8,2048]{2,1,0:T(8,128)(2,1)S(1)}, f16[3,8,2048]{2,1,0:T(8,128)(2,1)S(1)}, u32[]{:S(2)}, u32[]{:S(2)}) collective-permute-start(f16[3,8,2048]{2,1,0:T(8,128)(2,1)S(1)} %multiply_convert_fusion), channel_id=1, source_target_pairs={{0,6},{1,7},{2,4},{3,5},{4,2},{5,3},{6,0},{7,1},{8,14},{9,15},{10,... | collective-permute-start | bytes 294920 | tf_op jit(solution)/shard_map/ppermute | solution.py:364
  66.2 4.9 %collective-permute-start.10 = (bf16[3,8,2048]{2,1,0:T(8,128)(2,1)S(1)}, bf16[3,8,2048]{2,1,0:T(8,128)(2,1)S(1)}, u32[]{:S(2)}, u32[]{:S(2)}) collective-permute-start(bf16[3,8,2048]{2,1,0:T(8,128)(2,1)S(1)} %get-tuple-element.55.refs_0_), channel_id=1, source_target_pairs={{0,2},{1,3},{2,0},{3,1},{4,6},{5,7},{6,4},{7,5},{8,10},{9,11},{10,... | collective-permute-start | bytes 294920 | tf_op jit(solution)/shard_map/ppermute | solution.py:364
  67.1 6.6 %collective-permute-start.11 = (bf16[3,8,2048]{2,1,0:T(8,128)(2,1)S(1)}, bf16[3,8,2048]{2,1,0:T(8,128)(2,1)S(1)}, u32[]{:S(2)}, u32[]{:S(2)}) collective-permute-start(bf16[3,8,2048]{2,1,0:T(8,128)(2,1)S(1)} %get-tuple-element.55.refs_0_), channel_id=1, source_target_pairs={{0,4},{1,5},{2,6},{3,7},{4,0},{5,1},{6,2},{7,3},{8,12},{9,13},{10,... | collective-permute-start | bytes 294920 | tf_op jit(solution)/shard_map/ppermute | solution.py:364
  68.3 6.5 %collective-permute-start.12 = (bf16[3,8,2048]{2,1,0:T(8,128)(2,1)S(1)}, bf16[3,8,2048]{2,1,0:T(8,128)(2,1)S(1)}, u32[]{:S(2)}, u32[]{:S(2)}) collective-permute-start(bf16[3,8,2048]{2,1,0:T(8,128)(2,1)S(1)} %get-tuple-element.55.refs_0_), channel_id=1, source_target_pairs={{0,6},{1,7},{2,4},{3,5},{4,2},{5,3},{6,0},{7,1},{8,14},{9,15},{10,... | collective-permute-start | bytes 294920 | tf_op jit(solution)/shard_map/ppermute | solution.py:364
  75.5 6.4 %collective-permute-start.13 = (bf16[2,32,2048]{2,1,0:T(8,128)(2,1)S(1)}, bf16[2,32,2048]{2,1,0:T(8,128)(2,1)S(1)}, u32[]{:S(2)}, u32[]{:S(2)}) collective-permute-start(bf16[2,32,2048]{2,1,0:T(8,128)(2,1)S(1)} %get-tuple-element.37), channel_id=1, source_target_pairs={{0,8},{8,0},{16,24},{24,16},{1,9},{9,1},{17,25},{25,17},{2,10},{10... | collective-permute-start | bytes 786440 | tf_op jit(solution)/shard_map/ppermute | solution.py:368
  76.1 9.2 %collective-permute-start.14 = (bf16[2,32,2048]{2,1,0:T(8,128)(2,1)S(1)}, bf16[2,32,2048]{2,1,0:T(8,128)(2,1)S(1)}, u32[]{:S(2)}, u32[]{:S(2)}) collective-permute-start(bf16[2,32,2048]{2,1,0:T(8,128)(2,1)S(1)} %get-tuple-element.38), channel_id=1, source_target_pairs={{0,16},{8,24},{16,0},{24,8},{1,17},{9,25},{17,1},{25,9},{2,18},{10... | collective-permute-start | bytes 786440 | tf_op jit(solution)/shard_map/ppermute | solution.py:368
  76.5 8.8 %collective-permute-start.15 = (bf16[2,32,2048]{2,1,0:T(8,128)(2,1)S(1)}, bf16[2,32,2048]{2,1,0:T(8,128)(2,1)S(1)}, u32[]{:S(2)}, u32[]{:S(2)}) collective-permute-start(bf16[2,32,2048]{2,1,0:T(8,128)(2,1)S(1)} %get-tuple-element.39), channel_id=1, source_target_pairs={{0,24},{8,16},{16,8},{24,0},{1,25},{9,17},{17,9},{25,1},{2,26},{10... | collective-permute-start | bytes 786440 | tf_op jit(solution)/shard_map/ppermute | solution.py:368
  79.1 6.8 %collective-permute-start.16 = (bf16[2,32,2048]{2,1,0:T(8,128)(2,1)S(1)}, bf16[2,32,2048]{2,1,0:T(8,128)(2,1)S(1)}, u32[]{:S(2)}, u32[]{:S(2)}) collective-permute-start(bf16[2,32,2048]{2,1,0:T(8,128)(2,1)S(1)} %get-tuple-element.36.refs_3_.refs_1_), channel_id=1, source_target_pairs={{0,1},{1,0},{2,3},{3,2},{4,5},{5,4},{6,7},{7,6},{8,9},{9,8},{10,11... | collective-permute-start | bytes 786440 | tf_op jit(solution)/shard_map/ppermute | solution.py:360
  81.9 3.9 %collective-permute-start.17 = (bf16[2,32,2048]{2,1,0:T(8,128)(2,1)S(1)}, bf16[2,32,2048]{2,1,0:T(8,128)(2,1)S(1)}, u32[]{:S(2)}, u32[]{:S(2)}) collective-permute-start(bf16[2,32,2048]{2,1,0:T(8,128)(2,1)S(1)} %collective-permute-done.13.refs_4_.refs_2_), channel_id=1, source_target_pairs={{0,1},{1,0},{2,3},{3,2},{4,5},{5,4},{6,7},{7,6},{8,9},{9,8},{10,11... | collective-permute-start | bytes 786440 | tf_op jit(solution)/shard_map/ppermute | solution.py:360
  108.1 10.0 %collective-permute-start.21 = (f32[2,4,8,128]{3,2,0,1:T(8,128)S(1)}, f32[2,4,8,128]{3,2,0,1:T(8,128)S(1)}, u32[]{:S(2)}, u32[]{:S(2)}) collective-permute-start(f32[2,4,8,128]{3,2,0,1:T(8,128)S(1)} %bitcast.110), channel_id=1, source_target_pairs={{0,2},{1,3},{2,0},{3,1},{4,6},{5,7},{6,4},{7,5},{8,10},{9,11},{10,... | collective-permute-start | bytes 98312 | tf_op jit(solution)/shard_map/ppermute | solution.py:364
  109.7 8.4 %collective-permute-start.22 = (f32[2,4,8,128]{3,2,0,1:T(8,128)S(1)}, f32[2,4,8,128]{3,2,0,1:T(8,128)S(1)}, u32[]{:S(2)}, u32[]{:S(2)}) collective-permute-start(f32[2,4,8,128]{3,2,0,1:T(8,128)S(1)} %bitcast.111), channel_id=1, source_target_pairs={{0,4},{1,5},{2,6},{3,7},{4,0},{5,1},{6,2},{7,3},{8,12},{9,13},{10,... | collective-permute-start | bytes 98312 | tf_op jit(solution)/shard_map/ppermute | solution.py:364
  111.1 7.0 %collective-permute-start.23 = (f32[2,4,8,128]{3,2,0,1:T(8,128)S(1)}, f32[2,4,8,128]{3,2,0,1:T(8,128)S(1)}, u32[]{:S(2)}, u32[]{:S(2)}) collective-permute-start(f32[2,4,8,128]{3,2,0,1:T(8,128)S(1)} %bitcast.112), channel_id=1, source_target_pairs={{0,6},{1,7},{2,4},{3,5},{4,2},{5,3},{6,0},{7,1},{8,14},{9,15},{10,... | collective-permute-start | bytes 98312 | tf_op jit(solution)/shard_map/ppermute | solution.py:364
  118.1 9.1 %collective-permute-start.24 = (f32[2,8,128]{2,1,0:T(8,128)S(1)}, f32[2,8,128]{2,1,0:T(8,128)S(1)}, u32[]{:S(2)}, u32[]{:S(2)}) collective-permute-start(f32[2,8,128]{2,1,0:T(8,128)S(1)} %get-tuple-element.111), channel_id=1, source_target_pairs={{0,8},{8,0},{16,24},{24,16},{1,9},{9,1},{17,25},{25,17},{2,10},{10... | collective-permute-start | bytes 24584 | tf_op jit(solution)/shard_map/ppermute | solution.py:368
  119.7 7.5 %collective-permute-start.25 = (f32[2,8,128]{2,1,0:T(8,128)S(1)}, f32[2,8,128]{2,1,0:T(8,128)S(1)}, u32[]{:S(2)}, u32[]{:S(2)}) collective-permute-start(f32[2,8,128]{2,1,0:T(8,128)S(1)} %get-tuple-element.110), channel_id=1, source_target_pairs={{0,16},{8,24},{16,0},{24,8},{1,17},{9,25},{17,1},{25,9},{2,18},{10... | collective-permute-start | bytes 24584 | tf_op jit(solution)/shard_map/ppermute | solution.py:368
  120.1 7.1 %collective-permute-start.26 = (f32[2,8,128]{2,1,0:T(8,128)S(1)}, f32[2,8,128]{2,1,0:T(8,128)S(1)}, u32[]{:S(2)}, u32[]{:S(2)}) collective-permute-start(f32[2,8,128]{2,1,0:T(8,128)S(1)} %get-tuple-element.109), channel_id=1, source_target_pairs={{0,24},{8,16},{16,8},{24,0},{1,25},{9,17},{17,9},{25,1},{2,26},{10... | collective-permute-start | bytes 24584 | tf_op jit(solution)/shard_map/ppermute | solution.py:368
  (24 other events, 299.3 us)
